TPU v7x, 256 devices: a whole 4x4x8 slice. The times are simulated.
256 devices in a mesh: expert: 128 (over x, y, z_hi, core), hidden: 2 (over z_lo).
Axes of the slice: x: 4, y: 4, z: 8 (z_hi: 4, z_lo: 2; z = z_hi * 2 + z_lo), core: 2. Of those that a mesh axis runs over, the one named last changes fastest.
Arguments:
- tokens: bfloat16 [512, 196, 1024], P(('expert', 'hidden')), may hold values from -18 to 18
- grad_out: bfloat16 [512, 196, 1024], P(('expert', 'hidden')), may hold values from -192 to 192
- slot_weight: bfloat16 [1024, 128], replicated, may hold values from -3 to 3
- in_weight: bfloat16 [128, 1024, 4096], P('expert', None, 'hidden'), may hold values from -0.1875 to 0.1875
- out_weight: bfloat16 [128, 4096, 1024], P('expert', 'hidden'), may hold values from -0.09375 to 0.09375
Outputs:
- input_grad: bfloat16 [512, 196, 1024], P(('expert', 'hidden'))
- phi_grad: float32 [1024, 128], P(('expert', 'hidden'))
All inputs are finite; a program needn't handle non-finite values.
Results may differ from a plain program's by a relative error of at most 0.025.
Values may be sent and summed in bfloat16 or wider, within the bound.
No kernel may reach another device: no remote copies, remote signals or barrier semaphores. Data moves between devices by JAX's collectives and lax.ppermute only.
A program may use at most 128 MiB of HBM per device.

v0:
```python
import jax
import jax.numpy as jnp
from jax import lax
from jax.sharding import PartitionSpec as P


def gelu_tanh(inputs):
    return jax.nn.gelu(inputs, approximate=True)


def expert_pass(row_inputs, row_grads, first, second):
    pre_act = jnp.einsum("rkd,kdf->rkf", row_inputs, first, preferred_element_type=jnp.float32)
    activation = gelu_tanh(pre_act).astype(jnp.bfloat16)
    partial_out = jnp.einsum("rkf,kfd->rkd", activation, second, preferred_element_type=jnp.float32)
    act_grad = jnp.einsum("rkd,kfd->rkf", row_grads, second, preferred_element_type=jnp.float32)
    primal, pullback = jax.vjp(gelu_tanh, pre_act)
    pre_grad = pullback(act_grad)[0].astype(jnp.bfloat16)
    partial_back = jnp.einsum("rkf,kdf->rkd", pre_grad, first, preferred_element_type=jnp.float32)
    return (partial_out, partial_back)


def local(tokens, grad_out, slot_weight, in_weight, out_weight):
    logits = jnp.einsum("imd,dn->imn", tokens, slot_weight, preferred_element_type=jnp.float32)
    dispatch = jax.nn.softmax(logits, axis=1)
    combine = jax.nn.softmax(logits, axis=2)
    dispatch_b = dispatch.astype(jnp.bfloat16)
    combine_b = combine.astype(jnp.bfloat16)
    slot_inputs = jnp.einsum(
        "imn,imd->ind", dispatch_b, tokens, preferred_element_type=jnp.float32
    ).astype(jnp.bfloat16)
    slot_grads = jnp.einsum(
        "imn,imd->ind", combine_b, grad_out, preferred_element_type=jnp.float32
    ).astype(jnp.bfloat16)
    sent_inputs, sent_grads = (
        lax.all_to_all(slot_inputs, "expert", split_axis=1, concat_axis=0, tiled=True),
        lax.all_to_all(slot_grads, "expert", split_axis=1, concat_axis=0, tiled=True),
    )
    row_inputs, row_grads = (
        lax.all_gather(sent_inputs, "hidden", axis=0, tiled=True),
        lax.all_gather(sent_grads, "hidden", axis=0, tiled=True),
    )
    partial_out, partial_back = expert_pass(row_inputs, row_grads, in_weight, out_weight)
    summed_out, summed_back = (
        lax.psum_scatter(partial_out, "hidden", scatter_dimension=0, tiled=True),
        lax.psum_scatter(partial_back, "hidden", scatter_dimension=0, tiled=True),
    )
    slot_outputs, slot_in_grad = (
        lax.all_to_all(
            summed_out.astype(jnp.bfloat16), "expert", split_axis=0, concat_axis=1, tiled=True
        ),
        lax.all_to_all(
            summed_back.astype(jnp.bfloat16), "expert", split_axis=0, concat_axis=1, tiled=True
        ),
    )
    combine_dw = jnp.einsum(
        "imd,ind->imn", grad_out, slot_outputs, preferred_element_type=jnp.float32
    )
    combine_dl = combine * (combine_dw - jnp.sum(combine * combine_dw, axis=2, keepdims=True))
    dispatch_dw = jnp.einsum(
        "imd,ind->imn", tokens, slot_in_grad, preferred_element_type=jnp.float32
    )
    dispatch_dl = dispatch * (dispatch_dw - jnp.sum(dispatch * dispatch_dw, axis=1, keepdims=True))
    logit_grad = (combine_dl + dispatch_dl).astype(jnp.bfloat16)
    input_grad = jnp.einsum(
        "imn,ind->imd", dispatch_b, slot_in_grad, preferred_element_type=jnp.float32
    )
    input_grad = input_grad + jnp.einsum(
        "imn,dn->imd", logit_grad, slot_weight, preferred_element_type=jnp.float32
    )
    phi_term = jnp.einsum("imd,imn->dn", tokens, logit_grad, preferred_element_type=jnp.float32)
    phi_grad = lax.psum_scatter(phi_term, ("expert", "hidden"), scatter_dimension=0, tiled=True)
    return (input_grad.astype(jnp.bfloat16), phi_grad)


def solution(mesh):
    placed = (
        P(("expert", "hidden"), None, None),
        P(("expert", "hidden"), None, None),
        P(),
        P("expert", None, "hidden"),
        P("expert", "hidden", None),
    )
    return jax.shard_map(
        local,
        mesh=mesh,
        in_specs=placed,
        out_specs=(P(("expert", "hidden"), None, None), P(("expert", "hidden"), None)),
        check_vma=False,
    )
```

profile of v0, /device:TPU:1, one launch (start us, length us, event | category | flops | bytes accessed | tf_op | source)
XLA Modules:
  0.0 516.0 jit_solution(16927945651146080485)
XLA Ops:
  7.2 1.6 fusion.61
  9.6 1.6 convolution_convert_fusion
  11.2 1.3 copy.45
  12.5 16.4 %all-to-all-start.1 = ((bf16[2,128,1024]{2,0,1:T(2,128)(2,1)}), bf16[2,128,1024]{2,0,1:T(2,128)(2,1)S(1)}, u32[]{:S(2)}, u32[]{:S(2)}) async-start(bf16[2,128,1024]{2,0,1:T(2,128)(2,1)} %copy.45), calls=%async_computation.1 | async-start | bytes 1048576 | tf_op jit(solution)/shard_map/all_to_all | solution.py:35
  29.8 19.8 %all-to-all-done.1 = bf16[2,128,1024]{2,0,1:T(2,128)(2,1)S(1)} async-done(((bf16[2,128,1024]{2,0,1:T(2,128)(2,1)}), bf16[2,128,1024]{2,0,1:T(2,128)(2,1)S(1)}, u32[]{:S(2)}, u32[]{:S(2)}) %all-to-all-start.1) | async-done | bytes 524320 | tf_op jit(solution)/shard_map/all_to_all | solution.py:35
  50.6 1.0 convolution_convert_fusion.1
  52.2 32.5 %all_to_all.72 = bf16[2,128,1024]{2,0,1:T(2,128)(2,1)S(1)} all-to-all(bf16[2,128,1024]{2,0,1:T(2,128)(2,1)S(1)} %copy.43), channel_id=1, replica_groups=mesh['expert'=128,'hidden'=2] {'expert'}, dimensions={1} | all-to-all | bytes 1048576 | tf_op jit(solution)/shard_map/all_to_all | solution.py:36
  84.8 1.0 all_to_all.55
  86.0 6.8 %fusion.17 = f32[512,2048]{1,0:T(8,128)} fusion(bf16[1,1024,2048]{2,1,0:T(8,128)(2,1)} %param.8, bf16[512,1,1024]{2,0,1:T(8,128)(2,1)} %all-gather.5.cloned.1.call-done), kind=kOutput, calls=%fused_computation.22 | convolution fusion | flops 2147483648 | bytes 9437184 | tf_op jit(solution)/shard_map/rkd,kdf->rkf/dot_general | solution.py:12
  92.8 17.8 %all-gather.3.cloned.1.call-done = bf16[512,1,1024]{2,0,1:T(8,128)(2,1)} async-done(((bf16[256,1,1024]{2,0,1:T(8,128)(2,1)}), bf16[512,1,1024]{2,0,1:T(8,128)(2,1)}) %all-gather.3.cloned.1.call-update) | async-done | bytes 1048592 | tf_op jit(solution)/shard_map/all_gather | solution.py:40
  110.7 11.9 %fusion.38 = f32[512,1,1024]{2,0,1:T(8,128)} fusion(bf16[1,1024,2048]{2,1,0:T(8,128)(2,1)} %param.8, f32[512,2048]{1,0:T(8,128)} %fusion.17, bf16[1,2048,1024]{2,1,0:T(8,128)(2,1)} %param.9, bf16[512,1,1024]{2,0,1:T(8,128)(2,1)} %all-gather.3.cloned.1.call-done), kind=kOutput, calls=%fused_computation.35 | convolution fusion | flops 4315938816 | bytes 15728640 | tf_op jit(solution)/shard_map/rkf,kdf->rkd/dot_general | solution.py:18
  122.6 7.5 %fusion.33 = f32[512,1,1024]{2,0,1:T(8,128)} fusion(bf16[1,2048,1024]{2,1,0:T(8,128)(2,1)} %param.9, f32[512,2048]{1,0:T(8,128)} %fusion.17), kind=kOutput, calls=%fused_computation.34 | convolution fusion | flops 2156920832 | bytes 10485760 | tf_op jit(solution)/shard_map/rkf,kfd->rkd/dot_general | solution.py:14
  130.1 30.0 %reduce-scatter.4.cloned.1.call-done = f32[256,1,1024]{2,0,1:T(8,128)} async-done(((f32[512,1,1024]{2,0,1:T(8,128)}), f32[256,1,1024]{2,0,1:T(8,128)}) %reduce-scatter.4.cloned.1.call-update) | async-done | bytes 1048592 | tf_op jit(solution)/shard_map/reduce_scatter | solution.py:45
  160.1 1.3 convert_element_type.35
  161.9 1.0 reduce.2
  163.9 13.0 %all-to-all-start.2 = ((bf16[128,2,1024]{2,1,0:T(2,128)(2,1)}), bf16[128,2,1024]{2,1,0:T(2,128)(2,1)S(1)}, u32[]{:S(2)}, u32[]{:S(2)}) async-start(bf16[128,2,1024]{2,1,0:T(2,128)(2,1)} %reshape.46), calls=%async_computation.3 | async-start | bytes 1048576 | tf_op jit(solution)/shard_map/all_to_all | solution.py:51
  176.9 34.3 %reduce-scatter.6.cloned.1.call-done = f32[256,1,1024]{2,0,1:T(8,128)} async-done(((f32[512,1,1024]{2,0,1:T(8,128)}), f32[256,1,1024]{2,0,1:T(8,128)}) %reduce-scatter.6.cloned.1.call-update) | async-done | bytes 1048592 | tf_op jit(solution)/shard_map/reduce_scatter | solution.py:44
  211.2 1.3 convert_element_type.37
  212.5 1.0 reduce.3
  213.6 1.0 reshape.48
  214.6 13.7 %all-to-all-start.3 = ((bf16[128,2,1024]{2,1,0:T(2,128)(2,1)}), bf16[128,2,1024]{2,1,0:T(2,128)(2,1)}, u32[]{:S(2)}, u32[]{:S(2)}) async-start(bf16[128,2,1024]{2,1,0:T(2,128)(2,1)} %reshape.48), calls=%async_computation.5 | async-start | bytes 1048576 | tf_op jit(solution)/shard_map/all_to_all | solution.py:48
  228.8 3.1 reduce
  232.1 2.2 convolution_bitcast_fusion.1
  234.7 13.0 %all-to-all-done.3 = bf16[128,2,1024]{2,1,0:T(2,128)(2,1)} async-done(((bf16[128,2,1024]{2,1,0:T(2,128)(2,1)}), bf16[128,2,1024]{2,1,0:T(2,128)(2,1)}, u32[]{:S(2)}, u32[]{:S(2)}) %all-to-all-start.3) | async-done | bytes 524320 | tf_op jit(solution)/shard_map/all_to_all | solution.py:48
  247.7 3.6 reshape.49
  251.3 3.8 reduce.1
  255.1 1.3 all_to_all.65
  256.8 1.4 fusion.49
  258.2 4.2 convolution_bitcast_fusion
  262.5 3.0 add_convert_fusion
  265.5 1.7 copy.53
  267.2 240.7 %all-reduce.3.cloned.1.call-done = f32[1024,128]{0,1:T(8,128)} async-done(((f32[1024,128]{0,1:T(8,128)}), f32[1024,128]{0,1:T(8,128)}) %all-reduce.3.cloned.1.call-update) | async-done | bytes 524304
  (32 shorter events, 8.2 us)
Async XLA Ops:
  7.2 43.5 %copy-start = (bf16[2,196,1024]{2,0,1:T(2,128)(2,1)S(1)}, bf16[2,196,1024]{2,0,1:T(2,128)(2,1)}, u32[]{:S(2)}) copy-start(bf16[2,196,1024]{2,0,1:T(2,128)(2,1)} %param.6) | copy-start | bytes 2408452
  12.5 37.1 %all-to-all-start.1 = ((bf16[2,128,1024]{2,0,1:T(2,128)(2,1)}), bf16[2,128,1024]{2,0,1:T(2,128)(2,1)S(1)}, u32[]{:S(2)}, u32[]{:S(2)}) async-start(bf16[2,128,1024]{2,0,1:T(2,128)(2,1)} %copy.45), calls=%async_computation.1 | async-start | bytes 1048576 | tf_op jit(solution)/shard_map/all_to_all | solution.py:35
  28.9 57.1 %all-gather.5.cloned.1.call-start = ((), (), s32[]{:S(2)}) async-start(), calls=%async_computation.7 | async-start | bytes 1572864 | tf_op jit(solution)/shard_map/all_gather | solution.py:39
  50.6 60.1 %all-gather.3.cloned.1.call-start = ((), (), s32[]{:S(2)}) async-start(), calls=%async_computation.6 | async-start | bytes 1572864 | tf_op jit(solution)/shard_map/all_gather | solution.py:40
  85.8 74.3 %reduce-scatter.4.cloned.1.call-start = ((), (), s32[]{:S(2)}) async-start(), calls=%async_computation.8 | async-start | bytes 3145728 | tf_op jit(solution)/shard_map/reduce_scatter | solution.py:45
  122.6 88.7 %reduce-scatter.6.cloned.1.call-start = ((), (), s32[]{:S(2)}) async-start(), calls=%async_computation.9 | async-start | bytes 3145728 | tf_op jit(solution)/shard_map/reduce_scatter | solution.py:44
  163.9 50.7 %all-to-all-start.2 = ((bf16[128,2,1024]{2,1,0:T(2,128)(2,1)}), bf16[128,2,1024]{2,1,0:T(2,128)(2,1)S(1)}, u32[]{:S(2)}, u32[]{:S(2)}) async-start(bf16[128,2,1024]{2,1,0:T(2,128)(2,1)} %reshape.46), calls=%async_computation.3 | async-start | bytes 1048576 | tf_op jit(solution)/shard_map/all_to_all | solution.py:51
  214.6 33.1 %all-to-all-start.3 = ((bf16[128,2,1024]{2,1,0:T(2,128)(2,1)}), bf16[128,2,1024]{2,1,0:T(2,128)(2,1)}, u32[]{:S(2)}, u32[]{:S(2)}) async-start(bf16[128,2,1024]{2,1,0:T(2,128)(2,1)} %reshape.48), calls=%async_computation.5 | async-start | bytes 1048576 | tf_op jit(solution)/shard_map/all_to_all | solution.py:48
  228.3 279.7 %all-reduce.3.cloned.1.call-start = ((), (), s32[]{:S(2)}) async-start(), calls=%async_computation.10 | async-start | bytes 1048576
  255.1 7.3 %copy-start.1 = (bf16[1024,128]{1,0:T(8,128)(2,1)S(1)}, bf16[1024,128]{1,0:T(8,128)(2,1)}, u32[]{:S(2)}) copy-start(bf16[1024,128]{1,0:T(8,128)(2,1)} %param.7) | copy-start | bytes 786436
  256.8 5.6 %copy-start.3 = (f32[2,196,128]{2,1,0:T(8,128)}, f32[2,196,128]{2,1,0:T(8,128)S(1)}, u32[]{:S(2)}) copy-start(f32[2,196,128]{2,1,0:T(8,128)S(1)} %convolution_bitcast_fusion.2) | copy-start | bytes 602116
  258.2 4.2 copy-start.2
Sparse Core Ops, SparseCore 0:
  50.7 31.2 all-gather.4
  85.9 24.7 all-gather.2
  122.7 37.3 reduce-scatter.3
  162.6 48.6 reduce-scatter.5
  262.6 245.3 all-reduce.2
where the time goes:
time: 517 us; the launch traced here: 516 us
  waiting for transfers between devices  356 us (69%)
  starting transfers between devices  43.5 us (8%)
  matrix products  40.7 us (8%)
  blocking collectives  32.5 us (6%)
  local copies, waits for them, and re-layouts  15.2 us (3%)
  other arithmetic  14.5 us (3%)
  between operations  14 us (3%)
    unnamed x6, waiting for transfers between devices  241 us
    reduce_scatter x1, waiting for transfers between devices, local(): lax.psum_scatter(partial_out, 'hidden', scatter_dimension=0, tiled=True)  34.3 us
    all_to_all x1, blocking collectives, local(): lax.all_to_all(slot_grads, 'expert', split_axis=1, concat_axis=0, tiled=T...  32.5 us
    reduce_scatter x1, waiting for transfers between devices, local(): lax.psum_scatter(partial_back, 'hidden', scatter_dimension=0, tiled=True)  30 us
    all_to_all x1, waiting for transfers between devices, local(): lax.all_to_all(slot_inputs, 'expert', split_axis=1, concat_axis=0, tiled=...  19.8 us
    all_gather x1, waiting for transfers between devices, local(): lax.all_gather(sent_grads, 'hidden', axis=0, tiled=True)  17.8 us
    all_to_all x1, starting transfers between devices, local(): lax.all_to_all(slot_inputs, 'expert', split_axis=1, concat_axis=0, tiled=...  16.4 us
    all_to_all x1, starting transfers between devices, local(): lax.all_to_all(summed_out.astype(jnp.bfloat16), 'expert', split_axis=0, c...  13.7 us
  transfers between devices with their start and end apart: 8, of which 6 were waited for; matrix products, arithmetic and copies ran while one was open for 7% of the time, Pallas kernels for 0%

commit v1 on v0

--- a/solution.py
+++ b/solution.py
@@ -2,6 +2,9 @@
 import jax.numpy as jnp
 from jax import lax
 from jax.sharding import PartitionSpec as P
+
+
+BOTH = ("expert", "hidden")
 
 
 def gelu_tanh(inputs):
@@ -31,27 +34,27 @@
     slot_grads = jnp.einsum(
         "imn,imd->ind", combine_b, grad_out, preferred_element_type=jnp.float32
     ).astype(jnp.bfloat16)
-    sent_inputs, sent_grads = (
-        lax.all_to_all(slot_inputs, "expert", split_axis=1, concat_axis=0, tiled=True),
-        lax.all_to_all(slot_grads, "expert", split_axis=1, concat_axis=0, tiled=True),
+    both = jnp.stack([slot_inputs, slot_grads], axis=0)
+    both = jnp.transpose(both, (2, 0, 1, 3))
+    experts, _, images, width = both.shape
+    pairs = jnp.broadcast_to(both[:, None], (experts, 2, 2, images, width))
+    pairs = pairs.reshape(2 * experts, 2, images, width)
+    rows = lax.all_to_all(pairs, BOTH, split_axis=0, concat_axis=0, tiled=True)
+    row_inputs = rows[:, 0].reshape(-1, 1, width)
+    row_grads = rows[:, 1].reshape(-1, 1, width)
+    partial_out, partial_back = expert_pass(row_inputs, row_grads, in_weight, out_weight)
+    parts = jnp.stack(
+        [
+            partial_out.astype(jnp.bfloat16).reshape(-1, images, width),
+            partial_back.astype(jnp.bfloat16).reshape(-1, images, width),
+        ],
+        axis=1,
     )
-    row_inputs, row_grads = (
-        lax.all_gather(sent_inputs, "hidden", axis=0, tiled=True),
-        lax.all_gather(sent_grads, "hidden", axis=0, tiled=True),
-    )
-    partial_out, partial_back = expert_pass(row_inputs, row_grads, in_weight, out_weight)
-    summed_out, summed_back = (
-        lax.psum_scatter(partial_out, "hidden", scatter_dimension=0, tiled=True),
-        lax.psum_scatter(partial_back, "hidden", scatter_dimension=0, tiled=True),
-    )
-    slot_outputs, slot_in_grad = (
-        lax.all_to_all(
-            summed_out.astype(jnp.bfloat16), "expert", split_axis=0, concat_axis=1, tiled=True
-        ),
-        lax.all_to_all(
-            summed_back.astype(jnp.bfloat16), "expert", split_axis=0, concat_axis=1, tiled=True
-        ),
-    )
+    halves = lax.all_to_all(parts, BOTH, split_axis=0, concat_axis=0, tiled=True)
+    halves = halves.reshape(experts, 2, 2, images, width).astype(jnp.float32)
+    summed = (halves[:, 0] + halves[:, 1]).astype(jnp.bfloat16)
+    slot_outputs = jnp.transpose(summed[:, 0], (1, 0, 2))
+    slot_in_grad = jnp.transpose(summed[:, 1], (1, 0, 2))
     combine_dw = jnp.einsum(
         "imd,ind->imn", grad_out, slot_outputs, preferred_element_type=jnp.float32
     )
@@ -68,7 +71,9 @@
         "imn,dn->imd", logit_grad, slot_weight, preferred_element_type=jnp.float32
     )
     phi_term = jnp.einsum("imd,imn->dn", tokens, logit_grad, preferred_element_type=jnp.float32)
-    phi_grad = lax.psum_scatter(phi_term, ("expert", "hidden"), scatter_dimension=0, tiled=True)
+    phi_parts = phi_term.astype(jnp.bfloat16).reshape(2 * experts, -1, experts)
+    phi_parts = lax.all_to_all(phi_parts, BOTH, split_axis=0, concat_axis=0, tiled=True)
+    phi_grad = jnp.sum(phi_parts.astype(jnp.float32), axis=0)
     return (input_grad.astype(jnp.bfloat16), phi_grad)
 
 

time: 517 us -> 199 us (0.38)
  waiting for transfers between devices: 356 us -> 8.01 us
  blocking collectives: 32.5 us -> 129 us
  starting transfers between devices: 43.5 us -> 7.15 us
  between operations: 14 us -> 0.9 us
  matrix products: 40.7 us -> 31.4 us
  other arithmetic: 14.5 us -> 7.66 us
    unnamed x6 -> x0, waiting for transfers between devices: 241 us -> none
    all_to_all x1 -> x2, blocking collectives: 32.5 us -> 129 us  [the longest x1 69.2 us: local(): rows = lax.all_to_all(pairs, BOTH, split_axis=0, concat_axis=0, tiled=True)]
    reduce_scatter x2 -> x0, waiting for transfers between devices: 64.3 us -> none  [the longest x1 34.3 us: local(): lax.psum_scatter(partial_out, 'hidden', scatter_dimension=0, tiled=True)]
    all_to_all x3 -> x1, starting transfers between devices: 43.1 us -> 7.15 us  [local(): lax.all_to_all(phi_parts, BOTH, split_axis=0, concat_axis=0, tiled=True)]
    all_to_all x3 -> x1, waiting for transfers between devices: 32.7 us -> 8.01 us  [local(): lax.all_to_all(phi_parts, BOTH, split_axis=0, concat_axis=0, tiled=True)]
    all_gather x2 -> x0, waiting for transfers between devices: 17.9 us -> none  [the longest x1 17.8 us: local(): lax.all_gather(sent_grads, 'hidden', axis=0, tiled=True)]
    all_to_all x2 -> x0, other arithmetic: 6.9 us -> none  [the longest x1 3.84 us: local(): lax.all_to_all(summed_out.astype(jnp.bfloat16), 'expert', split_axis=0, c...]
    unnamed x15 -> x19, local copies, waits for them, and re-layouts: 9.33 us -> 3.67 us
  transfers between devices with their start and end apart: 8 -> 1, of which waited for: 6 -> 1; matrix products, arithmetic and copies ran while one was open for 7% -> 3% of each run, Pallas kernels for 0% -> 0%
where the time goes in v1:
time: 199 us
  blocking collectives  129 us (65%)
  matrix products  31.4 us (16%)
  local copies, waits for them, and re-layouts  14.6 us (7%)
  waiting for transfers between devices  8.01 us (4%)
  other arithmetic  7.66 us (4%)
  starting transfers between devices  7.15 us (4%)
    all_to_all x1, blocking collectives, local(): rows = lax.all_to_all(pairs, BOTH, split_axis=0, concat_axis=0, tiled=True)  69.2 us
    all_to_all x1, blocking collectives, local(): lax.all_to_all(parts, BOTH, split_axis=0, concat_axis=0, tiled=True)  59.7 us
    dot_general x1, matrix products, expert_pass(): jnp.einsum('rkf,kdf->rkd', pre_grad, first, preferred_element_type=jnp.fl...  11.2 us
    all_to_all x1, waiting for transfers between devices, local(): lax.all_to_all(phi_parts, BOTH, split_axis=0, concat_axis=0, tiled=True)  8.01 us
    all_to_all x1, starting transfers between devices, local(): lax.all_to_all(phi_parts, BOTH, split_axis=0, concat_axis=0, tiled=True)  7.15 us
    dot_general x1, matrix products, expert_pass(): jnp.einsum('rkd,kdf->rkf', row_inputs, first, preferred_element_type=jnp....  4.67 us
  transfers between devices with their start and end apart: 1, of which 1 were waited for; matrix products, arithmetic and copies ran while one was open for 3% of the time, Pallas kernels for 0%

profile of v1, /device:TPU:1, one launch (start us, length us, event | category | flops | bytes accessed | tf_op | source)
XLA Modules:
  0.0 198.6 jit_solution(11058697675508875840)
XLA Ops:
  0.6 1.6 fusion.74
  2.3 0.2 fusion.102
  2.5 0.4 fusion.101
  2.9 1.7 fusion.54
  4.6 1.0 fusion.55
  5.8 1.1 copy.18
  6.9 1.3 broadcast_in_dim.2
  8.2 69.2 %all_to_all.15 = bf16[256,2,2,1024]{3,2,1,0:T(2,128)(2,1)S(1)} all-to-all(bf16[256,2,2,1024]{3,2,1,0:T(2,128)(2,1)S(1)} %bitcast.158), channel_id=1, replica_groups=mesh['expert'=128,'hidden'=2] {'expert','hidden'}, dimensions={0} | all-to-all | bytes 4194304 | tf_op jit(solution)/shard_map/all_to_all | solution.py:42
  77.4 1.5 fusion.100
  78.9 1.2 reshape.55
  80.1 0.4 reshape.51
  80.5 4.7 %fusion.21 = f32[512,2048]{1,0:T(8,128)S(1)} fusion(bf16[512,1024]{1,0:T(8,128)(2,1)S(1)} %reshape.51, bf16[1,1024,2048]{2,1,0:T(8,128)(2,1)} %param.8), kind=kOutput, calls=%fused_computation.26 | convolution fusion | flops 2147483648 | bytes 9437184 | tf_op jit(solution)/shard_map/rkd,kdf->rkf/dot_general | solution.py:15
  85.2 1.9 copy-done.8
  87.2 2.7 %fusion.49 = bf16[512,1,1024]{2,0,1:T(8,128)(2,1)S(1)} fusion(bf16[1,2048,1024]{2,1,0:T(8,128)(2,1)S(1)} %copy-done.6, f32[512,2048]{1,0:T(8,128)S(1)} %fusion.21), kind=kOutput, calls=%fused_computation.40 | convolution fusion | flops 2157445120 | bytes 9437184 | tf_op jit(solution)/shard_map/rkf,kfd->rkd/dot_general | solution.py:17
  89.8 11.2 %fusion.44 = bf16[512,1,1024]{2,0,1:T(8,128)(2,1)} fusion(bf16[1,1024,2048]{2,1,0:T(8,128)(2,1)} %param.8, f32[512,2048]{1,0:T(8,128)} %copy-done.8, bf16[512,1024]{1,0:T(8,128)(2,1)S(1)} %copy-done.1, bf16[1,2048,1024]{2,1,0:T(8,128)(2,1)} %param.9), kind=kOutput, calls=%fused_computation.39 | convolution fusion | flops 4316463104 | bytes 14680064 | tf_op jit(solution)/shard_map/rkf,kdf->rkd/dot_general | solution.py:21
  101.1 0.4 stack_reshape.6
  101.5 1.7 stack_reshape.7
  103.2 2.7 %pad_maximum_fusion = bf16[256,2,2,1024]{3,2,1,0:T(2,128)(2,1)S(1)} fusion(bf16[256,1,2,1024]{3,2,1,0:T(2,128)(2,1)S(1)} %bitcast.160, bf16[256,1,2,1024]{3,2,1,0:T(2,128)(2,1)S(1)} %bitcast.159), kind=kLoop, calls=%fused_computation.29 | loop fusion | flops 1048576 | bytes 4194304 | tf_op jit(solution)/shard_map/stack | solution.py:46
  105.9 59.7 %all_to_all.16 = bf16[256,2,2,1024]{3,2,1,0:T(2,128)(2,1)S(1)} all-to-all(bf16[256,2,2,1024]{3,2,1,0:T(2,128)(2,1)S(1)} %pad_maximum_fusion), channel_id=1, replica_groups=mesh['expert'=128,'hidden'=2] {'expert','hidden'}, dimensions={0} | all-to-all | bytes 4194304 | tf_op jit(solution)/shard_map/all_to_all | solution.py:53
  165.6 2.4 %fusion.99 = (f32[128,1,2,2,1024]{4,3,2,1,0:T(2,128)S(1)}, f32[128,1,2,2,1024]{4,3,2,1,0:T(2,128)S(1)}) fusion(bf16[128,2,2,2,1024]{4,3,2,1,0:T(2,128)(2,1)S(1)} %bitcast.157), kind=kLoop, calls=%fused_computation.97 | loop fusion | bytes 8388608 | tf_op jit(solution)/shard_map/slice | solution.py:55
  168.0 2.3 %fusion.68 = bf16[128,2,2,1024]{3,0,2,1:T(8,128)(2,1)S(1)} fusion(f32[128,1,2,2,1024]{4,3,2,1,0:T(2,128)S(1)} %get-tuple-element.7, f32[128,1,2,2,1024]{4,3,2,1,0:T(2,128)S(1)} %get-tuple-element.6), kind=kLoop, calls=%fused_computation.60 | loop fusion | flops 1048576 | bytes 5242880 | tf_op jit(solution)/shard_map/convert_element_type | solution.py:55
  170.3 0.4 convolution_bitcast_fusion.2
  170.7 0.4 convolution_bitcast_fusion.1
  171.1 0.1 fusion.64
  171.3 3.2 %fusion.59 = bf16[1024,128]{0,1:T(8,128)(2,1)S(1)} fusion(f32[2,196,128]{2,1,0:T(8,128)S(1)} %fusion.64, f32[2,196,128]{2,1,0:T(8,128)S(1)} %convolution_bitcast_fusion.2, bf16[2,196,1024]{2,0,1:T(2,128)(2,1)} %param.5, f32[2,196,128]{2,1,0:T(8,128)S(1)} %get-tuple-element.11, f32[2,196]{1,0:T(2,128)S(1)} %get-tuple-element.10), kind=kOutput, calls=%fused_computation.49 | convolution fusion | flops 103243272 | bytes 1668640 | tf_op jit(solution)/shard_map/imd,imn->dn/dot_general | solution.py:73
  174.5 0.8 copy.26
  175.3 7.1 %all-to-all-start.2 = ((bf16[256,4,128]{2,1,0:T(4,128)(2,1)}), bf16[256,4,128]{2,1,0:T(4,128)(2,1)}, u32[]{:S(2)}, u32[]{:S(2)}) async-start(bf16[256,4,128]{2,1,0:T(4,128)(2,1)} %bitcast.39), calls=%async_computation.2 | async-start | bytes 524288 | tf_op jit(solution)/shard_map/all_to_all | solution.py:75
  182.5 1.4 fusion.76
  183.9 3.1 %add_convert_fusion = bf16[2,196,1024]{2,1,0:T(8,128)(2,1)S(1)} fusion(f32[2,196,1024]{2,1,0:T(8,128)S(1)} %fusion.76, f32[2,196,128]{2,1,0:T(8,128)} %copy-done.4, f32[2,196,128]{2,1,0:T(8,128)} %copy-done.5, bf16[1024,128]{1,0:T(8,128)(2,1)} %param.7, f32[2,196,128]{2,1,0:T(8,128)} %copy-done.3, f32[2,196]{1,0:T(2,128)S(1)} %get-tuple-element.10), kind=kOutput, calls=%fused_computation.36 | convolution fusion | flops 103915016 | bytes 3274272 | tf_op jit(solution)/shard_map/imn,dn->imd/dot_general | solution.py:70
  187.0 1.7 copy.27
  188.7 8.0 %all-to-all-done.2 = bf16[256,4,128]{2,1,0:T(4,128)(2,1)} async-done(((bf16[256,4,128]{2,1,0:T(4,128)(2,1)}), bf16[256,4,128]{2,1,0:T(4,128)(2,1)}, u32[]{:S(2)}, u32[]{:S(2)}) %all-to-all-start.2) | async-done | bytes 262176 | tf_op jit(solution)/shard_map/all_to_all | solution.py:75
  196.8 1.8 convert_reduce_fusion
  (18 shorter events, 0.1 us)
Async XLA Ops:
  0.6 4.0 %copy-start = (bf16[2,196,1024]{2,0,1:T(2,128)(2,1)S(1)}, bf16[2,196,1024]{2,0,1:T(2,128)(2,1)}, u32[]{:S(2)}) copy-start(bf16[2,196,1024]{2,0,1:T(2,128)(2,1)} %param.6) | copy-start | bytes 2408452
  2.3 4.6 %copy-start.2 = (f32[2,196,128]{2,1,0:T(8,128)}, f32[2,196,128]{2,1,0:T(8,128)S(1)}, u32[]{:S(2)}) copy-start(f32[2,196,128]{2,1,0:T(8,128)S(1)} %fusion.74) | copy-start | bytes 602116
  2.9 168.4 %copy-start.3 = (f32[2,196,128]{2,1,0:T(8,128)}, f32[2,196,128]{2,1,0:T(8,128)S(1)}, u32[]{:S(2)}) copy-start(f32[2,196,128]{2,1,0:T(8,128)S(1)} %get-tuple-element.11) | copy-start | bytes 602116
  80.5 6.6 %copy-start.6 = (bf16[1,2048,1024]{2,1,0:T(8,128)(2,1)S(1)}, bf16[1,2048,1024]{2,1,0:T(8,128)(2,1)}, u32[]{:S(2)}) copy-start(bf16[1,2048,1024]{2,1,0:T(8,128)(2,1)} %param.9) | copy-start | bytes 12582916
  85.2 1.9 copy-start.8
  87.1 2.7 %copy-start.1 = (bf16[512,1024]{1,0:T(8,128)(2,1)S(1)}, bf16[512,1024]{1,0:T(8,128)(2,1)}, u32[]{:S(2)}) copy-start(bf16[512,1024]{1,0:T(8,128)(2,1)} %reshape.55) | copy-start | bytes 3145732
  168.0 2.7 %copy-start.7 = (bf16[2,196,1024]{2,0,1:T(2,128)(2,1)S(1)}, bf16[2,196,1024]{2,0,1:T(2,128)(2,1)}, u32[]{:S(2)}) copy-start(bf16[2,196,1024]{2,0,1:T(2,128)(2,1)} %param.5) | copy-start | bytes 2408452
  170.7 4.6 %copy-start.5 = (f32[2,196,128]{2,1,0:T(8,128)}, f32[2,196,128]{2,1,0:T(8,128)S(1)}, u32[]{:S(2)}) copy-start(f32[2,196,128]{2,1,0:T(8,128)S(1)} %convolution_bitcast_fusion.2) | copy-start | bytes 602116
  171.3 4.1 %copy-start.4 = (f32[2,196,128]{2,1,0:T(8,128)}, f32[2,196,128]{2,1,0:T(8,128)S(1)}, u32[]{:S(2)}) copy-start(f32[2,196,128]{2,1,0:T(8,128)S(1)} %fusion.64) | copy-start | bytes 602116
  175.3 21.4 %all-to-all-start.2 = ((bf16[256,4,128]{2,1,0:T(4,128)(2,1)}), bf16[256,4,128]{2,1,0:T(4,128)(2,1)}, u32[]{:S(2)}, u32[]{:S(2)}) async-start(bf16[256,4,128]{2,1,0:T(4,128)(2,1)} %bitcast.39), calls=%async_computation.2 | async-start | bytes 524288 | tf_op jit(solution)/shard_map/all_to_all | solution.py:75

commit v2 on v0

v2 whole, which is shorter than its diff:
```python
import jax
import jax.numpy as jnp
from jax import lax
from jax.experimental import pallas as pl
from jax.experimental.pallas import tpu as pltpu
from jax.sharding import Mesh
from jax.sharding import PartitionSpec as P

ALL = ("x", "y", "z", "core", "half")
PLANE = ("x", "y", "core")
RING = ("z", "half")
FAR, NEAR, WIDE = (2, -2), (-1, 1), (-3, 3)
GELU_A = 0.7978845608028654
GELU_B = 0.7978845608028654 * 0.044715


def hops(steps, back=False):
    pairs = [(i, (i + steps[i % 2]) % 8) for i in range(8)]
    return [(b, a) for a, b in pairs] if back else pairs


def swap(block):
    return lax.ppermute(block, "half", [(0, 1), (1, 0)])


def expert_kernel(count, *refs):
    blocks = refs[:count]
    first, second = refs[count], refs[count + 1]
    outs = refs[count + 2 : 2 * count + 2]
    rows, acc = refs[2 * count + 2 :]
    size = blocks[0].shape[1]
    step = pl.program_id(0)

    @pl.when(step == 0)
    def _():
        for at, block in enumerate(blocks):
            rows[:, at * size : (at + 1) * size, :] = block[...]
        acc[...] = jnp.zeros_like(acc)

    contract_last = (((1,), (1,)), ((), ()))
    pre = jnp.dot(rows[0], first[...], preferred_element_type=jnp.float32)
    act_grad = lax.dot_general(
        rows[1], second[...], contract_last, preferred_element_type=jnp.float32
    )
    square = pre * pre
    bent = jnp.tanh(pre * (GELU_A + GELU_B * square))
    gate = 0.5 + 0.5 * bent
    activation = (pre * gate).astype(jnp.bfloat16)
    slope = gate + (0.5 * pre) * (1.0 - bent * bent) * (GELU_A + 3.0 * GELU_B * square)
    pre_grad = (act_grad * slope).astype(jnp.bfloat16)
    acc[0] += jnp.dot(activation, second[...], preferred_element_type=jnp.float32)
    acc[1] += lax.dot_general(
        pre_grad, first[...], contract_last, preferred_element_type=jnp.float32
    )

    @pl.when(step == pl.num_programs(0) - 1)
    def _():
        for at, out in enumerate(outs):
            out[...] = acc[:, at * size : (at + 1) * size, :].astype(out.dtype)


def expert_pass(mine, other, first, second):
    blocks = mine + other
    count = len(blocks)
    _, size, width = blocks[0].shape
    hidden = first.shape[1]
    part = 512
    whole = pl.BlockSpec((2, size, width), lambda j: (0, 0, 0))
    out = pl.pallas_call(
        lambda *refs: expert_kernel(count, *refs),
        grid=(hidden // part,),
        in_specs=[whole] * count
        + [
            pl.BlockSpec((width, part), lambda j: (0, j)),
            pl.BlockSpec((part, width), lambda j: (j, 0)),
        ],
        out_specs=[whole] * count,
        out_shape=[jax.ShapeDtypeStruct((2, size, width), jnp.float32)] * len(mine)
        + [jax.ShapeDtypeStruct((2, size, width), jnp.bfloat16)] * len(other),
        scratch_shapes=[
            pltpu.VMEM((2, count * size, width), jnp.bfloat16),
            pltpu.VMEM((2, count * size, width), jnp.float32),
        ],
        compiler_params=pltpu.CompilerParams(vmem_limit_bytes=40 * 2**20),
        cost_estimate=pl.CostEstimate(
            flops=8 * count * size * width * hidden,
            bytes_accessed=4 * width * hidden,
            transcendentals=count * size * hidden,
        ),
        name="expert_rows",
    )(*blocks, first, second)
    return out[: len(mine)], out[len(mine) :]


def slot_order(slots):
    at = lax.broadcasted_iota(jnp.int32, (slots, slots), 1)
    turn = 1 - 2 * lax.axis_index("half")
    kind = at % 4
    shift = jnp.where(kind == 1, turn, jnp.where(kind == 2, -turn, jnp.where(kind == 3, 2, 0)))
    plane = at // 4
    owner = (plane // 2) * 8 + ((lax.axis_index("z") + shift + 4) % 4) * 2 + plane % 2
    return (lax.broadcasted_iota(jnp.int32, (slots, slots), 0) == owner).astype(jnp.bfloat16)


def local(tokens, grad_out, slot_weight, in_weight, out_weight):
    images, _, width = tokens.shape
    slots = slot_weight.shape[1]
    order = slot_order(slots)
    slot_weight = jnp.dot(
        slot_weight, order, preferred_element_type=jnp.float32
    ).astype(jnp.bfloat16)
    logits = jnp.einsum("imd,dn->imn", tokens, slot_weight, preferred_element_type=jnp.float32)
    dispatch = jax.nn.softmax(logits, axis=1)
    combine = jax.nn.softmax(logits, axis=2)
    dispatch_b = dispatch.astype(jnp.bfloat16)
    combine_b = combine.astype(jnp.bfloat16)
    slot_inputs = jnp.einsum(
        "imn,imd->ind", dispatch_b, tokens, preferred_element_type=jnp.float32
    ).astype(jnp.bfloat16)
    slot_grads = jnp.einsum(
        "imn,imd->ind", combine_b, grad_out, preferred_element_type=jnp.float32
    ).astype(jnp.bfloat16)
    both = jnp.transpose(jnp.stack([slot_inputs, slot_grads], axis=0), (2, 0, 1, 3))
    both = both.reshape(slots // 4, 4, 2, images, width)
    both = lax.all_to_all(both, PLANE, split_axis=0, concat_axis=0, tiled=True)
    both = jnp.transpose(both, (1, 2, 0, 3, 4)).reshape(4, 2, -1, width)

    far = lax.ppermute(both[1], RING, hops(FAR))
    wide = lax.ppermute(both[3], RING, hops(WIDE))
    near = lax.ppermute(both[2], RING, hops(NEAR))
    own = both[0]
    far_pair, wide_pair = swap(far), swap(wide)
    own_pair, near_pair = swap(own), swap(near)
    first, second = in_weight[0], out_weight[0]
    mine_a, other_a = expert_pass([wide, far], [wide_pair, far_pair], first, second)
    mine_b, other_b = expert_pass([own, near], [own_pair, near_pair], first, second)

    def added(partial, sent):
        return (partial + swap(sent).astype(jnp.float32)).astype(jnp.bfloat16)

    wide_sum, far_sum = (added(a, b) for a, b in zip(mine_a, other_a))
    own_sum, near_sum = (added(a, b) for a, b in zip(mine_b, other_b))
    wide_sum = lax.ppermute(wide_sum, RING, hops(WIDE, True))
    far_sum = lax.ppermute(far_sum, RING, hops(FAR, True))
    near_sum = lax.ppermute(near_sum, RING, hops(NEAR, True))
    sums = jnp.stack([own_sum, far_sum, near_sum, wide_sum], axis=0)
    sums = jnp.transpose(sums.reshape(4, 2, slots // 4, images, width), (2, 0, 1, 3, 4))
    sums = lax.all_to_all(sums, PLANE, split_axis=0, concat_axis=0, tiled=True)
    sums = jnp.transpose(sums.reshape(slots, 2, images, width), (1, 2, 0, 3))
    slot_outputs, slot_in_grad = sums[0], sums[1]

    combine_dw = jnp.einsum(
        "imd,ind->imn", grad_out, slot_outputs, preferred_element_type=jnp.float32
    )
    combine_dl = combine * (combine_dw - jnp.sum(combine * combine_dw, axis=2, keepdims=True))
    dispatch_dw = jnp.einsum(
        "imd,ind->imn", tokens, slot_in_grad, preferred_element_type=jnp.float32
    )
    dispatch_dl = dispatch * (dispatch_dw - jnp.sum(dispatch * dispatch_dw, axis=1, keepdims=True))
    logit_grad = (combine_dl + dispatch_dl).astype(jnp.bfloat16)
    input_grad = jnp.einsum(
        "imn,ind->imd", dispatch_b, slot_in_grad, preferred_element_type=jnp.float32
    )
    input_grad = input_grad + jnp.einsum(
        "imn,dn->imd", logit_grad, slot_weight, preferred_element_type=jnp.float32
    )
    phi_term = jnp.einsum("imd,imn->dn", tokens, logit_grad, preferred_element_type=jnp.float32)
    phi_term = lax.dot_general(
        phi_term.astype(jnp.bfloat16),
        order,
        (((1,), (1,)), ((), ())),
        preferred_element_type=jnp.float32,
    )
    parts = phi_term.astype(jnp.bfloat16).reshape(2 * slots, -1, slots)
    parts = lax.all_to_all(parts, ALL, split_axis=0, concat_axis=0, tiled=True)
    phi_grad = jnp.sum(parts.astype(jnp.float32), axis=0)
    return (input_grad.astype(jnp.bfloat16), phi_grad)


def solution(mesh):
    expert = ("x", "y", "z", "core")
    fine = Mesh(mesh.devices.reshape(4, 4, 4, 2, 2), ALL)
    placed = (
        P(ALL, None, None),
        P(ALL, None, None),
        P(),
        P(expert, None, "half"),
        P(expert, "half", None),
    )
    return jax.shard_map(
        local,
        mesh=fine,
        in_specs=placed,
        out_specs=(P(ALL, None, None), P(ALL, None)),
        check_vma=False,
    )
```

time: 517 us -> 177 us (0.34)
  waiting for transfers between devices: 356 us -> 40 us
  matrix products: 40.7 us -> 11.1 us
  blocking collectives: 32.5 us -> 54.9 us
  between operations: 14 us -> 1.06 us
  Pallas kernels: 0 us -> 12.1 us
  other arithmetic: 14.5 us -> 4.07 us
  local copies, waits for them, and re-layouts: 15.2 us -> 10 us
    unnamed x6 -> x0, waiting for transfers between devices: 241 us -> none
    reduce_scatter x2 -> x0, waiting for transfers between devices: 64.3 us -> none  [the longest x1 34.3 us: local(): lax.psum_scatter(partial_out, 'hidden', scatter_dimension=0, tiled=True)]
    ppermute x0 -> x14, starting transfers between devices: none -> 33.3 us  [the longest x1 7.46 us: local(): wide_sum = lax.ppermute(wide_sum, RING, hops(WIDE, True))]
    all_to_all x3 -> x1, starting transfers between devices: 43.1 us -> 10.3 us  [local(): parts = lax.all_to_all(parts, ALL, split_axis=0, concat_axis=0, tiled=True)]
    ppermute x0 -> x14, waiting for transfers between devices: none -> 31.9 us  [the longest x1 13.5 us: local(): near = lax.ppermute(both[2], RING, hops(NEAR))]
    dot_general x4 -> x2, matrix products: 30.3 us -> 3.88 us  [the longest x1 2.6 us: local(): lax.dot_general(phi_term.astype(jnp.bfloat16), order, (((1,), (1,)), ((),...]
    all_to_all x3 -> x1, waiting for transfers between devices: 32.7 us -> 8.1 us  [local(): parts = lax.all_to_all(parts, ALL, split_axis=0, concat_axis=0, tiled=True)]
    all_to_all x1 -> x2, blocking collectives: 32.5 us -> 54.9 us  [the longest x1 29.6 us: local(): sums = lax.all_to_all(sums, PLANE, split_axis=0, concat_axis=0, tiled=True)]
  transfers between devices with their start and end apart: 8 -> 15, of which waited for: 6 -> 6; matrix products, arithmetic and copies ran while one was open for 7% -> 4% of each run, Pallas kernels for 0% -> 7%
where the time goes in v2:
time: 177 us
  blocking collectives  54.9 us (31%)
  starting transfers between devices  43.6 us (25%)
  waiting for transfers between devices  40 us (23%)
  Pallas kernels  12.1 us (7%)
  matrix products  11.1 us (6%)
  local copies, waits for them, and re-layouts  10 us (6%)
  other arithmetic  4.07 us (2%)
    all_to_all x1, blocking collectives, local(): sums = lax.all_to_all(sums, PLANE, split_axis=0, concat_axis=0, tiled=True)  29.6 us
    all_to_all x1, blocking collectives, local(): both = lax.all_to_all(both, PLANE, split_axis=0, concat_axis=0, tiled=True)  25.3 us
    ppermute x1, waiting for transfers between devices, local(): near = lax.ppermute(both[2], RING, hops(NEAR))  13.5 us
    pallas_call x2, Pallas kernels, expert_pass(): pl.pallas_call(lambda *refs: expert_kernel(count, *refs), grid=(hidden //...  12.1 us
    all_to_all x1, starting transfers between devices, local(): parts = lax.all_to_all(parts, ALL, split_axis=0, concat_axis=0, tiled=True)  10.3 us
    ppermute x8, waiting for transfers between devices, swap(): return lax.ppermute(block, 'half', [(0, 1), (1, 0)])  8.48 us
    all_to_all x1, waiting for transfers between devices, local(): parts = lax.all_to_all(parts, ALL, split_axis=0, concat_axis=0, tiled=True)  8.1 us
    ppermute x1, starting transfers between devices, local(): wide_sum = lax.ppermute(wide_sum, RING, hops(WIDE, True))  7.46 us
  transfers between devices with their start and end apart: 15, of which 6 were waited for; matrix products, arithmetic and copies ran while one was open for 4% of the time, Pallas kernels for 7%

profile of v2, /device:TPU:1, one launch (start us, length us, event | category | flops | bytes accessed | tf_op | source)
XLA Modules:
  0.0 176.8 jit_solution(16968202838415760252)
XLA Ops:
  0.7 1.3 fusion.9
  3.6 1.0 fusion.5
  4.8 1.1 copy.31
  5.9 25.3 %all_to_all.15 = bf16[32,4,2,2,1024]{4,3,2,1,0:T(2,128)(2,1)S(1)} all-to-all(bf16[32,4,2,2,1024]{4,3,2,1,0:T(2,128)(2,1)S(1)} %bitcast.51), channel_id=1, replica_groups=mesh['x'=4,'y'=4,'z'=4,'core'=2,'half'=2] {'x','y','core'}, dimensions={0} | all-to-all | bytes 2097152 | tf_op jit(solution)/shard_map/all_to_all | solution.py:125
  31.2 0.8 fusion.51
  32.3 5.7 %collective-permute-start = (bf16[2,64,1024]{2,1,0:T(8,128)(2,1)S(1)}, bf16[2,64,1024]{2,1,0:T(8,128)(2,1)S(1)}, u32[]{:S(2)}, u32[]{:S(2)}) collective-permute-start(bf16[2,64,1024]{2,1,0:T(8,128)(2,1)S(1)} %squeeze.25), channel_id=1, source_target_pairs={{0,13},{1,4},{4,1},{5,8},{8,5},{9,12},{12,9},{13,0},{2,15},{3,6},{... | collective-permute-start | bytes 786440 | tf_op jit(solution)/shard_map/ppermute | solution.py:130
  38.7 1.7 collective-permute-start.4
  41.1 13.5 %collective-permute-done.refs_1_ = bf16[2,64,1024]{2,1,0:T(8,128)(2,1)S(1)} collective-permute-done((bf16[2,64,1024]{2,1,0:T(8,128)(2,1)S(1)}, bf16[2,64,1024]{2,1,0:T(8,128)(2,1)S(1)}, u32[]{:S(2)}, u32[]{:S(2)}) %collective-permute-start) | collective-permute-done | bytes 262176 | tf_op jit(solution)/shard_map/ppermute | solution.py:130
  54.6 5.8 %collective-permute-done.4.refs_0_ = bf16[2,64,1024]{2,1,0:T(8,128)(2,1)S(1)} collective-permute-done((bf16[2,64,1024]{2,1,0:T(8,128)(2,1)S(1)}, bf16[2,64,1024]{2,1,0:T(8,128)(2,1)S(1)}, u32[]{:S(2)}, u32[]{:S(2)}) %collective-permute-start.4) | collective-permute-done | bytes 262176 | tf_op jit(solution)/shard_map/ppermute | solution.py:129
  60.4 2.6 %collective-permute-start.6 = (bf16[2,64,1024]{2,1,0:T(8,128)(2,1)S(1)}, bf16[2,64,1024]{2,1,0:T(8,128)(2,1)S(1)}, u32[]{:S(2)}, u32[]{:S(2)}) collective-permute-start(bf16[2,64,1024]{2,1,0:T(8,128)(2,1)S(1)} %collective-permute-done.4.refs_0_), channel_id=1, source_target_pairs={{0,1},{1,0},{2,3},{3,2},{4,5},{5,4},{6,7},{7,6},{8,9},{9,8},{10,11... | collective-permute-start | bytes 786440 | tf_op jit(solution)/shard_map/ppermute | solution.py:23
  63.0 0.7 collective-permute-done.2.refs_3_
  63.7 2.2 %copy-done.1 = bf16[1,1024,2048]{2,1,0:T(8,128)(2,1)S(1)} copy-done((bf16[1,1024,2048]{2,1,0:T(8,128)(2,1)S(1)}, bf16[1,1024,2048]{2,1,0:T(8,128)(2,1)}, u32[]{:S(2)}) %copy-start.1) | copy-done | bytes 4194328
  65.9 2.2 %copy-done.3 = bf16[1,2048,1024]{2,1,0:T(8,128)(2,1)S(1)} copy-done((bf16[1,2048,1024]{2,1,0:T(8,128)(2,1)S(1)}, bf16[1,2048,1024]{2,1,0:T(8,128)(2,1)}, u32[]{:S(2)}) %copy-start.3) | copy-done | bytes 4194328
  68.0 6.1 %expert_rows.2 = (f32[2,64,1024]{2,1,0:T(8,128)S(1)}, f32[2,64,1024]{2,1,0:T(8,128)S(1)}, bf16[2,64,1024]{2,1,0:T(8,128)(2,1)S(1)}, bf16[2,64,1024]{2,1,0:T(8,128)(2,1)S(1)}) custom-call(bf16[2,64,1024]{2,1,0:T(8,128)(2,1)S(1)} %squeeze.24.refs_0_, bf16[2,64,1024]{2,1,0:T(8,128)(2,1)S(1)} %collective-permute-done.refs_1_, ...), custom_call_target="tpu_custom_call" | custom-call | flops 4294967296 | bytes 8388608 | tf_op jit(solution)/shard_map/expert_rows/pallas_call | solution.py:69
  74.1 1.6 collective-permute-start.10
  75.7 6.0 %expert_rows.3 = (f32[2,64,1024]{2,1,0:T(8,128)S(1)}, f32[2,64,1024]{2,1,0:T(8,128)S(1)}, bf16[2,64,1024]{2,1,0:T(8,128)(2,1)S(1)}, bf16[2,64,1024]{2,1,0:T(8,128)(2,1)S(1)}) custom-call(bf16[2,64,1024]{2,1,0:T(8,128)(2,1)S(1)} %collective-permute-done.4.refs_0_, bf16[2,64,1024]{2,1,0:T(8,128)(2,1)S(1)} %collective-permute-done.5.refs_1_, ...), custom_call_target="tpu_custom_call" | custom-call | flops 4294967296 | bytes 8388608 | tf_op jit(solution)/shard_map/expert_rows/pallas_call | solution.py:69
  81.7 1.3 collective-permute-start.8
  83.3 1.3 collective-permute-start.12
  84.6 5.4 %collective-permute-start.11 = (bf16[2,64,1024]{2,1,0:T(8,128)(2,1)S(1)}, bf16[2,64,1024]{2,1,0:T(8,128)(2,1)S(1)}, u32[]{:S(2)}, u32[]{:S(2)}) collective-permute-start(bf16[2,64,1024]{2,1,0:T(8,128)(2,1)S(1)} %add_convert_fusion.2), channel_id=1, source_target_pairs={{13,0},{4,1},{1,4},{8,5},{5,8},{12,9},{9,12},{0,13},{15,2},{6,3},{... | collective-permute-start | bytes 786440 | tf_op jit(solution)/shard_map/ppermute | solution.py:145
  90.1 5.5 %collective-permute-start.9 = (bf16[2,64,1024]{2,1,0:T(8,128)(2,1)S(1)}, bf16[2,64,1024]{2,1,0:T(8,128)(2,1)S(1)}, u32[]{:S(2)}, u32[]{:S(2)}) collective-permute-start(bf16[2,64,1024]{2,1,0:T(8,128)(2,1)S(1)} %add_convert_fusion.3), channel_id=1, source_target_pairs={{4,0},{13,1},{8,4},{1,5},{12,8},{5,9},{0,12},{9,13},{6,2},{15,3},{... | collective-permute-start | bytes 786440 | tf_op jit(solution)/shard_map/ppermute | solution.py:144
  95.6 7.8 %collective-permute-done.12 = bf16[2,64,1024]{2,1,0:T(8,128)(2,1)S(1)} collective-permute-done((bf16[2,64,1024]{2,1,0:T(8,128)(2,1)S(1)}, bf16[2,64,1024]{2,1,0:T(8,128)(2,1)S(1)}, u32[]{:S(2)}, u32[]{:S(2)}) %collective-permute-start.12) | collective-permute-done | bytes 262176 | tf_op jit(solution)/shard_map/ppermute | solution.py:23
  103.5 7.5 %collective-permute-start.13 = (bf16[2,64,1024]{2,1,0:T(8,128)(2,1)S(1)}, bf16[2,64,1024]{2,1,0:T(8,128)(2,1)S(1)}, u32[]{:S(2)}, u32[]{:S(2)}) collective-permute-start(bf16[2,64,1024]{2,1,0:T(8,128)(2,1)S(1)} %add_convert_fusion.1), channel_id=1, source_target_pairs={{9,0},{8,1},{13,4},{12,5},{1,8},{0,9},{5,12},{4,13},{11,2},{10,3},... | collective-permute-start | bytes 786440 | tf_op jit(solution)/shard_map/ppermute | solution.py:143
  111.4 4.1 %collective-permute-done.13 = bf16[2,64,1024]{2,1,0:T(8,128)(2,1)S(1)} collective-permute-done((bf16[2,64,1024]{2,1,0:T(8,128)(2,1)S(1)}, bf16[2,64,1024]{2,1,0:T(8,128)(2,1)S(1)}, u32[]{:S(2)}, u32[]{:S(2)}) %collective-permute-start.13) | collective-permute-done | bytes 262176 | tf_op jit(solution)/shard_map/ppermute | solution.py:143
  115.5 1.2 copy_bitcast_fusion.1
  116.7 29.6 %all_to_all.16 = bf16[32,4,2,2,1024]{4,3,2,1,0:T(2,128)(2,1)S(1)} all-to-all(bf16[32,4,2,2,1024]{4,3,2,1,0:T(2,128)(2,1)S(1)} %copy_bitcast_fusion.1), channel_id=1, replica_groups=mesh['x'=4,'y'=4,'z'=4,'core'=2,'half'=2] {'x','y','core'}, dimensions={0} | all-to-all | bytes 2097152 | tf_op jit(solution)/shard_map/all_to_all | solution.py:148
  147.7 2.6 %convolution_convert_fusion.3 = bf16[1024,128]{1,0:T(8,128)(2,1)} fusion(f32[2,196,128]{2,1,0:T(8,128)S(1)} %fusion.14, f32[2,196,128]{2,1,0:T(8,128)S(1)} %convolution_bitcast_fusion.3, bf16[2,196,1024]{2,0,1:T(2,128)(2,1)S(1)} %copy-done, s32[]{:T(128)S(6)} %neg.3, s32[]{:T(128)S(6)} %sub.50, s32[128]{0:T(128)S(1)} %get-tuple-element.33, ...), kind=kOutput, calls=%fused_computation.12 | convolution fusion | flops 137666048 | bytes 1670956 | tf_op jit(solution)/shard_map/dot_general | solution.py:168
  150.3 10.3 %all-to-all-start.2 = ((bf16[256,4,128]{2,1,0:T(4,128)(2,1)}), bf16[256,4,128]{2,1,0:T(4,128)(2,1)}, u32[]{:S(2)}, u32[]{:S(2)}) async-start(bf16[256,4,128]{2,1,0:T(4,128)(2,1)} %bitcast.17), calls=%async_computation.2 | async-start | bytes 524288 | tf_op jit(solution)/shard_map/all_to_all | solution.py:175
  160.6 1.4 fusion.25
  162.1 3.1 %add_convert_fusion = bf16[2,196,1024]{2,1,0:T(8,128)(2,1)S(1)} fusion(f32[2,196,1024]{2,1,0:T(8,128)S(1)} %fusion.25, bf16[128,1024,1]{1,0,2:T(8,128)(2,1)} %copy-done.5, f32[2,196,128]{2,1,0:T(8,128)} %copy-done.7, f32[2,196,128]{2,1,0:T(8,128)} %copy-done.8, f32[2,196,128]{2,1,0:T(8,128)} %copy-done.6, f32[2,196]{1,0:T(2,128)S(1)} %get-tuple-element.26), kind=kOutput, calls=%fused_computation.4 | convolution fusion | flops 103915016 | bytes 3274272 | tf_op jit(solution)/shard_map/imn,dn->imd/dot_general | solution.py:164
  165.2 1.7 copy.30
  166.9 8.1 %all-to-all-done.2 = bf16[256,4,128]{2,1,0:T(4,128)(2,1)} async-done(((bf16[256,4,128]{2,1,0:T(4,128)(2,1)}), bf16[256,4,128]{2,1,0:T(4,128)(2,1)}, u32[]{:S(2)}, u32[]{:S(2)}) %all-to-all-start.2) | async-done | bytes 262176 | tf_op jit(solution)/shard_map/all_to_all | solution.py:175
  175.0 1.8 %convert_reduce_fusion = f32[4,128]{1,0:T(4,128)} fusion(bf16[256,4,128]{2,1,0:T(4,128)(2,1)} %all-to-all-done.2), kind=kLoop, calls=%fused_computation.39 | loop fusion | flops 261632 | bytes 264192 | tf_op jit(solution)/shard_map/reduce_sum | solution.py:176
  (62 shorter events, 5.6 us)
Async XLA Ops:
  0.6 1.4 copy-start
  2.0 1.1 copy-start.5
  2.4 2.3 %copy-start.4 = (f32[2,196,128]{2,1,0:T(8,128)}, f32[2,196,128]{2,1,0:T(8,128)S(1)}, u32[]{:S(2)}) copy-start(f32[2,196,128]{2,1,0:T(8,128)S(1)} %convolution_bitcast_fusion.1) | copy-start | bytes 602116
  2.4 1.2 copy-start.9
  3.1 144.5 %copy-start.6 = (f32[2,196,128]{2,1,0:T(8,128)}, f32[2,196,128]{2,1,0:T(8,128)S(1)}, u32[]{:S(2)}) copy-start(f32[2,196,128]{2,1,0:T(8,128)S(1)} %get-tuple-element.27) | copy-start | bytes 602116
  32.3 22.3 %collective-permute-start = (bf16[2,64,1024]{2,1,0:T(8,128)(2,1)S(1)}, bf16[2,64,1024]{2,1,0:T(8,128)(2,1)S(1)}, u32[]{:S(2)}, u32[]{:S(2)}) collective-permute-start(bf16[2,64,1024]{2,1,0:T(8,128)(2,1)S(1)} %squeeze.25), channel_id=1, source_target_pairs={{0,13},{1,4},{4,1},{5,8},{8,5},{9,12},{12,9},{13,0},{2,15},{3,6},{... | collective-permute-start | bytes 786440 | tf_op jit(solution)/shard_map/ppermute | solution.py:130
  38.7 21.7 %collective-permute-start.4 = (bf16[2,64,1024]{2,1,0:T(8,128)(2,1)S(1)}, bf16[2,64,1024]{2,1,0:T(8,128)(2,1)S(1)}, u32[]{:S(2)}, u32[]{:S(2)}) collective-permute-start(bf16[2,64,1024]{2,1,0:T(8,128)(2,1)S(1)} %squeeze.28), channel_id=1, source_target_pairs={{0,9},{1,8},{4,13},{5,12},{8,1},{9,0},{12,5},{13,4},{2,11},{3,10},... | collective-permute-start | bytes 786440 | tf_op jit(solution)/shard_map/ppermute | solution.py:129
  40.5 22.4 %collective-permute-start.5 = (bf16[2,64,1024]{2,1,0:T(8,128)(2,1)S(1)}, bf16[2,64,1024]{2,1,0:T(8,128)(2,1)S(1)}, u32[]{:S(2)}, u32[]{:S(2)}) collective-permute-start(bf16[2,64,1024]{2,1,0:T(8,128)(2,1)S(1)} %squeeze.29), channel_id=1, source_target_pairs={{0,4},{1,13},{4,8},{5,1},{8,12},{9,5},{12,0},{13,9},{2,6},{3,15},{... | collective-permute-start | bytes 786440 | tf_op jit(solution)/shard_map/ppermute | solution.py:128
  41.1 21.9 %collective-permute-start.1 = (bf16[2,64,1024]{2,1,0:T(8,128)(2,1)S(1)}, bf16[2,64,1024]{2,1,0:T(8,128)(2,1)S(1)}, u32[]{:S(2)}, u32[]{:S(2)}) collective-permute-start(bf16[2,64,1024]{2,1,0:T(8,128)(2,1)S(1)} %squeeze.24.refs_0_), channel_id=1, source_target_pairs={{0,1},{1,0},{2,3},{3,2},{4,5},{5,4},{6,7},{7,6},{8,9},{9,8},{10,11... | collective-permute-start | bytes 786440 | tf_op jit(solution)/shard_map/ppermute | solution.py:23
  54.6 9.1 %collective-permute-start.2 = (bf16[2,64,1024]{2,1,0:T(8,128)(2,1)S(1)}, bf16[2,64,1024]{2,1,0:T(8,128)(2,1)S(1)}, u32[]{:S(2)}, u32[]{:S(2)}) collective-permute-start(bf16[2,64,1024]{2,1,0:T(8,128)(2,1)S(1)} %collective-permute-done.refs_1_), channel_id=1, source_target_pairs={{0,1},{1,0},{2,3},{3,2},{4,5},{5,4},{6,7},{7,6},{8,9},{9,8},{10,11... | collective-permute-start | bytes 786440 | tf_op jit(solution)/shard_map/ppermute | solution.py:23
  60.4 15.3 %collective-permute-start.6 = (bf16[2,64,1024]{2,1,0:T(8,128)(2,1)S(1)}, bf16[2,64,1024]{2,1,0:T(8,128)(2,1)S(1)}, u32[]{:S(2)}, u32[]{:S(2)}) collective-permute-start(bf16[2,64,1024]{2,1,0:T(8,128)(2,1)S(1)} %collective-permute-done.4.refs_0_), channel_id=1, source_target_pairs={{0,1},{1,0},{2,3},{3,2},{4,5},{5,4},{6,7},{7,6},{8,9},{9,8},{10,11... | collective-permute-start | bytes 786440 | tf_op jit(solution)/shard_map/ppermute | solution.py:23
  63.0 12.7 %collective-permute-start.7 = (bf16[2,64,1024]{2,1,0:T(8,128)(2,1)S(1)}, bf16[2,64,1024]{2,1,0:T(8,128)(2,1)S(1)}, u32[]{:S(2)}, u32[]{:S(2)}) collective-permute-start(bf16[2,64,1024]{2,1,0:T(8,128)(2,1)S(1)} %collective-permute-done.5.refs_1_), channel_id=1, source_target_pairs={{0,1},{1,0},{2,3},{3,2},{4,5},{5,4},{6,7},{7,6},{8,9},{9,8},{10,11... | collective-permute-start | bytes 786440 | tf_op jit(solution)/shard_map/ppermute | solution.py:23
  63.7 2.2 %copy-start.1 = (bf16[1,1024,2048]{2,1,0:T(8,128)(2,1)S(1)}, bf16[1,1024,2048]{2,1,0:T(8,128)(2,1)}, u32[]{:S(2)}) copy-start(bf16[1,1024,2048]{2,1,0:T(8,128)(2,1)} %param.8) | copy-start | bytes 12582916
  65.9 2.2 %copy-start.3 = (bf16[1,2048,1024]{2,1,0:T(8,128)(2,1)S(1)}, bf16[1,2048,1024]{2,1,0:T(8,128)(2,1)}, u32[]{:S(2)}) copy-start(bf16[1,2048,1024]{2,1,0:T(8,128)(2,1)} %param.9) | copy-start | bytes 12582916
  68.0 7.6 %copy-start.2 = (bf16[1,1024,2048]{2,1,0:T(8,128)(2,1)S(1)}, bf16[1,1024,2048]{2,1,0:T(8,128)(2,1)}, u32[]{:S(2)}) copy-start(bf16[1,1024,2048]{2,1,0:T(8,128)(2,1)} %param.8) | copy-start | bytes 12582916
  74.1 10.4 %collective-permute-start.10 = (bf16[2,64,1024]{2,1,0:T(8,128)(2,1)S(1)}, bf16[2,64,1024]{2,1,0:T(8,128)(2,1)S(1)}, u32[]{:S(2)}, u32[]{:S(2)}) collective-permute-start(bf16[2,64,1024]{2,1,0:T(8,128)(2,1)S(1)} %get-tuple-element.15), channel_id=1, source_target_pairs={{0,1},{1,0},{2,3},{3,2},{4,5},{5,4},{6,7},{7,6},{8,9},{9,8},{10,11... | collective-permute-start | bytes 786440 | tf_op jit(solution)/shard_map/ppermute | solution.py:23
  81.7 8.3 %collective-permute-start.8 = (bf16[2,64,1024]{2,1,0:T(8,128)(2,1)S(1)}, bf16[2,64,1024]{2,1,0:T(8,128)(2,1)S(1)}, u32[]{:S(2)}, u32[]{:S(2)}) collective-permute-start(bf16[2,64,1024]{2,1,0:T(8,128)(2,1)S(1)} %get-tuple-element.13), channel_id=1, source_target_pairs={{0,1},{1,0},{2,3},{3,2},{4,5},{5,4},{6,7},{7,6},{8,9},{9,8},{10,11... | collective-permute-start | bytes 786440 | tf_op jit(solution)/shard_map/ppermute | solution.py:23
  83.1 27.9 %collective-permute-start.3 = (bf16[2,64,1024]{2,1,0:T(8,128)(2,1)S(1)}, bf16[2,64,1024]{2,1,0:T(8,128)(2,1)S(1)}, u32[]{:S(2)}, u32[]{:S(2)}) collective-permute-start(bf16[2,64,1024]{2,1,0:T(8,128)(2,1)S(1)} %get-tuple-element.11), channel_id=1, source_target_pairs={{0,1},{1,0},{2,3},{3,2},{4,5},{5,4},{6,7},{7,6},{8,9},{9,8},{10,11... | collective-permute-start | bytes 786440 | tf_op jit(solution)/shard_map/ppermute | solution.py:23
  83.3 20.1 %collective-permute-start.12 = (bf16[2,64,1024]{2,1,0:T(8,128)(2,1)S(1)}, bf16[2,64,1024]{2,1,0:T(8,128)(2,1)S(1)}, u32[]{:S(2)}, u32[]{:S(2)}) collective-permute-start(bf16[2,64,1024]{2,1,0:T(8,128)(2,1)S(1)} %get-tuple-element.17), channel_id=1, source_target_pairs={{0,1},{1,0},{2,3},{3,2},{4,5},{5,4},{6,7},{7,6},{8,9},{9,8},{10,11... | collective-permute-start | bytes 786440 | tf_op jit(solution)/shard_map/ppermute | solution.py:23
  84.6 26.5 %collective-permute-start.11 = (bf16[2,64,1024]{2,1,0:T(8,128)(2,1)S(1)}, bf16[2,64,1024]{2,1,0:T(8,128)(2,1)S(1)}, u32[]{:S(2)}, u32[]{:S(2)}) collective-permute-start(bf16[2,64,1024]{2,1,0:T(8,128)(2,1)S(1)} %add_convert_fusion.2), channel_id=1, source_target_pairs={{13,0},{4,1},{1,4},{8,5},{5,8},{12,9},{9,12},{0,13},{15,2},{6,3},{... | collective-permute-start | bytes 786440 | tf_op jit(solution)/shard_map/ppermute | solution.py:145
  90.1 21.2 %collective-permute-start.9 = (bf16[2,64,1024]{2,1,0:T(8,128)(2,1)S(1)}, bf16[2,64,1024]{2,1,0:T(8,128)(2,1)S(1)}, u32[]{:S(2)}, u32[]{:S(2)}) collective-permute-start(bf16[2,64,1024]{2,1,0:T(8,128)(2,1)S(1)} %add_convert_fusion.3), channel_id=1, source_target_pairs={{4,0},{13,1},{8,4},{1,5},{12,8},{5,9},{0,12},{9,13},{6,2},{15,3},{... | collective-permute-start | bytes 786440 | tf_op jit(solution)/shard_map/ppermute | solution.py:144
  103.5 11.9 %collective-permute-start.13 = (bf16[2,64,1024]{2,1,0:T(8,128)(2,1)S(1)}, bf16[2,64,1024]{2,1,0:T(8,128)(2,1)S(1)}, u32[]{:S(2)}, u32[]{:S(2)}) collective-permute-start(bf16[2,64,1024]{2,1,0:T(8,128)(2,1)S(1)} %add_convert_fusion.1), channel_id=1, source_target_pairs={{9,0},{8,1},{13,4},{12,5},{1,8},{0,9},{5,12},{4,13},{11,2},{10,3},... | collective-permute-start | bytes 786440 | tf_op jit(solution)/shard_map/ppermute | solution.py:143
  116.7 29.9 %copy-start.10 = (bf16[2,196,1024]{2,0,1:T(2,128)(2,1)S(1)}, bf16[2,196,1024]{2,0,1:T(2,128)(2,1)}, u32[]{:S(2)}) copy-start(bf16[2,196,1024]{2,0,1:T(2,128)(2,1)} %param.6) | copy-start | bytes 2408452
  147.0 0.7 copy-start.8
  147.6 2.7 %copy-start.7 = (f32[2,196,128]{2,1,0:T(8,128)}, f32[2,196,128]{2,1,0:T(8,128)S(1)}, u32[]{:S(2)}) copy-start(f32[2,196,128]{2,1,0:T(8,128)S(1)} %fusion.14) | copy-start | bytes 602116
  150.3 24.7 %all-to-all-start.2 = ((bf16[256,4,128]{2,1,0:T(4,128)(2,1)}), bf16[256,4,128]{2,1,0:T(4,128)(2,1)}, u32[]{:S(2)}, u32[]{:S(2)}) async-start(bf16[256,4,128]{2,1,0:T(4,128)(2,1)} %bitcast.17), calls=%async_computation.2 | async-start | bytes 524288 | tf_op jit(solution)/shard_map/all_to_all | solution.py:175

commit v3 on v2

--- a/solution.py
+++ b/solution.py
@@ -21,6 +21,10 @@
 
 def swap(block):
     return lax.ppermute(block, "half", [(0, 1), (1, 0)])
+
+
+def after(value, *earlier):
+    return lax.optimization_barrier((value,) + earlier)[0]
 
 
 def expert_kernel(count, *refs):
@@ -81,7 +85,7 @@
             pltpu.VMEM((2, count * size, width), jnp.bfloat16),
             pltpu.VMEM((2, count * size, width), jnp.float32),
         ],
-        compiler_params=pltpu.CompilerParams(vmem_limit_bytes=40 * 2**20),
+        compiler_params=pltpu.CompilerParams(vmem_limit_bytes=24 * 2**20),
         cost_estimate=pl.CostEstimate(
             flops=8 * count * size * width * hidden,
             bytes_accessed=4 * width * hidden,
@@ -127,19 +131,27 @@
 
     far = lax.ppermute(both[1], RING, hops(FAR))
     wide = lax.ppermute(both[3], RING, hops(WIDE))
-    near = lax.ppermute(both[2], RING, hops(NEAR))
     own = both[0]
+    own_pair = swap(own)
+    first, second = (
+        pltpu.with_memory_space_constraint(weight[0], pltpu.HBM)
+        for weight in (in_weight, out_weight)
+    )
+    near = lax.ppermute(after(both[2], far, wide), RING, hops(NEAR))
     far_pair, wide_pair = swap(far), swap(wide)
-    own_pair, near_pair = swap(own), swap(near)
-    first, second = in_weight[0], out_weight[0]
+    near_pair = swap(near)
     mine_a, other_a = expert_pass([wide, far], [wide_pair, far_pair], first, second)
-    mine_b, other_b = expert_pass([own, near], [own_pair, near_pair], first, second)
+    back_a = [swap(sent) for sent in other_a]
+    mine_b, other_b = expert_pass(
+        [after(own, *mine_a), near], [own_pair, near_pair], first, second
+    )
+    back_b = [swap(after(sent, *back_a)) for sent in other_b]
 
     def added(partial, sent):
-        return (partial + swap(sent).astype(jnp.float32)).astype(jnp.bfloat16)
-
-    wide_sum, far_sum = (added(a, b) for a, b in zip(mine_a, other_a))
-    own_sum, near_sum = (added(a, b) for a, b in zip(mine_b, other_b))
+        return (partial + sent.astype(jnp.float32)).astype(jnp.bfloat16)
+
+    wide_sum, far_sum = (added(a, b) for a, b in zip(mine_a, back_a))
+    own_sum, near_sum = (added(a, b) for a, b in zip(mine_b, back_b))
     wide_sum = lax.ppermute(wide_sum, RING, hops(WIDE, True))
     far_sum = lax.ppermute(far_sum, RING, hops(FAR, True))
     near_sum = lax.ppermute(near_sum, RING, hops(NEAR, True))

time: 177 us -> 173 us (0.977)
  waiting for transfers between devices: 40 us -> 58.3 us
  starting transfers between devices: 43.6 us -> 26.8 us
  blocking collectives: 54.9 us -> 50.2 us
  local copies, waits for them, and re-layouts: 10 us -> 5.66 us
  Pallas kernels: 12.1 us -> 15.1 us
    ppermute x8, waiting for transfers between devices: 8.48 us -> 31.9 us  [swap(): return lax.ppermute(block, 'half', [(0, 1), (1, 0)])]
    ppermute x1, waiting for transfers between devices: 13.5 us -> 4.4 us  [local(): near = lax.ppermute(after(both[2], far, wide), RING, hops(NEAR))]
    ppermute x1, waiting for transfers between devices: 5.8 us -> 13.5 us  [local(): wide = lax.ppermute(both[3], RING, hops(WIDE))]
    ppermute x1, starting transfers between devices: 7.46 us -> 1.52 us  [local(): wide_sum = lax.ppermute(wide_sum, RING, hops(WIDE, True))]
    ppermute x1, starting transfers between devices: 5.53 us -> 0.08 us  [local(): far_sum = lax.ppermute(far_sum, RING, hops(FAR, True))]
    ppermute x1, starting transfers between devices: 5.41 us -> 0.09 us  [local(): near_sum = lax.ppermute(near_sum, RING, hops(NEAR, True))]
    ppermute x1, starting transfers between devices: 1.72 us -> 6.55 us  [local(): wide = lax.ppermute(both[3], RING, hops(WIDE))]
    all_to_all x1, blocking collectives: 29.6 us -> 24.9 us  [local(): sums = lax.all_to_all(sums, PLANE, split_axis=0, concat_axis=0, tiled=True)]
  transfers between devices with their start and end apart: 15 -> 15, of which waited for: 6 -> 10; matrix products, arithmetic and copies ran while one was open for 4% -> 4% of each run, Pallas kernels for 7% -> 9%
where the time goes in v3:
time: 173 us; the launch traced here: 172 us
  waiting for transfers between devices  58.3 us (34%)
  blocking collectives  50.2 us (29%)
  starting transfers between devices  26.8 us (15%)
  Pallas kernels  15.1 us (9%)
  matrix products  11.1 us (6%)
  local copies, waits for them, and re-layouts  5.66 us (3%)
  other arithmetic  4.06 us (2%)
    ppermute x8, waiting for transfers between devices, swap(): return lax.ppermute(block, 'half', [(0, 1), (1, 0)])  31.9 us
    all_to_all x1, blocking collectives, local(): both = lax.all_to_all(both, PLANE, split_axis=0, concat_axis=0, tiled=True)  25.3 us
    all_to_all x1, blocking collectives, local(): sums = lax.all_to_all(sums, PLANE, split_axis=0, concat_axis=0, tiled=True)  24.9 us
    pallas_call x2, Pallas kernels, expert_pass(): pl.pallas_call(lambda *refs: expert_kernel(count, *refs), grid=(hidden //...  15.1 us
    ppermute x1, waiting for transfers between devices, local(): wide = lax.ppermute(both[3], RING, hops(WIDE))  13.5 us
    all_to_all x1, waiting for transfers between devices, local(): parts = lax.all_to_all(parts, ALL, split_axis=0, concat_axis=0, tiled=True)  8.02 us
    all_to_all x1, starting transfers between devices, local(): parts = lax.all_to_all(parts, ALL, split_axis=0, concat_axis=0, tiled=True)  7 us
    ppermute x1, starting transfers between devices, local(): wide = lax.ppermute(both[3], RING, hops(WIDE))  6.55 us
  transfers between devices with their start and end apart: 15, of which 10 were waited for; matrix products, arithmetic and copies ran while one was open for 4% of the time, Pallas kernels for 9%

profile of v3, /device:TPU:1, one launch (start us, length us, event | category | flops | bytes accessed | tf_op | source)
XLA Modules:
  0.0 172.2 jit_solution(10327526907087577106)
XLA Ops:
  0.7 1.3 fusion.9
  3.1 0.4 fusion.4
  3.6 1.0 fusion.5
  4.8 1.1 copy.31
  5.9 25.3 %all_to_all.15 = bf16[32,4,2,2,1024]{4,3,2,1,0:T(2,128)(2,1)S(1)} all-to-all(bf16[32,4,2,2,1024]{4,3,2,1,0:T(2,128)(2,1)S(1)} %bitcast.47), channel_id=1, replica_groups=mesh['x'=4,'y'=4,'z'=4,'core'=2,'half'=2] {'x','y','core'}, dimensions={0} | all-to-all | bytes 2097152 | tf_op jit(solution)/shard_map/all_to_all | solution.py:129
  31.2 0.8 fusion.51
  32.6 6.6 %collective-permute-start = (bf16[2,64,1024]{2,1,0:T(8,128)(2,1)S(1)}, bf16[2,64,1024]{2,1,0:T(8,128)(2,1)S(1)}, u32[]{:S(2)}, u32[]{:S(2)}) collective-permute-start(bf16[2,64,1024]{2,1,0:T(8,128)(2,1)S(1)} %squeeze.25), channel_id=1, source_target_pairs={{0,9},{1,8},{4,13},{5,12},{8,1},{9,0},{12,5},{13,4},{2,11},{3,10},... | collective-permute-start | bytes 786440 | tf_op jit(solution)/shard_map/ppermute | solution.py:133
  39.1 1.2 collective-permute-start.1
  40.6 13.5 %collective-permute-done.refs_0_ = bf16[2,64,1024]{2,1,0:T(8,128)(2,1)S(1)} collective-permute-done((bf16[2,64,1024]{2,1,0:T(8,128)(2,1)S(1)}, bf16[2,64,1024]{2,1,0:T(8,128)(2,1)S(1)}, u32[]{:S(2)}, u32[]{:S(2)}) %collective-permute-start) | collective-permute-done | bytes 262176 | tf_op jit(solution)/shard_map/ppermute | solution.py:133
  54.2 5.8 %collective-permute-start.4 = (bf16[2,64,1024]{2,1,0:T(8,128)(2,1)S(1)}, bf16[2,64,1024]{2,1,0:T(8,128)(2,1)S(1)}, u32[]{:S(2)}, u32[]{:S(2)}) collective-permute-start(bf16[2,64,1024]{2,1,0:T(8,128)(2,1)S(1)} %squeeze.29), channel_id=1, source_target_pairs={{0,13},{1,4},{4,1},{5,8},{8,5},{9,12},{12,9},{13,0},{2,15},{3,6},{... | collective-permute-start | bytes 786440 | tf_op jit(solution)/shard_map/ppermute | solution.py:140
  59.9 1.5 collective-permute-start.3
  61.8 4.4 %collective-permute-done.4.refs_1_ = bf16[2,64,1024]{2,1,0:T(8,128)(2,1)S(1)} collective-permute-done((bf16[2,64,1024]{2,1,0:T(8,128)(2,1)S(1)}, bf16[2,64,1024]{2,1,0:T(8,128)(2,1)S(1)}, u32[]{:S(2)}, u32[]{:S(2)}) %collective-permute-start.4) | collective-permute-done | bytes 262176 | tf_op jit(solution)/shard_map/ppermute | solution.py:140
  66.2 0.8 collective-permute-done.2.refs_2_
  67.0 5.6 %collective-permute-done.3.refs_3_ = bf16[2,64,1024]{2,1,0:T(8,128)(2,1)S(1)} collective-permute-done((bf16[2,64,1024]{2,1,0:T(8,128)(2,1)S(1)}, bf16[2,64,1024]{2,1,0:T(8,128)(2,1)S(1)}, u32[]{:S(2)}, u32[]{:S(2)}) %collective-permute-start.3) | collective-permute-done | bytes 262176 | tf_op jit(solution)/shard_map/ppermute | solution.py:23
  72.6 7.5 %expert_rows.2 = (f32[2,64,1024]{2,1,0:T(8,128)S(1)}, f32[2,64,1024]{2,1,0:T(8,128)S(1)}, bf16[2,64,1024]{2,1,0:T(8,128)(2,1)S(1)}, bf16[2,64,1024]{2,1,0:T(8,128)(2,1)S(1)}) custom-call(bf16[2,64,1024]{2,1,0:T(8,128)(2,1)S(1)} %collective-permute-done.refs_0_, bf16[2,64,1024]{2,1,0:T(8,128)(2,1)S(1)} %collective-permute-done.1.refs_1_, ...), custom_call_target="tpu_custom_call" | custom-call | flops 4294967296 | bytes 8388608 | tf_op jit(solution)/shard_map/expert_rows/pallas_call | solution.py:73
  80.6 1.1 collective-permute-start.8
  81.7 2.1 %collective-permute-done.6.refs_3_ = bf16[2,64,1024]{2,1,0:T(8,128)(2,1)S(1)} collective-permute-done((bf16[2,64,1024]{2,1,0:T(8,128)(2,1)S(1)}, bf16[2,64,1024]{2,1,0:T(8,128)(2,1)S(1)}, u32[]{:S(2)}, u32[]{:S(2)}) %collective-permute-start.6) | collective-permute-done | bytes 262176 | tf_op jit(solution)/shard_map/ppermute | solution.py:23
  83.9 7.5 %expert_rows.3 = (f32[2,64,1024]{2,1,0:T(8,128)S(1)}, f32[2,64,1024]{2,1,0:T(8,128)S(1)}, bf16[2,64,1024]{2,1,0:T(8,128)(2,1)S(1)}, bf16[2,64,1024]{2,1,0:T(8,128)(2,1)S(1)}) custom-call(bf16[2,64,1024]{2,1,0:T(8,128)(2,1)S(1)} %squeeze.24.refs_0_, bf16[2,64,1024]{2,1,0:T(8,128)(2,1)S(1)} %collective-permute-done.4.refs_1_, ...), custom_call_target="tpu_custom_call" | custom-call | flops 4294967296 | bytes 8388608 | tf_op jit(solution)/shard_map/expert_rows/pallas_call | solution.py:73
  91.4 3.7 %collective-permute-done.8 = bf16[2,64,1024]{2,1,0:T(8,128)(2,1)S(1)} collective-permute-done((bf16[2,64,1024]{2,1,0:T(8,128)(2,1)S(1)}, bf16[2,64,1024]{2,1,0:T(8,128)(2,1)S(1)}, u32[]{:S(2)}, u32[]{:S(2)}) %collective-permute-start.8) | collective-permute-done | bytes 262176 | tf_op jit(solution)/shard_map/ppermute | solution.py:23
  95.5 1.5 collective-permute-start.13
  97.0 1.2 collective-permute-start.9
  98.3 8.4 %collective-permute-done.11 = bf16[2,64,1024]{2,1,0:T(8,128)(2,1)S(1)} collective-permute-done((bf16[2,64,1024]{2,1,0:T(8,128)(2,1)S(1)}, bf16[2,64,1024]{2,1,0:T(8,128)(2,1)S(1)}, u32[]{:S(2)}, u32[]{:S(2)}) %collective-permute-start.11) | collective-permute-done | bytes 262176 | tf_op jit(solution)/shard_map/ppermute | solution.py:23
  106.8 11.2 %collective-permute-done.9 = bf16[2,64,1024]{2,1,0:T(8,128)(2,1)S(1)} collective-permute-done((bf16[2,64,1024]{2,1,0:T(8,128)(2,1)S(1)}, bf16[2,64,1024]{2,1,0:T(8,128)(2,1)S(1)}, u32[]{:S(2)}, u32[]{:S(2)}) %collective-permute-start.9) | collective-permute-done | bytes 262176 | tf_op jit(solution)/shard_map/ppermute | solution.py:23
  119.0 1.2 copy_bitcast_fusion.1
  120.2 24.9 %all_to_all.16 = bf16[32,4,2,2,1024]{4,3,2,1,0:T(2,128)(2,1)S(1)} all-to-all(bf16[32,4,2,2,1024]{4,3,2,1,0:T(2,128)(2,1)S(1)} %copy_bitcast_fusion.1), channel_id=1, replica_groups=mesh['x'=4,'y'=4,'z'=4,'core'=2,'half'=2] {'x','y','core'}, dimensions={0} | all-to-all | bytes 2097152 | tf_op jit(solution)/shard_map/all_to_all | solution.py:160
  146.5 2.6 %convolution_convert_fusion.3 = bf16[1024,128]{1,0:T(8,128)(2,1)} fusion(f32[2,196,128]{2,1,0:T(8,128)S(1)} %fusion.14, f32[2,196,128]{2,1,0:T(8,128)S(1)} %convolution_bitcast_fusion.3, bf16[2,196,1024]{2,0,1:T(2,128)(2,1)S(1)} %copy-done, s32[]{:T(128)S(6)} %neg.3, s32[]{:T(128)S(6)} %sub.50, s32[128]{0:T(128)S(1)} %get-tuple-element.41, ...), kind=kOutput, calls=%fused_computation.12 | convolution fusion | flops 137666048 | bytes 1670956 | tf_op jit(solution)/shard_map/dot_general | solution.py:180
  149.1 7.0 %all-to-all-start.2 = ((bf16[256,4,128]{2,1,0:T(4,128)(2,1)}), bf16[256,4,128]{2,1,0:T(4,128)(2,1)}, u32[]{:S(2)}, u32[]{:S(2)}) async-start(bf16[256,4,128]{2,1,0:T(4,128)(2,1)} %bitcast.17), calls=%async_computation.2 | async-start | bytes 524288 | tf_op jit(solution)/shard_map/all_to_all | solution.py:187
  156.1 1.4 fusion.25
  157.5 3.1 %add_convert_fusion = bf16[2,196,1024]{2,1,0:T(8,128)(2,1)S(1)} fusion(f32[2,196,1024]{2,1,0:T(8,128)S(1)} %fusion.25, bf16[128,1024,1]{1,0,2:T(8,128)(2,1)} %copy-done.2, f32[2,196,128]{2,1,0:T(8,128)} %copy-done.4, f32[2,196,128]{2,1,0:T(8,128)} %copy-done.5, f32[2,196,128]{2,1,0:T(8,128)} %copy-done.3, f32[2,196]{1,0:T(2,128)S(1)} %get-tuple-element.34), kind=kOutput, calls=%fused_computation.4 | convolution fusion | flops 103915016 | bytes 3274272 | tf_op jit(solution)/shard_map/imn,dn->imd/dot_general | solution.py:176
  160.6 1.7 copy.30
  162.4 8.0 %all-to-all-done.2 = bf16[256,4,128]{2,1,0:T(4,128)(2,1)} async-done(((bf16[256,4,128]{2,1,0:T(4,128)(2,1)}), bf16[256,4,128]{2,1,0:T(4,128)(2,1)}, u32[]{:S(2)}, u32[]{:S(2)}) %all-to-all-start.2) | async-done | bytes 262176 | tf_op jit(solution)/shard_map/all_to_all | solution.py:187
  170.4 1.8 %convert_reduce_fusion = f32[4,128]{1,0:T(4,128)} fusion(bf16[256,4,128]{2,1,0:T(4,128)(2,1)} %all-to-all-done.2), kind=kLoop, calls=%fused_computation.39 | loop fusion | flops 261632 | bytes 264192 | tf_op jit(solution)/shard_map/reduce_sum | solution.py:188
  (56 shorter events, 5.8 us)
Async XLA Ops:
  0.6 1.4 copy-start
  2.0 1.1 copy-start.2
  2.4 2.3 %copy-start.1 = (f32[2,196,128]{2,1,0:T(8,128)}, f32[2,196,128]{2,1,0:T(8,128)S(1)}, u32[]{:S(2)}) copy-start(f32[2,196,128]{2,1,0:T(8,128)S(1)} %convolution_bitcast_fusion.1) | copy-start | bytes 602116
  2.4 1.2 copy-start.6
  3.1 143.4 %copy-start.3 = (f32[2,196,128]{2,1,0:T(8,128)}, f32[2,196,128]{2,1,0:T(8,128)S(1)}, u32[]{:S(2)}) copy-start(f32[2,196,128]{2,1,0:T(8,128)S(1)} %get-tuple-element.35) | copy-start | bytes 602116
  32.6 21.6 %collective-permute-start = (bf16[2,64,1024]{2,1,0:T(8,128)(2,1)S(1)}, bf16[2,64,1024]{2,1,0:T(8,128)(2,1)S(1)}, u32[]{:S(2)}, u32[]{:S(2)}) collective-permute-start(bf16[2,64,1024]{2,1,0:T(8,128)(2,1)S(1)} %squeeze.25), channel_id=1, source_target_pairs={{0,9},{1,8},{4,13},{5,12},{8,1},{9,0},{12,5},{13,4},{2,11},{3,10},... | collective-permute-start | bytes 786440 | tf_op jit(solution)/shard_map/ppermute | solution.py:133
  39.1 15.0 %collective-permute-start.1 = (bf16[2,64,1024]{2,1,0:T(8,128)(2,1)S(1)}, bf16[2,64,1024]{2,1,0:T(8,128)(2,1)S(1)}, u32[]{:S(2)}, u32[]{:S(2)}) collective-permute-start(bf16[2,64,1024]{2,1,0:T(8,128)(2,1)S(1)} %squeeze.26), channel_id=1, source_target_pairs={{0,4},{1,13},{4,8},{5,1},{8,12},{9,5},{12,0},{13,9},{2,6},{3,15},{... | collective-permute-start | bytes 786440 | tf_op jit(solution)/shard_map/ppermute | solution.py:132
  54.2 12.0 %collective-permute-start.4 = (bf16[2,64,1024]{2,1,0:T(8,128)(2,1)S(1)}, bf16[2,64,1024]{2,1,0:T(8,128)(2,1)S(1)}, u32[]{:S(2)}, u32[]{:S(2)}) collective-permute-start(bf16[2,64,1024]{2,1,0:T(8,128)(2,1)S(1)} %squeeze.29), channel_id=1, source_target_pairs={{0,13},{1,4},{4,1},{5,8},{8,5},{9,12},{12,9},{13,0},{2,15},{3,6},{... | collective-permute-start | bytes 786440 | tf_op jit(solution)/shard_map/ppermute | solution.py:140
  59.9 7.1 %collective-permute-start.2 = (bf16[2,64,1024]{2,1,0:T(8,128)(2,1)S(1)}, bf16[2,64,1024]{2,1,0:T(8,128)(2,1)S(1)}, u32[]{:S(2)}, u32[]{:S(2)}) collective-permute-start(bf16[2,64,1024]{2,1,0:T(8,128)(2,1)S(1)} %collective-permute-done.refs_0_), channel_id=1, source_target_pairs={{0,1},{1,0},{2,3},{3,2},{4,5},{5,4},{6,7},{7,6},{8,9},{9,8},{10,11... | collective-permute-start | bytes 786440 | tf_op jit(solution)/shard_map/ppermute | solution.py:23
  59.9 12.7 %collective-permute-start.3 = (bf16[2,64,1024]{2,1,0:T(8,128)(2,1)S(1)}, bf16[2,64,1024]{2,1,0:T(8,128)(2,1)S(1)}, u32[]{:S(2)}, u32[]{:S(2)}) collective-permute-start(bf16[2,64,1024]{2,1,0:T(8,128)(2,1)S(1)} %collective-permute-done.1.refs_1_), channel_id=1, source_target_pairs={{0,1},{1,0},{2,3},{3,2},{4,5},{5,4},{6,7},{7,6},{8,9},{9,8},{10,11... | collective-permute-start | bytes 786440 | tf_op jit(solution)/shard_map/ppermute | solution.py:23
  61.7 20.1 %collective-permute-start.5 = (bf16[2,64,1024]{2,1,0:T(8,128)(2,1)S(1)}, bf16[2,64,1024]{2,1,0:T(8,128)(2,1)S(1)}, u32[]{:S(2)}, u32[]{:S(2)}) collective-permute-start(bf16[2,64,1024]{2,1,0:T(8,128)(2,1)S(1)} %squeeze.24.refs_0_), channel_id=1, source_target_pairs={{0,1},{1,0},{2,3},{3,2},{4,5},{5,4},{6,7},{7,6},{8,9},{9,8},{10,11... | collective-permute-start | bytes 786440 | tf_op jit(solution)/shard_map/ppermute | solution.py:23
  66.2 17.7 %collective-permute-start.6 = (bf16[2,64,1024]{2,1,0:T(8,128)(2,1)S(1)}, bf16[2,64,1024]{2,1,0:T(8,128)(2,1)S(1)}, u32[]{:S(2)}, u32[]{:S(2)}) collective-permute-start(bf16[2,64,1024]{2,1,0:T(8,128)(2,1)S(1)} %collective-permute-done.4.refs_1_), channel_id=1, source_target_pairs={{0,1},{1,0},{2,3},{3,2},{4,5},{5,4},{6,7},{7,6},{8,9},{9,8},{10,11... | collective-permute-start | bytes 786440 | tf_op jit(solution)/shard_map/ppermute | solution.py:23
  80.2 11.2 %collective-permute-start.7 = (bf16[2,64,1024]{2,1,0:T(8,128)(2,1)S(1)}, bf16[2,64,1024]{2,1,0:T(8,128)(2,1)S(1)}, u32[]{:S(2)}, u32[]{:S(2)}) collective-permute-start(bf16[2,64,1024]{2,1,0:T(8,128)(2,1)S(1)} %get-tuple-element.20), channel_id=1, source_target_pairs={{0,1},{1,0},{2,3},{3,2},{4,5},{5,4},{6,7},{7,6},{8,9},{9,8},{10,11... | collective-permute-start | bytes 786440 | tf_op jit(solution)/shard_map/ppermute | solution.py:23
  80.6 14.5 %collective-permute-start.8 = (bf16[2,64,1024]{2,1,0:T(8,128)(2,1)S(1)}, bf16[2,64,1024]{2,1,0:T(8,128)(2,1)S(1)}, u32[]{:S(2)}, u32[]{:S(2)}) collective-permute-start(bf16[2,64,1024]{2,1,0:T(8,128)(2,1)S(1)} %get-tuple-element.21), channel_id=1, source_target_pairs={{0,1},{1,0},{2,3},{3,2},{4,5},{5,4},{6,7},{7,6},{8,9},{9,8},{10,11... | collective-permute-start | bytes 786440 | tf_op jit(solution)/shard_map/ppermute | solution.py:23
  95.1 11.6 %collective-permute-start.11 = (bf16[2,64,1024]{2,1,0:T(8,128)(2,1)S(1)}, bf16[2,64,1024]{2,1,0:T(8,128)(2,1)S(1)}, u32[]{:S(2)}, u32[]{:S(2)}) collective-permute-start(bf16[2,64,1024]{2,1,0:T(8,128)(2,1)S(1)} %get-tuple-element.25), channel_id=1, source_target_pairs={{0,1},{1,0},{2,3},{3,2},{4,5},{5,4},{6,7},{7,6},{8,9},{9,8},{10,11... | collective-permute-start | bytes 786440 | tf_op jit(solution)/shard_map/ppermute | solution.py:23
  95.5 22.8 %collective-permute-start.13 = (bf16[2,64,1024]{2,1,0:T(8,128)(2,1)S(1)}, bf16[2,64,1024]{2,1,0:T(8,128)(2,1)S(1)}, u32[]{:S(2)}, u32[]{:S(2)}) collective-permute-start(bf16[2,64,1024]{2,1,0:T(8,128)(2,1)S(1)} %add_convert_fusion.1), channel_id=1, source_target_pairs={{9,0},{8,1},{13,4},{12,5},{1,8},{0,9},{5,12},{4,13},{11,2},{10,3},... | collective-permute-start | bytes 786440 | tf_op jit(solution)/shard_map/ppermute | solution.py:155
  97.0 21.1 %collective-permute-start.9 = (bf16[2,64,1024]{2,1,0:T(8,128)(2,1)S(1)}, bf16[2,64,1024]{2,1,0:T(8,128)(2,1)S(1)}, u32[]{:S(2)}, u32[]{:S(2)}) collective-permute-start(bf16[2,64,1024]{2,1,0:T(8,128)(2,1)S(1)} %get-tuple-element.22), channel_id=1, source_target_pairs={{0,1},{1,0},{2,3},{3,2},{4,5},{5,4},{6,7},{7,6},{8,9},{9,8},{10,11... | collective-permute-start | bytes 786440 | tf_op jit(solution)/shard_map/ppermute | solution.py:23
  98.2 20.1 %collective-permute-start.10 = (bf16[2,64,1024]{2,1,0:T(8,128)(2,1)S(1)}, bf16[2,64,1024]{2,1,0:T(8,128)(2,1)S(1)}, u32[]{:S(2)}, u32[]{:S(2)}) collective-permute-start(bf16[2,64,1024]{2,1,0:T(8,128)(2,1)S(1)} %add_convert_fusion.3), channel_id=1, source_target_pairs={{4,0},{13,1},{8,4},{1,5},{12,8},{5,9},{0,12},{9,13},{6,2},{15,3},{... | collective-permute-start | bytes 786440 | tf_op jit(solution)/shard_map/ppermute | solution.py:156
  106.7 12.2 %collective-permute-start.12 = (bf16[2,64,1024]{2,1,0:T(8,128)(2,1)S(1)}, bf16[2,64,1024]{2,1,0:T(8,128)(2,1)S(1)}, u32[]{:S(2)}, u32[]{:S(2)}) collective-permute-start(bf16[2,64,1024]{2,1,0:T(8,128)(2,1)S(1)} %add_convert_fusion.2), channel_id=1, source_target_pairs={{13,0},{4,1},{1,4},{8,5},{5,8},{12,9},{9,12},{0,13},{15,2},{6,3},{... | collective-permute-start | bytes 786440 | tf_op jit(solution)/shard_map/ppermute | solution.py:157
  120.2 25.2 %copy-start.7 = (bf16[2,196,1024]{2,0,1:T(2,128)(2,1)S(1)}, bf16[2,196,1024]{2,0,1:T(2,128)(2,1)}, u32[]{:S(2)}) copy-start(bf16[2,196,1024]{2,0,1:T(2,128)(2,1)} %param.6) | copy-start | bytes 2408452
  145.8 0.7 copy-start.5
  146.4 2.7 %copy-start.4 = (f32[2,196,128]{2,1,0:T(8,128)}, f32[2,196,128]{2,1,0:T(8,128)S(1)}, u32[]{:S(2)}) copy-start(f32[2,196,128]{2,1,0:T(8,128)S(1)} %fusion.14) | copy-start | bytes 602116
  149.1 21.3 %all-to-all-start.2 = ((bf16[256,4,128]{2,1,0:T(4,128)(2,1)}), bf16[256,4,128]{2,1,0:T(4,128)(2,1)}, u32[]{:S(2)}, u32[]{:S(2)}) async-start(bf16[256,4,128]{2,1,0:T(4,128)(2,1)} %bitcast.17), calls=%async_computation.2 | async-start | bytes 524288 | tf_op jit(solution)/shard_map/all_to_all | solution.py:187

commit v4 on v3

v4 whole, which is shorter than its diff:
```python
import jax
import jax.numpy as jnp
from jax import lax
from jax.experimental import pallas as pl
from jax.experimental.pallas import tpu as pltpu
from jax.sharding import PartitionSpec as P

BOTH = ("expert", "hidden")
GELU_A = 0.7978845608028654
GELU_B = 0.7978845608028654 * 0.044715


def swap(block):
    return lax.ppermute(block, "hidden", [(0, 1), (1, 0)])


def after(value, *earlier):
    return lax.optimization_barrier((value,) + earlier)[0]


def expert_kernel(count, *refs):
    blocks = refs[:count]
    first, second = refs[count], refs[count + 1]
    outs = refs[count + 2 : 2 * count + 2]
    rows, acc = refs[2 * count + 2 :]
    size = blocks[0].shape[1]
    step = pl.program_id(0)

    @pl.when(step == 0)
    def _():
        for at, block in enumerate(blocks):
            rows[:, at * size : (at + 1) * size, :] = block[...]
        acc[...] = jnp.zeros_like(acc)

    contract_last = (((1,), (1,)), ((), ()))
    pre = jnp.dot(rows[0], first[...], preferred_element_type=jnp.float32)
    act_grad = lax.dot_general(
        rows[1], second[...], contract_last, preferred_element_type=jnp.float32
    )
    square = pre * pre
    bent = jnp.tanh(pre * (GELU_A + GELU_B * square))
    gate = 0.5 + 0.5 * bent
    activation = (pre * gate).astype(jnp.bfloat16)
    slope = gate + (0.5 * pre) * (1.0 - bent * bent) * (GELU_A + 3.0 * GELU_B * square)
    pre_grad = (act_grad * slope).astype(jnp.bfloat16)
    acc[0] += jnp.dot(activation, second[...], preferred_element_type=jnp.float32)
    acc[1] += lax.dot_general(
        pre_grad, first[...], contract_last, preferred_element_type=jnp.float32
    )

    @pl.when(step == pl.num_programs(0) - 1)
    def _():
        for at, out in enumerate(outs):
            out[...] = acc[:, at * size : (at + 1) * size, :].astype(out.dtype)


def expert_pass(blocks, dtype, first, second):
    count = len(blocks)
    _, size, width = blocks[0].shape
    hidden = first.shape[1]
    part = 512
    whole = pl.BlockSpec((2, size, width), lambda j: (0, 0, 0))
    return pl.pallas_call(
        lambda *refs: expert_kernel(count, *refs),
        grid=(hidden // part,),
        in_specs=[whole] * count
        + [
            pl.BlockSpec((width, part), lambda j: (0, j)),
            pl.BlockSpec((part, width), lambda j: (j, 0)),
        ],
        out_specs=[whole] * count,
        out_shape=[jax.ShapeDtypeStruct((2, size, width), dtype)] * count,
        scratch_shapes=[
            pltpu.VMEM((2, count * size, width), jnp.bfloat16),
            pltpu.VMEM((2, count * size, width), jnp.float32),
        ],
        compiler_params=pltpu.CompilerParams(vmem_limit_bytes=24 * 2**20),
        cost_estimate=pl.CostEstimate(
            flops=8 * count * size * width * hidden,
            bytes_accessed=4 * width * hidden,
            transcendentals=count * size * hidden,
        ),
        name="expert_rows",
    )(*blocks, first, second)


def local(tokens, grad_out, slot_weight, in_weight, out_weight):
    images = tokens.shape[0]
    logits = jnp.einsum("imd,dn->imn", tokens, slot_weight, preferred_element_type=jnp.float32)
    dispatch = jax.nn.softmax(logits, axis=1)
    combine = jax.nn.softmax(logits, axis=2)
    dispatch_b = dispatch.astype(jnp.bfloat16)
    combine_b = combine.astype(jnp.bfloat16)
    slot_inputs = jnp.einsum(
        "imn,imd->ind", dispatch_b, tokens, preferred_element_type=jnp.float32
    ).astype(jnp.bfloat16)
    slot_grads = jnp.einsum(
        "imn,imd->ind", combine_b, grad_out, preferred_element_type=jnp.float32
    ).astype(jnp.bfloat16)
    both = jnp.stack([slot_inputs, slot_grads], axis=0)
    both = jnp.transpose(both, (2, 0, 1, 3))
    experts, _, _, width = both.shape
    both = lax.all_to_all(both, "expert", split_axis=0, concat_axis=0, tiled=True)
    both = jnp.transpose(both.reshape(2, experts // 2, 2, images, width), (0, 2, 1, 3, 4))
    both = both.reshape(2, 2, -1, width)
    first, second = (
        pltpu.with_memory_space_constraint(weight[0], pltpu.HBM)
        for weight in (in_weight, out_weight)
    )
    pair_a = swap(both[0])
    mine = expert_pass([both[0], both[1]], jnp.float32, first, second)
    pair_b = swap(after(both[1], mine[0]))
    (sent_a,) = expert_pass([pair_a], jnp.bfloat16, first, second)
    back_a = swap(sent_a)
    (sent_b,) = expert_pass([pair_b], jnp.bfloat16, first, second)
    back_b = swap(sent_b)
    sums = [
        (partial + back.astype(jnp.float32)).astype(jnp.bfloat16)
        for partial, back in zip(mine, (back_a, back_b))
    ]
    sums = jnp.stack(sums, axis=0).reshape(2, 2, experts // 2, images, width)
    sums = jnp.transpose(sums, (0, 2, 1, 3, 4)).reshape(experts, 2, images, width)
    summed = lax.all_to_all(sums, "expert", split_axis=0, concat_axis=0, tiled=True)
    slot_outputs = jnp.transpose(summed[:, 0], (1, 0, 2))
    slot_in_grad = jnp.transpose(summed[:, 1], (1, 0, 2))
    combine_dw = jnp.einsum(
        "imd,ind->imn", grad_out, slot_outputs, preferred_element_type=jnp.float32
    )
    combine_dl = combine * (combine_dw - jnp.sum(combine * combine_dw, axis=2, keepdims=True))
    dispatch_dw = jnp.einsum(
        "imd,ind->imn", tokens, slot_in_grad, preferred_element_type=jnp.float32
    )
    dispatch_dl = dispatch * (dispatch_dw - jnp.sum(dispatch * dispatch_dw, axis=1, keepdims=True))
    logit_grad = (combine_dl + dispatch_dl).astype(jnp.bfloat16)
    input_grad = jnp.einsum(
        "imn,ind->imd", dispatch_b, slot_in_grad, preferred_element_type=jnp.float32
    )
    input_grad = input_grad + jnp.einsum(
        "imn,dn->imd", logit_grad, slot_weight, preferred_element_type=jnp.float32
    )
    phi_term = jnp.einsum("imd,imn->dn", tokens, logit_grad, preferred_element_type=jnp.float32)
    phi_parts = phi_term.astype(jnp.bfloat16).reshape(2 * experts, -1, experts)
    phi_parts = lax.all_to_all(phi_parts, BOTH, split_axis=0, concat_axis=0, tiled=True)
    phi_grad = jnp.sum(phi_parts.astype(jnp.float32), axis=0)
    return (input_grad.astype(jnp.bfloat16), phi_grad)


def solution(mesh):
    placed = (
        P(("expert", "hidden"), None, None),
        P(("expert", "hidden"), None, None),
        P(),
        P("expert", None, "hidden"),
        P("expert", "hidden", None),
    )
    return jax.shard_map(
        local,
        mesh=mesh,
        in_specs=placed,
        out_specs=(P(("expert", "hidden"), None, None), P(("expert", "hidden"), None)),
        check_vma=False,
    )
```

time: 173 us -> 174 us (level)
  blocking collectives: 50.2 us -> 86.6 us
  waiting for transfers between devices: 58.3 us -> 28.1 us
  starting transfers between devices: 26.8 us -> 11.7 us
  Pallas kernels: 15.1 us -> 21.5 us
  local copies, waits for them, and re-layouts: 5.66 us -> 7.48 us
    all_to_all x2, blocking collectives: 50.2 us -> 86.6 us  [the longest x1 47.9 us: local(): lax.all_to_all(both, 'expert', split_axis=0, concat_axis=0, tiled=True)]
    ppermute x14 -> x4, waiting for transfers between devices: 50.2 us -> 19.3 us  [swap(): return lax.ppermute(block, 'hidden', [(0, 1), (1, 0)])]
    ppermute x14 -> x4, starting transfers between devices: 19.8 us -> 4.72 us  [swap(): return lax.ppermute(block, 'hidden', [(0, 1), (1, 0)])]
    pallas_call x2 -> x3, Pallas kernels: 15.1 us -> 21.5 us  [expert_pass(): pl.pallas_call(lambda *refs: expert_kernel(count, *refs), grid=(hidden //...]
    transpose x0 -> x2, local copies, waits for them, and re-layouts: none -> 1.8 us  [the longest x1 1.08 us: local(): both = jnp.transpose(both, (2, 0, 1, 3))]
    dot_general x2 -> x1, matrix products: 3.86 us -> 3.09 us  [local(): jnp.einsum('imd,imn->dn', tokens, logit_grad, preferred_element_type=jnp....]
  transfers between devices with their start and end apart: 15 -> 5, of which waited for: 10 -> 5; matrix products, arithmetic and copies ran while one was open for 4% -> 4% of each run, Pallas kernels for 9% -> 12%
where the time goes in v4:
time: 174 us; the launch traced here: 173 us
  blocking collectives  86.6 us (50%)
  waiting for transfers between devices  28.1 us (16%)
  Pallas kernels  21.5 us (12%)
  starting transfers between devices  11.7 us (7%)
  matrix products  11.6 us (7%)
  local copies, waits for them, and re-layouts  7.48 us (4%)
  other arithmetic  5.45 us (3%)
    all_to_all x1, blocking collectives, local(): lax.all_to_all(both, 'expert', split_axis=0, concat_axis=0, tiled=True)  47.9 us
    all_to_all x1, blocking collectives, local(): lax.all_to_all(sums, 'expert', split_axis=0, concat_axis=0, tiled=True)  38.6 us
    pallas_call x3, Pallas kernels, expert_pass(): pl.pallas_call(lambda *refs: expert_kernel(count, *refs), grid=(hidden //...  21.5 us
    ppermute x4, waiting for transfers between devices, swap(): return lax.ppermute(block, 'hidden', [(0, 1), (1, 0)])  19.3 us
    all_to_all x1, waiting for transfers between devices, local(): lax.all_to_all(phi_parts, BOTH, split_axis=0, concat_axis=0, tiled=True)  8.81 us
    all_to_all x1, starting transfers between devices, local(): lax.all_to_all(phi_parts, BOTH, split_axis=0, concat_axis=0, tiled=True)  6.97 us
    ppermute x4, starting transfers between devices, swap(): return lax.ppermute(block, 'hidden', [(0, 1), (1, 0)])  4.72 us
  transfers between devices with their start and end apart: 5, of which 5 were waited for; matrix products, arithmetic and copies ran while one was open for 4% of the time, Pallas kernels for 12%

profile of v4, /device:TPU:1, one launch (start us, length us, event | category | flops | bytes accessed | tf_op | source)
XLA Modules:
  0.0 173.2 jit_solution(15410838505839093974)
XLA Ops:
  0.7 1.7 fusion.23
  2.4 0.8 fusion.41
  3.1 0.8 fusion.40
  4.4 1.0 fusion.5
  5.6 1.1 copy.29
  6.6 47.9 %all_to_all.15 = bf16[128,2,2,1024]{3,2,1,0:T(2,128)(2,1)S(1)} all-to-all(bf16[128,2,2,1024]{3,2,1,0:T(2,128)(2,1)S(1)} %copy.29), channel_id=1, replica_groups=mesh['expert'=128,'hidden'=2] {'expert'}, dimensions={0} | all-to-all | bytes 2097152 | tf_op jit(solution)/shard_map/all_to_all | solution.py:103
  54.6 0.7 copy.59
  55.3 0.7 fusion.39
  56.5 1.1 collective-permute-start
  57.6 7.5 %expert_rows.3 = (f32[2,128,1024]{2,1,0:T(8,128)S(1)}, f32[2,128,1024]{2,1,0:T(8,128)S(1)}) custom-call(bf16[2,128,1024]{2,1,0:T(8,128)(2,1)S(1)} %squeeze.20.refs_0_, bf16[2,128,1024]{2,1,0:T(8,128)(2,1)S(1)} %squeeze.21.refs_1_, bf16[1024,2048]{1,0:T(8,128)(2,1)} %bitcast.49, bf16[2048,1024]{1,0:T(8,128)(2,1)} %bitcast.52), custom_call_target="tpu_custom_call" | custom-call | flops 4294967296 | bytes 8388608 | tf_op jit(solution)/shard_map/expert_rows/pallas_call | solution.py:63
  65.1 0.5 collective-permute-start.2
  65.6 2.8 %collective-permute-done.refs_0_ = bf16[2,128,1024]{2,1,0:T(8,128)(2,1)S(1)} collective-permute-done((bf16[2,128,1024]{2,1,0:T(8,128)(2,1)S(1)}, bf16[2,128,1024]{2,1,0:T(8,128)(2,1)S(1)}, u32[]{:S(2)}, u32[]{:S(2)}) %collective-permute-start) | collective-permute-done | bytes 524320 | tf_op jit(solution)/shard_map/ppermute | solution.py:14
  68.5 7.0 %expert_rows.4 = bf16[2,128,1024]{2,1,0:T(8,128)(2,1)S(1)} custom-call(bf16[2,128,1024]{2,1,0:T(8,128)(2,1)S(1)} %collective-permute-done.refs_0_, bf16[1024,2048]{1,0:T(8,128)(2,1)} %bitcast.50, bf16[2048,1024]{1,0:T(8,128)(2,1)} %bitcast.53), custom_call_target="tpu_custom_call" | custom-call | flops 2147483648 | bytes 8388608 | tf_op jit(solution)/shard_map/expert_rows/pallas_call | solution.py:63
  75.4 1.6 collective-permute-start.1
  77.1 2.6 %collective-permute-done.2.refs_0_ = bf16[2,128,1024]{2,1,0:T(8,128)(2,1)S(1)} collective-permute-done((bf16[2,128,1024]{2,1,0:T(8,128)(2,1)S(1)}, bf16[2,128,1024]{2,1,0:T(8,128)(2,1)S(1)}, u32[]{:S(2)}, u32[]{:S(2)}) %collective-permute-start.2) | collective-permute-done | bytes 524320 | tf_op jit(solution)/shard_map/ppermute | solution.py:14
  79.7 7.0 %expert_rows.5 = bf16[2,128,1024]{2,1,0:T(8,128)(2,1)S(1)} custom-call(bf16[2,128,1024]{2,1,0:T(8,128)(2,1)S(1)} %collective-permute-done.2.refs_0_, bf16[1024,2048]{1,0:T(8,128)(2,1)} %bitcast.51, bf16[2048,1024]{1,0:T(8,128)(2,1)} %bitcast.54), custom_call_target="tpu_custom_call" | custom-call | flops 2147483648 | bytes 8388608 | tf_op jit(solution)/shard_map/expert_rows/pallas_call | solution.py:63
  86.7 1.4 collective-permute-start.3
  88.1 2.8 %collective-permute-done.1 = bf16[2,128,1024]{2,1,0:T(8,128)(2,1)S(1)} collective-permute-done((bf16[2,128,1024]{2,1,0:T(8,128)(2,1)S(1)}, bf16[2,128,1024]{2,1,0:T(8,128)(2,1)S(1)}, u32[]{:S(2)}, u32[]{:S(2)}) %collective-permute-start.1) | collective-permute-done | bytes 524320 | tf_op jit(solution)/shard_map/ppermute | solution.py:14
  91.3 11.0 %collective-permute-done.3 = bf16[2,128,1024]{2,1,0:T(8,128)(2,1)} collective-permute-done((bf16[2,128,1024]{2,1,0:T(8,128)(2,1)S(1)}, bf16[2,128,1024]{2,1,0:T(8,128)(2,1)}, u32[]{:S(2)}, u32[]{:S(2)}) %collective-permute-start.3) | collective-permute-done | bytes 524320 | tf_op jit(solution)/shard_map/ppermute | solution.py:14
  102.3 1.2 add_convert_fusion.1
  103.7 1.5 maximum_bitcast_fusion.1
  105.2 0.7 copy.31
  105.9 38.6 %all_to_all.16 = bf16[128,2,2,1024]{3,2,1,0:T(2,128)(2,1)S(1)} all-to-all(bf16[128,2,2,1024]{3,2,1,0:T(2,128)(2,1)S(1)} %bitcast.57), channel_id=1, replica_groups=mesh['expert'=128,'hidden'=2] {'expert'}, dimensions={0} | all-to-all | bytes 2097152 | tf_op jit(solution)/shard_map/all_to_all | solution.py:123
  144.5 0.7 fusion.38
  146.4 3.1 %fusion.9 = bf16[1024,128]{0,1:T(8,128)(2,1)S(1)} fusion(f32[2,196,128]{2,1,0:T(8,128)S(1)} %fusion.14, f32[2,196,128]{2,1,0:T(8,128)S(1)} %convolution_bitcast_fusion.2, bf16[2,196,1024]{2,0,1:T(2,128)(2,1)S(1)} %copy-done.6, f32[2,196,128]{2,1,0:T(8,128)} %get-tuple-element.19, f32[2,196]{1,0:T(2,128)S(1)} %get-tuple-element.18), kind=kOutput, calls=%fused_computation.13 | convolution fusion | flops 103243272 | bytes 1668640 | tf_op jit(solution)/shard_map/imd,imn->dn/dot_general | solution.py:141
  149.5 0.8 copy.37
  150.3 7.0 %all-to-all-start.2 = ((bf16[256,4,128]{2,1,0:T(4,128)(2,1)}), bf16[256,4,128]{2,1,0:T(4,128)(2,1)S(1)}, u32[]{:S(2)}, u32[]{:S(2)}) async-start(bf16[256,4,128]{2,1,0:T(4,128)(2,1)} %bitcast.19), calls=%async_computation.2 | async-start | bytes 524288 | tf_op jit(solution)/shard_map/all_to_all | solution.py:143
  157.3 1.5 fusion.25
  158.7 3.1 %add_convert_fusion = bf16[2,196,1024]{2,1,0:T(8,128)(2,1)S(1)} fusion(f32[2,196,1024]{2,1,0:T(8,128)S(1)} %fusion.25, f32[2,196,128]{2,1,0:T(8,128)} %copy-done.3, f32[2,196,128]{2,1,0:T(8,128)} %copy-done.4, bf16[1024,128]{1,0:T(8,128)(2,1)} %param.7, f32[2,196,128]{2,1,0:T(8,128)} %get-tuple-element.19, f32[2,196]{1,0:T(2,128)S(1)} %get-tuple-element.18), kind=kOutput, calls=%fused_computation.4 | convolution fusion | flops 103915016 | bytes 3274272 | tf_op jit(solution)/shard_map/imn,dn->imd/dot_general | solution.py:138
  161.9 1.7 copy.38
  163.6 8.8 %all-to-all-done.2 = bf16[256,4,128]{2,1,0:T(4,128)(2,1)S(1)} async-done(((bf16[256,4,128]{2,1,0:T(4,128)(2,1)}), bf16[256,4,128]{2,1,0:T(4,128)(2,1)S(1)}, u32[]{:S(2)}, u32[]{:S(2)}) %all-to-all-start.2) | async-done | bytes 262176 | tf_op jit(solution)/shard_map/all_to_all | solution.py:143
  172.4 0.9 convert_reduce_fusion
  (24 shorter events, 2.6 us)
Async XLA Ops:
  0.6 3.8 %copy-start = (bf16[2,196,1024]{2,0,1:T(2,128)(2,1)S(1)}, bf16[2,196,1024]{2,0,1:T(2,128)(2,1)}, u32[]{:S(2)}) copy-start(bf16[2,196,1024]{2,0,1:T(2,128)(2,1)} %param.6) | copy-start | bytes 2408452
  0.6 3.3 %copy-start.5 = (bf16[2,196,1024]{2,0,1:T(2,128)(2,1)S(1)}, bf16[2,196,1024]{2,0,1:T(2,128)(2,1)}, u32[]{:S(2)}) copy-start(bf16[2,196,1024]{2,0,1:T(2,128)(2,1)} %param.5) | copy-start | bytes 2408452
  2.4 3.1 %copy-start.1 = (f32[2,196,128]{2,1,0:T(8,128)}, f32[2,196,128]{2,1,0:T(8,128)S(1)}, u32[]{:S(2)}) copy-start(f32[2,196,128]{2,1,0:T(8,128)S(1)} %fusion.23) | copy-start | bytes 602116
  56.5 12.0 %collective-permute-start = (bf16[2,128,1024]{2,1,0:T(8,128)(2,1)S(1)}, bf16[2,128,1024]{2,1,0:T(8,128)(2,1)S(1)}, u32[]{:S(2)}, u32[]{:S(2)}) collective-permute-start(bf16[2,128,1024]{2,1,0:T(8,128)(2,1)S(1)} %squeeze.20.refs_0_), channel_id=1, source_target_pairs={{0,1},{1,0},{2,3},{3,2},{4,5},{5,4},{6,7},{7,6},{8,9},{9,8},{10,11... | collective-permute-start | bytes 1572872 | tf_op jit(solution)/shard_map/ppermute | solution.py:14
  65.1 14.6 %collective-permute-start.2 = (bf16[2,128,1024]{2,1,0:T(8,128)(2,1)S(1)}, bf16[2,128,1024]{2,1,0:T(8,128)(2,1)S(1)}, u32[]{:S(2)}, u32[]{:S(2)}) collective-permute-start(bf16[2,128,1024]{2,1,0:T(8,128)(2,1)S(1)} %squeeze.21.refs_1_), channel_id=1, source_target_pairs={{0,1},{1,0},{2,3},{3,2},{4,5},{5,4},{6,7},{7,6},{8,9},{9,8},{10,11... | collective-permute-start | bytes 1572872 | tf_op jit(solution)/shard_map/ppermute | solution.py:14
  75.4 15.5 %collective-permute-start.1 = (bf16[2,128,1024]{2,1,0:T(8,128)(2,1)S(1)}, bf16[2,128,1024]{2,1,0:T(8,128)(2,1)S(1)}, u32[]{:S(2)}, u32[]{:S(2)}) collective-permute-start(bf16[2,128,1024]{2,1,0:T(8,128)(2,1)S(1)} %expert_rows.4), channel_id=1, source_target_pairs={{0,1},{1,0},{2,3},{3,2},{4,5},{5,4},{6,7},{7,6},{8,9},{9,8},{10,11... | collective-permute-start | bytes 1572872 | tf_op jit(solution)/shard_map/ppermute | solution.py:14
  86.7 15.6 %collective-permute-start.3 = (bf16[2,128,1024]{2,1,0:T(8,128)(2,1)S(1)}, bf16[2,128,1024]{2,1,0:T(8,128)(2,1)}, u32[]{:S(2)}, u32[]{:S(2)}) collective-permute-start(bf16[2,128,1024]{2,1,0:T(8,128)(2,1)S(1)} %expert_rows.5), channel_id=1, source_target_pairs={{0,1},{1,0},{2,3},{3,2},{4,5},{5,4},{6,7},{7,6},{8,9},{9,8},{10,11... | collective-permute-start | bytes 1572872 | tf_op jit(solution)/shard_map/ppermute | solution.py:14
  144.5 1.2 copy-start.6
  145.2 1.0 copy-start.2
  145.7 11.6 %copy-start.4 = (f32[2,196,128]{2,1,0:T(8,128)}, f32[2,196,128]{2,1,0:T(8,128)S(1)}, u32[]{:S(2)}) copy-start(f32[2,196,128]{2,1,0:T(8,128)S(1)} %convolution_bitcast_fusion.2) | copy-start | bytes 602116
  146.4 3.9 %copy-start.3 = (f32[2,196,128]{2,1,0:T(8,128)}, f32[2,196,128]{2,1,0:T(8,128)S(1)}, u32[]{:S(2)}) copy-start(f32[2,196,128]{2,1,0:T(8,128)S(1)} %fusion.14) | copy-start | bytes 602116
  150.3 22.1 %all-to-all-start.2 = ((bf16[256,4,128]{2,1,0:T(4,128)(2,1)}), bf16[256,4,128]{2,1,0:T(4,128)(2,1)S(1)}, u32[]{:S(2)}, u32[]{:S(2)}) async-start(bf16[256,4,128]{2,1,0:T(4,128)(2,1)} %bitcast.19), calls=%async_computation.2 | async-start | bytes 524288 | tf_op jit(solution)/shard_map/all_to_all | solution.py:143

commit v5 on v4

--- a/solution.py
+++ b/solution.py
@@ -84,9 +84,66 @@
     )(*blocks, first, second)
 
 
+def sum_kernel(mine_a, back_a, mine_b, back_b, out):
+    out[0] = (mine_a[...] + back_a[...].astype(jnp.float32)).astype(jnp.bfloat16)
+    out[1] = (mine_b[...] + back_b[...].astype(jnp.float32)).astype(jnp.bfloat16)
+
+
+def sum_halves(*parts):
+    return pl.pallas_call(
+        sum_kernel,
+        out_shape=jax.ShapeDtypeStruct((2,) + parts[0].shape, jnp.bfloat16),
+        compiler_params=pltpu.CompilerParams(vmem_limit_bytes=16 * 2**20),
+        cost_estimate=pl.CostEstimate(
+            flops=2 * parts[0].size, bytes_accessed=16 * parts[0].size, transcendentals=0
+        ),
+        name="sum_halves",
+    )(*parts)
+
+
+def grad_kernel(tokens, turned, grads, combine, dispatch, outs, backs, logit_grad, phi):
+    contract_last = (((1,), (1,)), ((), ()))
+    total = None
+    for image in range(tokens.shape[0]):
+        comb, disp = combine[image], dispatch[image]
+        wide = lax.dot_general(
+            grads[image], outs[image], contract_last, preferred_element_type=jnp.float32
+        )
+        deep = lax.dot_general(
+            tokens[image], backs[image], contract_last, preferred_element_type=jnp.float32
+        )
+        wide = comb * (wide - jnp.sum(comb * wide, axis=1, keepdims=True))
+        deep = disp * (deep - jnp.sum(disp * deep, axis=0, keepdims=True))
+        grad = (wide + deep).astype(jnp.bfloat16)
+        logit_grad[image] = grad
+        term = jnp.dot(turned[image], grad, preferred_element_type=jnp.float32)
+        total = term if total is None else total + term
+    phi[...] = total.astype(jnp.bfloat16)
+
+
+def logit_grads(tokens, turned, grads, combine, dispatch, outs, backs):
+    images, rows, width = tokens.shape
+    slots = outs.shape[1]
+    return pl.pallas_call(
+        grad_kernel,
+        out_shape=[
+            jax.ShapeDtypeStruct((images, rows, slots), jnp.bfloat16),
+            jax.ShapeDtypeStruct((width, slots), jnp.bfloat16),
+        ],
+        compiler_params=pltpu.CompilerParams(vmem_limit_bytes=24 * 2**20),
+        cost_estimate=pl.CostEstimate(
+            flops=6 * images * rows * width * slots,
+            bytes_accessed=8 * images * rows * width,
+            transcendentals=0,
+        ),
+        name="logit_grads",
+    )(tokens, turned, grads, combine, dispatch, outs, backs)
+
+
 def local(tokens, grad_out, slot_weight, in_weight, out_weight):
     images = tokens.shape[0]
     logits = jnp.einsum("imd,dn->imn", tokens, slot_weight, preferred_element_type=jnp.float32)
+    logits = lax.optimization_barrier(logits)
     dispatch = jax.nn.softmax(logits, axis=1)
     combine = jax.nn.softmax(logits, axis=2)
     dispatch_b = dispatch.astype(jnp.bfloat16)
@@ -110,36 +167,28 @@
     pair_a = swap(both[0])
     mine = expert_pass([both[0], both[1]], jnp.float32, first, second)
     pair_b = swap(after(both[1], mine[0]))
+    flat_tokens, flat_grads, _ = lax.optimization_barrier((tokens, grad_out, mine[0]))
+    turned = jnp.transpose(flat_tokens, (0, 2, 1))
     (sent_a,) = expert_pass([pair_a], jnp.bfloat16, first, second)
     back_a = swap(sent_a)
     (sent_b,) = expert_pass([pair_b], jnp.bfloat16, first, second)
     back_b = swap(sent_b)
-    sums = [
-        (partial + back.astype(jnp.float32)).astype(jnp.bfloat16)
-        for partial, back in zip(mine, (back_a, back_b))
-    ]
-    sums = jnp.stack(sums, axis=0).reshape(2, 2, experts // 2, images, width)
+    sums = sum_halves(mine[0], back_a, mine[1], back_b)
+    sums = sums.reshape(2, 2, experts // 2, images, width)
     sums = jnp.transpose(sums, (0, 2, 1, 3, 4)).reshape(experts, 2, images, width)
     summed = lax.all_to_all(sums, "expert", split_axis=0, concat_axis=0, tiled=True)
     slot_outputs = jnp.transpose(summed[:, 0], (1, 0, 2))
     slot_in_grad = jnp.transpose(summed[:, 1], (1, 0, 2))
-    combine_dw = jnp.einsum(
-        "imd,ind->imn", grad_out, slot_outputs, preferred_element_type=jnp.float32
-    )
-    combine_dl = combine * (combine_dw - jnp.sum(combine * combine_dw, axis=2, keepdims=True))
-    dispatch_dw = jnp.einsum(
-        "imd,ind->imn", tokens, slot_in_grad, preferred_element_type=jnp.float32
-    )
-    dispatch_dl = dispatch * (dispatch_dw - jnp.sum(dispatch * dispatch_dw, axis=1, keepdims=True))
-    logit_grad = (combine_dl + dispatch_dl).astype(jnp.bfloat16)
+    logit_grad, phi_parts = logit_grads(
+        flat_tokens, turned, flat_grads, combine, dispatch, slot_outputs, slot_in_grad
+    )
     input_grad = jnp.einsum(
         "imn,ind->imd", dispatch_b, slot_in_grad, preferred_element_type=jnp.float32
     )
     input_grad = input_grad + jnp.einsum(
         "imn,dn->imd", logit_grad, slot_weight, preferred_element_type=jnp.float32
     )
-    phi_term = jnp.einsum("imd,imn->dn", tokens, logit_grad, preferred_element_type=jnp.float32)
-    phi_parts = phi_term.astype(jnp.bfloat16).reshape(2 * experts, -1, experts)
+    phi_parts = phi_parts.reshape(2 * experts, -1, experts)
     phi_parts = lax.all_to_all(phi_parts, BOTH, split_axis=0, concat_axis=0, tiled=True)
     phi_grad = jnp.sum(phi_parts.astype(jnp.float32), axis=0)
     return (input_grad.astype(jnp.bfloat16), phi_grad)

time: 174 us -> 173 us (level)
  blocking collectives: 86.6 us -> 48 us
  waiting for transfers between devices: 28.1 us -> 58.1 us
  local copies, waits for them, and re-layouts: 7.48 us -> 16.5 us
  starting transfers between devices: 11.7 us -> 20.4 us
  matrix products: 11.6 us -> 4.26 us
  other arithmetic: 5.45 us -> 1.71 us
    all_to_all x1 -> x0, blocking collectives: 38.6 us -> none  [local(): lax.all_to_all(sums, 'expert', split_axis=0, concat_axis=0, tiled=True)]
    all_to_all x0 -> x1, waiting for transfers between devices: none -> 27.3 us  [local(): lax.all_to_all(sums, 'expert', split_axis=0, concat_axis=0, tiled=True)]
    all_to_all x0 -> x1, starting transfers between devices: none -> 8.65 us  [local(): lax.all_to_all(sums, 'expert', split_axis=0, concat_axis=0, tiled=True)]
    dot_general x3 -> x0, matrix products: 3.89 us -> none  [the longest x1 3.09 us: local(): jnp.einsum('imd,imn->dn', tokens, logit_grad, preferred_element_type=jnp....]
    dot_general x1, matrix products: 3.11 us -> 0.41 us  [local(): jnp.einsum('imn,dn->imd', logit_grad, slot_weight, preferred_element_type...]
    all_to_all x1, waiting for transfers between devices: 8.81 us -> 11.5 us  [local(): lax.all_to_all(phi_parts, BOTH, split_axis=0, concat_axis=0, tiled=True)]
    optimization_barrier x0 -> x3, local copies, waits for them, and re-layouts: none -> 2.56 us  [local(): lax.optimization_barrier((tokens, grad_out, mine[0]))]
    transpose x1, local copies, waits for them, and re-layouts: 0.72 us -> 2.92 us  [local(): jnp.transpose(sums, (0, 2, 1, 3, 4)).reshape(experts, 2, images, width)]
  transfers between devices with their start and end apart: 5 -> 6, of which waited for: 5 -> 6; matrix products, arithmetic and copies ran while one was open for 4% -> 4% of each run, Pallas kernels for 12% -> 13%
where the time goes in v5:
time: 173 us
  waiting for transfers between devices  58.1 us (34%)
  blocking collectives  48 us (28%)
  Pallas kernels  22.9 us (13%)
  starting transfers between devices  20.4 us (12%)
  local copies, waits for them, and re-layouts  16.5 us (10%)
  matrix products  4.26 us (2%)
    all_to_all x1, blocking collectives, local(): lax.all_to_all(both, 'expert', split_axis=0, concat_axis=0, tiled=True)  48 us
    all_to_all x1, waiting for transfers between devices, local(): lax.all_to_all(sums, 'expert', split_axis=0, concat_axis=0, tiled=True)  27.3 us
    pallas_call x3, Pallas kernels, expert_pass(): pl.pallas_call(lambda *refs: expert_kernel(count, *refs), grid=(hidden //...  21.6 us
    ppermute x4, waiting for transfers between devices, swap(): return lax.ppermute(block, 'hidden', [(0, 1), (1, 0)])  19.3 us
    all_to_all x1, waiting for transfers between devices, local(): lax.all_to_all(phi_parts, BOTH, split_axis=0, concat_axis=0, tiled=True)  11.5 us
    all_to_all x1, starting transfers between devices, local(): lax.all_to_all(sums, 'expert', split_axis=0, concat_axis=0, tiled=True)  8.65 us
    all_to_all x1, starting transfers between devices, local(): lax.all_to_all(phi_parts, BOTH, split_axis=0, concat_axis=0, tiled=True)  7.01 us
    ppermute x4, starting transfers between devices, swap(): return lax.ppermute(block, 'hidden', [(0, 1), (1, 0)])  4.73 us
  transfers between devices with their start and end apart: 6, of which 6 were waited for; matrix products, arithmetic and copies ran while one was open for 4% of the time, Pallas kernels for 13%

profile of v5, /device:TPU:1, one launch (start us, length us, event | category | flops | bytes accessed | tf_op | source)
XLA Modules:
  0.0 172.7 jit_solution(3332360123692691264)
XLA Ops:
  0.7 0.9 copy-done
  1.6 1.5 fusion.10
  4.9 1.1 copy.19
  6.0 48.0 %all_to_all.15 = bf16[128,2,2,1024]{3,2,1,0:T(2,128)(2,1)S(1)} all-to-all(bf16[128,2,2,1024]{3,2,1,0:T(2,128)(2,1)S(1)} %copy.19), channel_id=1, replica_groups=mesh['expert'=128,'hidden'=2] {'expert'}, dimensions={0} | all-to-all | bytes 2097152 | tf_op jit(solution)/shard_map/all_to_all | solution.py:160
  54.0 0.7 copy.40
  54.7 0.7 fusion.19
  55.4 1.0 squeeze.21.refs_1_
  56.6 1.1 collective-permute-start
  57.7 7.7 %expert_rows.3 = (f32[2,128,1024]{2,1,0:T(8,128)S(1)}, f32[2,128,1024]{2,1,0:T(8,128)S(1)}) custom-call(bf16[2,128,1024]{2,1,0:T(8,128)(2,1)S(1)} %squeeze.20.refs_0_, bf16[2,128,1024]{2,1,0:T(8,128)(2,1)} %squeeze.21.refs_1_, bf16[1024,2048]{1,0:T(8,128)(2,1)} %bitcast.37, bf16[2048,1024]{1,0:T(8,128)(2,1)} %bitcast.40), custom_call_target="tpu_custom_call" | custom-call | flops 4294967296 | bytes 8388608 | tf_op jit(solution)/shard_map/expert_rows/pallas_call | solution.py:63
  65.4 0.5 collective-permute-start.2
  66.0 2.7 %collective-permute-done.refs_0_ = bf16[2,128,1024]{2,1,0:T(8,128)(2,1)S(1)} collective-permute-done((bf16[2,128,1024]{2,1,0:T(8,128)(2,1)S(1)}, bf16[2,128,1024]{2,1,0:T(8,128)(2,1)S(1)}, u32[]{:S(2)}, u32[]{:S(2)}) %collective-permute-start) | collective-permute-done | bytes 524320 | tf_op jit(solution)/shard_map/ppermute | solution.py:14
  68.6 7.0 %expert_rows.4 = bf16[2,128,1024]{2,1,0:T(8,128)(2,1)S(1)} custom-call(bf16[2,128,1024]{2,1,0:T(8,128)(2,1)S(1)} %collective-permute-done.refs_0_, bf16[1024,2048]{1,0:T(8,128)(2,1)} %bitcast.38, bf16[2048,1024]{1,0:T(8,128)(2,1)} %bitcast.41), custom_call_target="tpu_custom_call" | custom-call | flops 2147483648 | bytes 8388608 | tf_op jit(solution)/shard_map/expert_rows/pallas_call | solution.py:63
  75.6 1.5 collective-permute-start.1
  77.1 2.8 %collective-permute-done.2.refs_0_ = bf16[2,128,1024]{2,1,0:T(8,128)(2,1)S(1)} collective-permute-done((bf16[2,128,1024]{2,1,0:T(8,128)(2,1)}, bf16[2,128,1024]{2,1,0:T(8,128)(2,1)S(1)}, u32[]{:S(2)}, u32[]{:S(2)}) %collective-permute-start.2) | collective-permute-done | bytes 524320 | tf_op jit(solution)/shard_map/ppermute | solution.py:14
  79.9 7.0 %expert_rows.5 = bf16[2,128,1024]{2,1,0:T(8,128)(2,1)S(1)} custom-call(bf16[2,128,1024]{2,1,0:T(8,128)(2,1)S(1)} %collective-permute-done.2.refs_0_, bf16[1024,2048]{1,0:T(8,128)(2,1)} %bitcast.39, bf16[2048,1024]{1,0:T(8,128)(2,1)} %bitcast.42), custom_call_target="tpu_custom_call" | custom-call | flops 2147483648 | bytes 8388608 | tf_op jit(solution)/shard_map/expert_rows/pallas_call | solution.py:63
  86.8 1.6 collective-permute-start.3
  88.5 2.6 %collective-permute-done.1.back_a = bf16[2,128,1024]{2,1,0:T(8,128)(2,1)S(1)} collective-permute-done((bf16[2,128,1024]{2,1,0:T(8,128)(2,1)S(1)}, bf16[2,128,1024]{2,1,0:T(8,128)(2,1)S(1)}, u32[]{:S(2)}, u32[]{:S(2)}) %collective-permute-start.1) | collective-permute-done | bytes 524320 | tf_op jit(solution)/shard_map/ppermute | solution.py:14
  91.1 11.2 %collective-permute-done.3.back_b = bf16[2,128,1024]{2,1,0:T(8,128)(2,1)S(1)} collective-permute-done((bf16[2,128,1024]{2,1,0:T(8,128)(2,1)S(1)}, bf16[2,128,1024]{2,1,0:T(8,128)(2,1)S(1)}, u32[]{:S(2)}, u32[]{:S(2)}) %collective-permute-start.3) | collective-permute-done | bytes 524320 | tf_op jit(solution)/shard_map/ppermute | solution.py:14
  102.5 1.2 reshape.26
  103.8 2.9 %copy.21 = bf16[2,64,2,2,1024]{4,3,2,1,0:T(2,128)(2,1)} copy(bf16[2,64,2,2,1024]{4,3,1,2,0:T(2,128)(2,1)} %bitcast.45) | data formatting | bytes 2097152 | tf_op jit(solution)/shard_map/transpose | solution.py:178
  106.7 8.6 %all-to-all-start.1 = ((bf16[128,2,2,1024]{3,2,1,0:T(2,128)(2,1)}), bf16[128,2,2,1024]{3,2,1,0:T(2,128)(2,1)}, u32[]{:S(2)}, u32[]{:S(2)}) async-start(bf16[128,2,2,1024]{3,2,1,0:T(2,128)(2,1)} %bitcast.9), calls=%async_computation.1 | async-start | bytes 2097152 | tf_op jit(solution)/shard_map/all_to_all | solution.py:179
  115.6 1.0 copy.23
  116.6 1.3 copy.26.grads
  117.9 27.3 %all-to-all-done.1 = bf16[128,2,2,1024]{3,2,1,0:T(2,128)(2,1)} async-done(((bf16[128,2,2,1024]{3,2,1,0:T(2,128)(2,1)}), bf16[128,2,2,1024]{3,2,1,0:T(2,128)(2,1)}, u32[]{:S(2)}, u32[]{:S(2)}) %all-to-all-start.1) | async-done | bytes 1048608 | tf_op jit(solution)/shard_map/all_to_all | solution.py:179
  145.2 1.9 %fusion.18 = (bf16[128,1,2,1024]{3,2,1,0:T(2,128)(2,1)S(1)}, bf16[128,1,2,1024]{3,2,1,0:T(2,128)(2,1)S(1)}) fusion(bf16[128,2,2,1024]{3,2,1,0:T(2,128)(2,1)} %all-to-all-done.1), kind=kLoop, calls=%fused_computation.28 | loop fusion | bytes 2097152 | tf_op jit(solution)/shard_map/slice | solution.py:180
  148.0 1.1 logit_grads.1
  149.1 0.7 copy-done.1
  149.7 7.0 %all-to-all-start.2 = ((bf16[256,4,128]{2,1,0:T(4,128)(2,1)}), bf16[256,4,128]{2,1,0:T(4,128)(2,1)S(1)}, u32[]{:S(2)}, u32[]{:S(2)}) async-start(bf16[256,4,128]{2,1,0:T(4,128)(2,1)} %bitcast.36), calls=%async_computation.2 | async-start | bytes 524288 | tf_op jit(solution)/shard_map/all_to_all | solution.py:192
  156.8 1.4 fusion.15
  158.6 1.7 copy.27
  160.3 11.5 %all-to-all-done.2 = bf16[256,4,128]{2,1,0:T(4,128)(2,1)S(1)} async-done(((bf16[256,4,128]{2,1,0:T(4,128)(2,1)}), bf16[256,4,128]{2,1,0:T(4,128)(2,1)S(1)}, u32[]{:S(2)}, u32[]{:S(2)}) %all-to-all-start.2) | async-done | bytes 262176 | tf_op jit(solution)/shard_map/all_to_all | solution.py:192
  171.8 0.9 convert_reduce_fusion
  (20 shorter events, 3.5 us)
Async XLA Ops:
  0.6 1.0 copy-start
  0.6 3.1 %copy-start.2 = (bf16[2,196,1024]{2,0,1:T(2,128)(2,1)S(1)}, bf16[2,196,1024]{2,0,1:T(2,128)(2,1)}, u32[]{:S(2)}) copy-start(bf16[2,196,1024]{2,0,1:T(2,128)(2,1)} %param.5) | copy-start | bytes 2408452
  3.1 1.3 copy-start.4
  56.6 12.0 %collective-permute-start = (bf16[2,128,1024]{2,1,0:T(8,128)(2,1)S(1)}, bf16[2,128,1024]{2,1,0:T(8,128)(2,1)S(1)}, u32[]{:S(2)}, u32[]{:S(2)}) collective-permute-start(bf16[2,128,1024]{2,1,0:T(8,128)(2,1)S(1)} %squeeze.20.refs_0_), channel_id=1, source_target_pairs={{0,1},{1,0},{2,3},{3,2},{4,5},{5,4},{6,7},{7,6},{8,9},{9,8},{10,11... | collective-permute-start | bytes 1572872 | tf_op jit(solution)/shard_map/ppermute | solution.py:14
  65.4 14.4 %collective-permute-start.2 = (bf16[2,128,1024]{2,1,0:T(8,128)(2,1)}, bf16[2,128,1024]{2,1,0:T(8,128)(2,1)S(1)}, u32[]{:S(2)}, u32[]{:S(2)}) collective-permute-start(bf16[2,128,1024]{2,1,0:T(8,128)(2,1)} %squeeze.21.refs_1_), channel_id=1, source_target_pairs={{0,1},{1,0},{2,3},{3,2},{4,5},{5,4},{6,7},{7,6},{8,9},{9,8},{10,11... | collective-permute-start | bytes 1572872 | tf_op jit(solution)/shard_map/ppermute | solution.py:14
  75.6 15.5 %collective-permute-start.1 = (bf16[2,128,1024]{2,1,0:T(8,128)(2,1)S(1)}, bf16[2,128,1024]{2,1,0:T(8,128)(2,1)S(1)}, u32[]{:S(2)}, u32[]{:S(2)}) collective-permute-start(bf16[2,128,1024]{2,1,0:T(8,128)(2,1)S(1)} %expert_rows.4), channel_id=1, source_target_pairs={{0,1},{1,0},{2,3},{3,2},{4,5},{5,4},{6,7},{7,6},{8,9},{9,8},{10,11... | collective-permute-start | bytes 1572872 | tf_op jit(solution)/shard_map/ppermute | solution.py:14
  86.8 15.5 %collective-permute-start.3 = (bf16[2,128,1024]{2,1,0:T(8,128)(2,1)S(1)}, bf16[2,128,1024]{2,1,0:T(8,128)(2,1)S(1)}, u32[]{:S(2)}, u32[]{:S(2)}) collective-permute-start(bf16[2,128,1024]{2,1,0:T(8,128)(2,1)S(1)} %expert_rows.5), channel_id=1, source_target_pairs={{0,1},{1,0},{2,3},{3,2},{4,5},{5,4},{6,7},{7,6},{8,9},{9,8},{10,11... | collective-permute-start | bytes 1572872 | tf_op jit(solution)/shard_map/ppermute | solution.py:14
  106.7 38.5 %all-to-all-start.1 = ((bf16[128,2,2,1024]{3,2,1,0:T(2,128)(2,1)}), bf16[128,2,2,1024]{3,2,1,0:T(2,128)(2,1)}, u32[]{:S(2)}, u32[]{:S(2)}) async-start(bf16[128,2,2,1024]{3,2,1,0:T(2,128)(2,1)} %bitcast.9), calls=%async_computation.1 | async-start | bytes 2097152 | tf_op jit(solution)/shard_map/all_to_all | solution.py:179
  147.2 0.8 copy-start.3
  149.0 0.7 copy-start.1
  149.7 22.1 %all-to-all-start.2 = ((bf16[256,4,128]{2,1,0:T(4,128)(2,1)}), bf16[256,4,128]{2,1,0:T(4,128)(2,1)S(1)}, u32[]{:S(2)}, u32[]{:S(2)}) async-start(bf16[256,4,128]{2,1,0:T(4,128)(2,1)} %bitcast.36), calls=%async_computation.2 | async-start | bytes 524288 | tf_op jit(solution)/shard_map/all_to_all | solution.py:192

commit v6 on v5

--- a/solution.py
+++ b/solution.py
@@ -99,6 +99,30 @@
         ),
         name="sum_halves",
     )(*parts)
+
+
+def lay_out_kernel(tokens, grads, flat_tokens, turned, flat_grads):
+    flat_tokens[...] = tokens[...]
+    flat_grads[...] = grads[...]
+    for image in range(tokens.shape[0]):
+        turned[image] = tokens[image].T
+
+
+def lay_out(tokens, grads):
+    images, rows, width = tokens.shape
+    return pl.pallas_call(
+        lay_out_kernel,
+        out_shape=[
+            jax.ShapeDtypeStruct(tokens.shape, tokens.dtype),
+            jax.ShapeDtypeStruct((images, width, rows), tokens.dtype),
+            jax.ShapeDtypeStruct(grads.shape, grads.dtype),
+        ],
+        compiler_params=pltpu.CompilerParams(vmem_limit_bytes=16 * 2**20),
+        cost_estimate=pl.CostEstimate(
+            flops=0, bytes_accessed=10 * tokens.size, transcendentals=0
+        ),
+        name="lay_out",
+    )(tokens, grads)
 
 
 def grad_kernel(tokens, turned, grads, combine, dispatch, outs, backs, logit_grad, phi):
@@ -158,22 +182,26 @@
     both = jnp.transpose(both, (2, 0, 1, 3))
     experts, _, _, width = both.shape
     both = lax.all_to_all(both, "expert", split_axis=0, concat_axis=0, tiled=True)
-    both = jnp.transpose(both.reshape(2, experts // 2, 2, images, width), (0, 2, 1, 3, 4))
-    both = both.reshape(2, 2, -1, width)
+    both = both.reshape(2, experts // 2, 2, images, width)
+    piece_a = jnp.transpose(both[0], (1, 0, 2, 3)).reshape(2, -1, width)
+    piece_b = jnp.transpose(after(both, piece_a)[1], (1, 0, 2, 3)).reshape(2, -1, width)
     first, second = (
         pltpu.with_memory_space_constraint(weight[0], pltpu.HBM)
         for weight in (in_weight, out_weight)
     )
-    pair_a = swap(both[0])
-    mine = expert_pass([both[0], both[1]], jnp.float32, first, second)
-    pair_b = swap(after(both[1], mine[0]))
-    flat_tokens, flat_grads, _ = lax.optimization_barrier((tokens, grad_out, mine[0]))
-    turned = jnp.transpose(flat_tokens, (0, 2, 1))
+    pair_a = swap(piece_a)
+    mine = expert_pass([piece_a, piece_b], jnp.float32, first, second)
+    pair_b = swap(after(piece_b, mine[0]))
+    early_tokens, early_grads, _ = lax.optimization_barrier((tokens, grad_out, mine[0]))
+    flat_tokens, turned, flat_grads = lay_out(early_tokens, early_grads)
     (sent_a,) = expert_pass([pair_a], jnp.bfloat16, first, second)
     back_a = swap(sent_a)
     (sent_b,) = expert_pass([pair_b], jnp.bfloat16, first, second)
     back_b = swap(sent_b)
     sums = sum_halves(mine[0], back_a, mine[1], back_b)
+    sums, flat_tokens, turned, flat_grads = lax.optimization_barrier(
+        (sums, flat_tokens, turned, flat_grads)
+    )
     sums = sums.reshape(2, 2, experts // 2, images, width)
     sums = jnp.transpose(sums, (0, 2, 1, 3, 4)).reshape(experts, 2, images, width)
     summed = lax.all_to_all(sums, "expert", split_axis=0, concat_axis=0, tiled=True)

time: 173 us -> 169 us (0.977)
  blocking collectives: 48 us -> 86.5 us
  waiting for transfers between devices: 58.1 us -> 29 us
  starting transfers between devices: 20.4 us -> 11.6 us
  local copies, waits for them, and re-layouts: 16.5 us -> 12 us
    all_to_all x0 -> x1, blocking collectives: none -> 38.5 us  [local(): lax.all_to_all(sums, 'expert', split_axis=0, concat_axis=0, tiled=True)]
    all_to_all x1 -> x0, waiting for transfers between devices: 27.3 us -> none  [local(): lax.all_to_all(sums, 'expert', split_axis=0, concat_axis=0, tiled=True)]
    all_to_all x1 -> x0, starting transfers between devices: 8.65 us -> none  [local(): lax.all_to_all(sums, 'expert', split_axis=0, concat_axis=0, tiled=True)]
    ppermute x4, waiting for transfers between devices: 19.3 us -> 16.4 us  [swap(): return lax.ppermute(block, 'hidden', [(0, 1), (1, 0)])]
    optimization_barrier x3 -> x2, local copies, waits for them, and re-layouts: 2.56 us -> 0.4 us  [local(): lax.optimization_barrier((tokens, grad_out, mine[0]))]
    unnamed x11 -> x19, local copies, waits for them, and re-layouts: 3.85 us -> 4.89 us
  transfers between devices with their start and end apart: 6 -> 5, of which waited for: 6 -> 4; matrix products, arithmetic and copies ran while one was open for 4% -> 2% of each run, Pallas kernels for 13% -> 13%
where the time goes in v6:
time: 169 us
  blocking collectives  86.5 us (51%)
  waiting for transfers between devices  29 us (17%)
  Pallas kernels  23.8 us (14%)
  local copies, waits for them, and re-layouts  12 us (7%)
  starting transfers between devices  11.6 us (7%)
  matrix products  3.21 us (2%)
  other arithmetic  1.71 us (1%)
    all_to_all x1, blocking collectives, local(): lax.all_to_all(both, 'expert', split_axis=0, concat_axis=0, tiled=True)  48 us
    all_to_all x1, blocking collectives, local(): lax.all_to_all(sums, 'expert', split_axis=0, concat_axis=0, tiled=True)  38.5 us
    pallas_call x3, Pallas kernels, expert_pass(): pl.pallas_call(lambda *refs: expert_kernel(count, *refs), grid=(hidden //...  21.5 us
    ppermute x4, waiting for transfers between devices, swap(): return lax.ppermute(block, 'hidden', [(0, 1), (1, 0)])  16.4 us
    all_to_all x1, waiting for transfers between devices, local(): lax.all_to_all(phi_parts, BOTH, split_axis=0, concat_axis=0, tiled=True)  12.6 us
    all_to_all x1, starting transfers between devices, local(): lax.all_to_all(phi_parts, BOTH, split_axis=0, concat_axis=0, tiled=True)  6.95 us
    unnamed x19, local copies, waits for them, and re-layouts  4.89 us
    ppermute x4, starting transfers between devices, swap(): return lax.ppermute(block, 'hidden', [(0, 1), (1, 0)])  4.64 us
  transfers between devices with their start and end apart: 5, of which 4 were waited for; matrix products, arithmetic and copies ran while one was open for 2% of the time, Pallas kernels for 13%

profile of v6, /device:TPU:1, one launch (start us, length us, event | category | flops | bytes accessed | tf_op | source)
XLA Modules:
  0.0 168.7 jit_solution(2328254853342494631)
XLA Ops:
  0.7 0.9 copy-done
  1.6 1.5 fusion.10
  3.3 0.4 fusion.20
  3.8 0.4 fusion.2
  4.4 0.4 fusion.3
  4.9 1.1 copy.19
  6.0 48.0 %all_to_all.15 = bf16[128,2,2,1024]{3,2,1,0:T(2,128)(2,1)S(1)} all-to-all(bf16[128,2,2,1024]{3,2,1,0:T(2,128)(2,1)S(1)} %copy.19), channel_id=1, replica_groups=mesh['expert'=128,'hidden'=2] {'expert'}, dimensions={0} | all-to-all | bytes 2097152 | tf_op jit(solution)/shard_map/all_to_all | solution.py:184
  54.0 0.4 slice_bitcast_fusion.1
  54.9 1.1 collective-permute-start
  56.6 7.5 %expert_rows.3 = (f32[2,128,1024]{2,1,0:T(8,128)S(1)}, f32[2,128,1024]{2,1,0:T(8,128)S(1)}) custom-call(bf16[2,128,1024]{2,1,0:T(8,128)(2,1)S(1)} %reshape.28.refs_0_, bf16[2,128,1024]{2,1,0:T(8,128)(2,1)S(1)} %reshape.30.refs_1_, bf16[1024,2048]{1,0:T(8,128)(2,1)} %bitcast.37, bf16[2048,1024]{1,0:T(8,128)(2,1)} %bitcast.40), custom_call_target="tpu_custom_call" | custom-call | flops 4294967296 | bytes 8388608 | tf_op jit(solution)/shard_map/expert_rows/pallas_call | solution.py:63
  64.2 0.5 collective-permute-start.2
  64.7 2.3 %collective-permute-done.refs_0_ = bf16[2,128,1024]{2,1,0:T(8,128)(2,1)S(1)} collective-permute-done((bf16[2,128,1024]{2,1,0:T(8,128)(2,1)S(1)}, bf16[2,128,1024]{2,1,0:T(8,128)(2,1)S(1)}, u32[]{:S(2)}, u32[]{:S(2)}) %collective-permute-start) | collective-permute-done | bytes 524320 | tf_op jit(solution)/shard_map/ppermute | solution.py:14
  66.9 7.0 %expert_rows.4 = bf16[2,128,1024]{2,1,0:T(8,128)(2,1)S(1)} custom-call(bf16[2,128,1024]{2,1,0:T(8,128)(2,1)S(1)} %collective-permute-done.refs_0_, bf16[1024,2048]{1,0:T(8,128)(2,1)} %bitcast.38, bf16[2048,1024]{1,0:T(8,128)(2,1)} %bitcast.41), custom_call_target="tpu_custom_call" | custom-call | flops 2147483648 | bytes 8388608 | tf_op jit(solution)/shard_map/expert_rows/pallas_call | solution.py:63
  73.9 1.5 collective-permute-start.1
  75.4 2.9 %collective-permute-done.2.refs_0_ = bf16[2,128,1024]{2,1,0:T(8,128)(2,1)S(1)} collective-permute-done((bf16[2,128,1024]{2,1,0:T(8,128)(2,1)S(1)}, bf16[2,128,1024]{2,1,0:T(8,128)(2,1)S(1)}, u32[]{:S(2)}, u32[]{:S(2)}) %collective-permute-start.2) | collective-permute-done | bytes 524320 | tf_op jit(solution)/shard_map/ppermute | solution.py:14
  78.2 7.0 %expert_rows.5 = bf16[2,128,1024]{2,1,0:T(8,128)(2,1)S(1)} custom-call(bf16[2,128,1024]{2,1,0:T(8,128)(2,1)S(1)} %collective-permute-done.2.refs_0_, bf16[1024,2048]{1,0:T(8,128)(2,1)} %bitcast.39, bf16[2048,1024]{1,0:T(8,128)(2,1)} %bitcast.42), custom_call_target="tpu_custom_call" | custom-call | flops 2147483648 | bytes 8388608 | tf_op jit(solution)/shard_map/expert_rows/pallas_call | solution.py:63
  85.2 1.6 collective-permute-start.3
  87.2 0.4 lay_out.1
  87.6 0.9 copy-done.1
  88.6 0.9 copy-done.3
  89.5 11.2 %collective-permute-done.3.back_b = bf16[2,128,1024]{2,1,0:T(8,128)(2,1)S(1)} collective-permute-done((bf16[2,128,1024]{2,1,0:T(8,128)(2,1)S(1)}, bf16[2,128,1024]{2,1,0:T(8,128)(2,1)S(1)}, u32[]{:S(2)}, u32[]{:S(2)}) %collective-permute-start.3) | collective-permute-done | bytes 524320 | tf_op jit(solution)/shard_map/ppermute | solution.py:14
  100.9 1.2 reshape.31
  102.1 1.9 %copy.24 = bf16[2,64,2,2,1024]{4,3,2,1,0:T(2,128)(2,1)S(1)} copy(bf16[2,64,2,2,1024]{4,3,1,2,0:T(2,128)(2,1)} %bitcast.44) | data formatting | bytes 2097152 | tf_op jit(solution)/shard_map/transpose | solution.py:206
  104.1 38.5 %all_to_all.16 = bf16[128,2,2,1024]{3,2,1,0:T(2,128)(2,1)S(1)} all-to-all(bf16[128,2,2,1024]{3,2,1,0:T(2,128)(2,1)S(1)} %bitcast.45), channel_id=1, replica_groups=mesh['expert'=128,'hidden'=2] {'expert'}, dimensions={0} | all-to-all | bytes 2097152 | tf_op jit(solution)/shard_map/all_to_all | solution.py:207
  142.6 0.7 fusion.18
  144.0 1.8 %logit_grads.1 = (bf16[2,196,128]{2,1,0:T(8,128)(2,1)S(1)}, bf16[1024,128]{1,0:T(8,128)(2,1)}) custom-call(bf16[2,196,1024]{2,1,0:T(8,128)(2,1)S(1)} %copy-done.2, bf16[2,1024,196]{2,1,0:T(8,128)(2,1)S(1)} %get-tuple-element.28.turned, bf16[2,196,1024]{2,1,0:T(8,128)(2,1)S(1)} %copy-done.4, f32[2,196,128]{2,1,0:T(8,128)S(1)} %broadcast_divide_fusion.combine, ...), custom_call_target="tpu_custom_call" | custom-call | flops 308281344 | bytes 3211264 | tf_op jit(solution)/shard_map/logit_grads/pallas_call | solution.py:151
  145.8 7.0 %all-to-all-start.2 = ((bf16[256,4,128]{2,1,0:T(4,128)(2,1)}), bf16[256,4,128]{2,1,0:T(4,128)(2,1)S(1)}, u32[]{:S(2)}, u32[]{:S(2)}) async-start(bf16[256,4,128]{2,1,0:T(4,128)(2,1)} %bitcast.17), calls=%async_computation.2 | async-start | bytes 524288 | tf_op jit(solution)/shard_map/all_to_all | solution.py:220
  152.8 0.4 fusion.15
  153.1 0.4 add_convert_fusion
  153.6 1.7 %copy.27 = bf16[2,196,1024]{2,0,1:T(2,128)(2,1)} copy(bf16[2,196,1024]{2,1,0:T(8,128)(2,1)S(1)} %add_convert_fusion) | data formatting | bytes 1605632
  155.3 12.6 %all-to-all-done.2 = bf16[256,4,128]{2,1,0:T(4,128)(2,1)S(1)} async-done(((bf16[256,4,128]{2,1,0:T(4,128)(2,1)}), bf16[256,4,128]{2,1,0:T(4,128)(2,1)S(1)}, u32[]{:S(2)}, u32[]{:S(2)}) %all-to-all-start.2) | async-done | bytes 262176 | tf_op jit(solution)/shard_map/all_to_all | solution.py:220
  167.9 0.9 convert_reduce_fusion
  (28 shorter events, 2.8 us)
Async XLA Ops:
  0.6 1.0 copy-start
  0.6 3.1 %copy-start.5 = (bf16[2,196,1024]{2,0,1:T(2,128)(2,1)S(1)}, bf16[2,196,1024]{2,0,1:T(2,128)(2,1)}, u32[]{:S(2)}) copy-start(bf16[2,196,1024]{2,0,1:T(2,128)(2,1)} %param.5) | copy-start | bytes 2408452
  3.1 1.3 copy-start.7
  54.9 12.0 %collective-permute-start = (bf16[2,128,1024]{2,1,0:T(8,128)(2,1)S(1)}, bf16[2,128,1024]{2,1,0:T(8,128)(2,1)S(1)}, u32[]{:S(2)}, u32[]{:S(2)}) collective-permute-start(bf16[2,128,1024]{2,1,0:T(8,128)(2,1)S(1)} %reshape.28.refs_0_), channel_id=1, source_target_pairs={{0,1},{1,0},{2,3},{3,2},{4,5},{5,4},{6,7},{7,6},{8,9},{9,8},{10,11... | collective-permute-start | bytes 1572872 | tf_op jit(solution)/shard_map/ppermute | solution.py:14
  64.2 14.1 %collective-permute-start.2 = (bf16[2,128,1024]{2,1,0:T(8,128)(2,1)S(1)}, bf16[2,128,1024]{2,1,0:T(8,128)(2,1)S(1)}, u32[]{:S(2)}, u32[]{:S(2)}) collective-permute-start(bf16[2,128,1024]{2,1,0:T(8,128)(2,1)S(1)} %reshape.30.refs_1_), channel_id=1, source_target_pairs={{0,1},{1,0},{2,3},{3,2},{4,5},{5,4},{6,7},{7,6},{8,9},{9,8},{10,11... | collective-permute-start | bytes 1572872 | tf_op jit(solution)/shard_map/ppermute | solution.py:14
  73.9 12.9 %copy-start.6 = (bf16[2,196,1024]{2,0,1:T(2,128)(2,1)S(1)}, bf16[2,196,1024]{2,0,1:T(2,128)(2,1)}, u32[]{:S(2)}) copy-start(bf16[2,196,1024]{2,0,1:T(2,128)(2,1)} %param.5) | copy-start | bytes 2408452
  73.9 15.6 %collective-permute-start.1 = (bf16[2,128,1024]{2,1,0:T(8,128)(2,1)S(1)}, bf16[2,128,1024]{2,1,0:T(8,128)(2,1)S(1)}, u32[]{:S(2)}, u32[]{:S(2)}) collective-permute-start(bf16[2,128,1024]{2,1,0:T(8,128)(2,1)S(1)} %expert_rows.4), channel_id=1, source_target_pairs={{0,1},{1,0},{2,3},{3,2},{4,5},{5,4},{6,7},{7,6},{8,9},{9,8},{10,11... | collective-permute-start | bytes 1572872 | tf_op jit(solution)/shard_map/ppermute | solution.py:14
  85.2 1.8 %copy-start.8 = (bf16[2,196,1024]{2,0,1:T(2,128)(2,1)S(1)}, bf16[2,196,1024]{2,0,1:T(2,128)(2,1)}, u32[]{:S(2)}) copy-start(bf16[2,196,1024]{2,0,1:T(2,128)(2,1)} %param.6) | copy-start | bytes 2408452
  85.2 15.5 %collective-permute-start.3 = (bf16[2,128,1024]{2,1,0:T(8,128)(2,1)S(1)}, bf16[2,128,1024]{2,1,0:T(8,128)(2,1)S(1)}, u32[]{:S(2)}, u32[]{:S(2)}) collective-permute-start(bf16[2,128,1024]{2,1,0:T(8,128)(2,1)S(1)} %expert_rows.5), channel_id=1, source_target_pairs={{0,1},{1,0},{2,3},{3,2},{4,5},{5,4},{6,7},{7,6},{8,9},{9,8},{10,11... | collective-permute-start | bytes 1572872 | tf_op jit(solution)/shard_map/ppermute | solution.py:14
  87.6 0.9 copy-start.1
  88.6 0.9 copy-start.3
  142.6 1.1 copy-start.2
  142.6 1.4 copy-start.4
  145.8 22.1 %all-to-all-start.2 = ((bf16[256,4,128]{2,1,0:T(4,128)(2,1)}), bf16[256,4,128]{2,1,0:T(4,128)(2,1)S(1)}, u32[]{:S(2)}, u32[]{:S(2)}) async-start(bf16[256,4,128]{2,1,0:T(4,128)(2,1)} %bitcast.17), calls=%async_computation.2 | async-start | bytes 524288 | tf_op jit(solution)/shard_map/all_to_all | solution.py:220

commit v7 on v6

--- a/solution.py
+++ b/solution.py
@@ -84,21 +84,20 @@
     )(*blocks, first, second)
 
 
-def sum_kernel(mine_a, back_a, mine_b, back_b, out):
-    out[0] = (mine_a[...] + back_a[...].astype(jnp.float32)).astype(jnp.bfloat16)
-    out[1] = (mine_b[...] + back_b[...].astype(jnp.float32)).astype(jnp.bfloat16)
-
-
-def sum_halves(*parts):
+def sum_kernel(mine, back, out):
+    out[...] = (mine[...] + back[...].astype(jnp.float32)).astype(jnp.bfloat16)
+
+
+def sum_halves(mine, back):
     return pl.pallas_call(
         sum_kernel,
-        out_shape=jax.ShapeDtypeStruct((2,) + parts[0].shape, jnp.bfloat16),
-        compiler_params=pltpu.CompilerParams(vmem_limit_bytes=16 * 2**20),
-        cost_estimate=pl.CostEstimate(
-            flops=2 * parts[0].size, bytes_accessed=16 * parts[0].size, transcendentals=0
+        out_shape=jax.ShapeDtypeStruct(back.shape, back.dtype),
+        compiler_params=pltpu.CompilerParams(vmem_limit_bytes=8 * 2**20),
+        cost_estimate=pl.CostEstimate(
+            flops=mine.size, bytes_accessed=8 * mine.size, transcendentals=0
         ),
         name="sum_halves",
-    )(*parts)
+    )(mine, back)
 
 
 def lay_out_kernel(tokens, grads, flat_tokens, turned, flat_grads):
@@ -198,12 +197,16 @@
     back_a = swap(sent_a)
     (sent_b,) = expert_pass([pair_b], jnp.bfloat16, first, second)
     back_b = swap(sent_b)
-    sums = sum_halves(mine[0], back_a, mine[1], back_b)
-    sums, flat_tokens, turned, flat_grads = lax.optimization_barrier(
-        (sums, flat_tokens, turned, flat_grads)
-    )
-    sums = sums.reshape(2, 2, experts // 2, images, width)
-    sums = jnp.transpose(sums, (0, 2, 1, 3, 4)).reshape(experts, 2, images, width)
+    def packed(mine_part, back_part):
+        half = sum_halves(mine_part, back_part)
+        half = half.reshape(2, experts // 2, images, width)
+        return jnp.transpose(half, (1, 0, 2, 3))
+
+    sums = jnp.pad(packed(mine[0], back_a), ((0, experts // 2), (0, 0), (0, 0), (0, 0)))
+    sums, flat_tokens, turned, flat_grads, back_b = lax.optimization_barrier(
+        (sums, flat_tokens, turned, flat_grads, back_b)
+    )
+    sums = lax.dynamic_update_slice(sums, packed(mine[1], back_b), (experts // 2, 0, 0, 0))
     summed = lax.all_to_all(sums, "expert", split_axis=0, concat_axis=0, tiled=True)
     slot_outputs = jnp.transpose(summed[:, 0], (1, 0, 2))
     slot_in_grad = jnp.transpose(summed[:, 1], (1, 0, 2))

time: 169 us -> 167 us (0.988)
  local copies, waits for them, and re-layouts: 12 us -> 9.62 us
    unnamed x19 -> x11, local copies, waits for them, and re-layouts: 4.89 us -> 2.67 us
    transpose x1 -> x0, local copies, waits for them, and re-layouts: 1.94 us -> none  [local(): jnp.transpose(sums, (0, 2, 1, 3, 4)).reshape(experts, 2, images, width)]
  transfers between devices with their start and end apart: 5 -> 5, of which waited for: 4 -> 5; matrix products, arithmetic and copies ran while one was open for 2% -> 3% of each run, Pallas kernels for 13% -> 13%
where the time goes in v7:
time: 167 us
  blocking collectives  86.5 us (52%)
  waiting for transfers between devices  29.5 us (18%)
  Pallas kernels  23.9 us (14%)
  starting transfers between devices  11.6 us (7%)
  local copies, waits for them, and re-layouts  9.62 us (6%)
  matrix products  3.21 us (2%)
  other arithmetic  1.71 us (1%)
    all_to_all x1, blocking collectives, local(): lax.all_to_all(both, 'expert', split_axis=0, concat_axis=0, tiled=True)  48 us
    all_to_all x1, blocking collectives, local(): lax.all_to_all(sums, 'expert', split_axis=0, concat_axis=0, tiled=True)  38.5 us
    pallas_call x3, Pallas kernels, expert_pass(): pl.pallas_call(lambda *refs: expert_kernel(count, *refs), grid=(hidden //...  21.5 us
    ppermute x4, waiting for transfers between devices, swap(): return lax.ppermute(block, 'hidden', [(0, 1), (1, 0)])  16.9 us
    all_to_all x1, waiting for transfers between devices, local(): lax.all_to_all(phi_parts, BOTH, split_axis=0, concat_axis=0, tiled=True)  12.6 us
    all_to_all x1, starting transfers between devices, local(): lax.all_to_all(phi_parts, BOTH, split_axis=0, concat_axis=0, tiled=True)  6.93 us
    ppermute x4, starting transfers between devices, swap(): return lax.ppermute(block, 'hidden', [(0, 1), (1, 0)])  4.64 us
  transfers between devices with their start and end apart: 5, of which 5 were waited for; matrix products, arithmetic and copies ran while one was open for 3% of the time, Pallas kernels for 13%

profile of v7, /device:TPU:1, one launch (start us, length us, event | category | flops | bytes accessed | tf_op | source)
XLA Modules:
  0.0 166.9 jit_solution(17725017613867295191)
XLA Ops:
  0.7 0.9 copy-done
  1.6 1.5 fusion.10
  3.3 0.4 fusion.20
  3.8 0.4 fusion.2
  4.4 0.4 fusion.3
  4.9 1.1 copy.30
  6.0 48.0 %all_to_all.15 = bf16[128,2,2,1024]{3,2,1,0:T(2,128)(2,1)S(1)} all-to-all(bf16[128,2,2,1024]{3,2,1,0:T(2,128)(2,1)S(1)} %copy.30), channel_id=1, replica_groups=mesh['expert'=128,'hidden'=2] {'expert'}, dimensions={0} | all-to-all | bytes 2097152 | tf_op jit(solution)/shard_map/all_to_all | solution.py:183
  54.9 1.1 collective-permute-start
  56.6 7.5 %expert_rows.3 = (f32[2,128,1024]{2,1,0:T(8,128)S(1)}, f32[2,128,1024]{2,1,0:T(8,128)S(1)}) custom-call(bf16[2,128,1024]{2,1,0:T(8,128)(2,1)S(1)} %reshape.28.refs_0_, bf16[2,128,1024]{2,1,0:T(8,128)(2,1)S(1)} %reshape.30.refs_1_, bf16[1024,2048]{1,0:T(8,128)(2,1)} %bitcast.39, bf16[2048,1024]{1,0:T(8,128)(2,1)} %bitcast.42), custom_call_target="tpu_custom_call" | custom-call | flops 4294967296 | bytes 8388608 | tf_op jit(solution)/shard_map/expert_rows/pallas_call | solution.py:63
  64.2 0.5 collective-permute-start.2
  64.7 2.3 %collective-permute-done.refs_0_ = bf16[2,128,1024]{2,1,0:T(8,128)(2,1)S(1)} collective-permute-done((bf16[2,128,1024]{2,1,0:T(8,128)(2,1)S(1)}, bf16[2,128,1024]{2,1,0:T(8,128)(2,1)S(1)}, u32[]{:S(2)}, u32[]{:S(2)}) %collective-permute-start) | collective-permute-done | bytes 524320 | tf_op jit(solution)/shard_map/ppermute | solution.py:14
  66.9 7.0 %expert_rows.4 = bf16[2,128,1024]{2,1,0:T(8,128)(2,1)S(1)} custom-call(bf16[2,128,1024]{2,1,0:T(8,128)(2,1)S(1)} %collective-permute-done.refs_0_, bf16[1024,2048]{1,0:T(8,128)(2,1)} %bitcast.40, bf16[2048,1024]{1,0:T(8,128)(2,1)} %bitcast.43), custom_call_target="tpu_custom_call" | custom-call | flops 2147483648 | bytes 8388608 | tf_op jit(solution)/shard_map/expert_rows/pallas_call | solution.py:63
  73.9 1.5 collective-permute-start.1
  75.4 2.9 %collective-permute-done.2.refs_0_ = bf16[2,128,1024]{2,1,0:T(8,128)(2,1)S(1)} collective-permute-done((bf16[2,128,1024]{2,1,0:T(8,128)(2,1)S(1)}, bf16[2,128,1024]{2,1,0:T(8,128)(2,1)S(1)}, u32[]{:S(2)}, u32[]{:S(2)}) %collective-permute-start.2) | collective-permute-done | bytes 524320 | tf_op jit(solution)/shard_map/ppermute | solution.py:14
  78.2 7.0 %expert_rows.5 = bf16[2,128,1024]{2,1,0:T(8,128)(2,1)S(1)} custom-call(bf16[2,128,1024]{2,1,0:T(8,128)(2,1)S(1)} %collective-permute-done.2.refs_0_, bf16[1024,2048]{1,0:T(8,128)(2,1)} %bitcast.41, bf16[2048,1024]{1,0:T(8,128)(2,1)} %bitcast.44), custom_call_target="tpu_custom_call" | custom-call | flops 2147483648 | bytes 8388608 | tf_op jit(solution)/shard_map/expert_rows/pallas_call | solution.py:63
  85.2 1.6 collective-permute-start.3
  87.2 0.4 lay_out.1
  87.6 1.8 %collective-permute-done.1.back = bf16[2,128,1024]{2,1,0:T(8,128)(2,1)S(1)} collective-permute-done((bf16[2,128,1024]{2,1,0:T(8,128)(2,1)S(1)}, bf16[2,128,1024]{2,1,0:T(8,128)(2,1)S(1)}, u32[]{:S(2)}, u32[]{:S(2)}) %collective-permute-start.1) | collective-permute-done | bytes 524320 | tf_op jit(solution)/shard_map/ppermute | solution.py:14
  89.6 0.5 copy.33
  90.1 0.7 pad.4
  90.8 9.9 %collective-permute-done.3.back = bf16[2,128,1024]{2,1,0:T(8,128)(2,1)S(1)} collective-permute-done((bf16[2,128,1024]{2,1,0:T(8,128)(2,1)S(1)}, bf16[2,128,1024]{2,1,0:T(8,128)(2,1)S(1)}, u32[]{:S(2)}, u32[]{:S(2)}) %collective-permute-start.3) | collective-permute-done | bytes 524320 | tf_op jit(solution)/shard_map/ppermute | solution.py:14
  100.8 0.5 copy.36
  101.4 0.4 constant_dynamic-update-slice_fusion
  101.8 0.8 copy.37
  102.6 38.5 %all_to_all.16 = bf16[128,2,2,1024]{3,2,1,0:T(2,128)(2,1)S(1)} all-to-all(bf16[128,2,2,1024]{3,2,1,0:T(2,128)(2,1)S(1)} %copy.37), channel_id=1, replica_groups=mesh['expert'=128,'hidden'=2] {'expert'}, dimensions={0} | all-to-all | bytes 2097152 | tf_op jit(solution)/shard_map/all_to_all | solution.py:210
  141.2 0.7 fusion.18
  142.2 1.8 %logit_grads.1 = (bf16[2,196,128]{2,1,0:T(8,128)(2,1)S(1)}, bf16[1024,128]{1,0:T(8,128)(2,1)}) custom-call(bf16[2,196,1024]{2,1,0:T(8,128)(2,1)S(1)} %get-tuple-element.29.tokens, bf16[2,1024,196]{2,1,0:T(8,128)(2,1)S(1)} %get-tuple-element.30.turned, bf16[2,196,1024]{2,1,0:T(8,128)(2,1)S(1)} %get-tuple-element.31.grads, ...), custom_call_target="tpu_custom_call" | custom-call | flops 308281344 | bytes 3211264 | tf_op jit(solution)/shard_map/logit_grads/pallas_call | solution.py:150
  144.0 6.9 %all-to-all-start.2 = ((bf16[256,4,128]{2,1,0:T(4,128)(2,1)}), bf16[256,4,128]{2,1,0:T(4,128)(2,1)S(1)}, u32[]{:S(2)}, u32[]{:S(2)}) async-start(bf16[256,4,128]{2,1,0:T(4,128)(2,1)} %bitcast.19), calls=%async_computation.2 | async-start | bytes 524288 | tf_op jit(solution)/shard_map/all_to_all | solution.py:223
  151.3 0.4 add_convert_fusion
  151.7 1.7 %copy.40 = bf16[2,196,1024]{2,0,1:T(2,128)(2,1)} copy(bf16[2,196,1024]{2,1,0:T(8,128)(2,1)S(1)} %add_convert_fusion) | data formatting | bytes 1605632
  153.4 12.6 %all-to-all-done.2 = bf16[256,4,128]{2,1,0:T(4,128)(2,1)S(1)} async-done(((bf16[256,4,128]{2,1,0:T(4,128)(2,1)}), bf16[256,4,128]{2,1,0:T(4,128)(2,1)S(1)}, u32[]{:S(2)}, u32[]{:S(2)}) %all-to-all-start.2) | async-done | bytes 262176 | tf_op jit(solution)/shard_map/all_to_all | solution.py:223
  166.0 0.9 convert_reduce_fusion
  (24 shorter events, 3.2 us)
Async XLA Ops:
  0.6 1.0 copy-start
  0.6 3.1 %copy-start.1 = (bf16[2,196,1024]{2,0,1:T(2,128)(2,1)S(1)}, bf16[2,196,1024]{2,0,1:T(2,128)(2,1)}, u32[]{:S(2)}) copy-start(bf16[2,196,1024]{2,0,1:T(2,128)(2,1)} %param.5) | copy-start | bytes 2408452
  3.1 1.3 copy-start.3
  54.9 12.0 %collective-permute-start = (bf16[2,128,1024]{2,1,0:T(8,128)(2,1)S(1)}, bf16[2,128,1024]{2,1,0:T(8,128)(2,1)S(1)}, u32[]{:S(2)}, u32[]{:S(2)}) collective-permute-start(bf16[2,128,1024]{2,1,0:T(8,128)(2,1)S(1)} %reshape.28.refs_0_), channel_id=1, source_target_pairs={{0,1},{1,0},{2,3},{3,2},{4,5},{5,4},{6,7},{7,6},{8,9},{9,8},{10,11... | collective-permute-start | bytes 1572872 | tf_op jit(solution)/shard_map/ppermute | solution.py:14
  64.2 14.1 %collective-permute-start.2 = (bf16[2,128,1024]{2,1,0:T(8,128)(2,1)S(1)}, bf16[2,128,1024]{2,1,0:T(8,128)(2,1)S(1)}, u32[]{:S(2)}, u32[]{:S(2)}) collective-permute-start(bf16[2,128,1024]{2,1,0:T(8,128)(2,1)S(1)} %reshape.30.refs_1_), channel_id=1, source_target_pairs={{0,1},{1,0},{2,3},{3,2},{4,5},{5,4},{6,7},{7,6},{8,9},{9,8},{10,11... | collective-permute-start | bytes 1572872 | tf_op jit(solution)/shard_map/ppermute | solution.py:14
  73.9 12.9 %copy-start.2 = (bf16[2,196,1024]{2,0,1:T(2,128)(2,1)S(1)}, bf16[2,196,1024]{2,0,1:T(2,128)(2,1)}, u32[]{:S(2)}) copy-start(bf16[2,196,1024]{2,0,1:T(2,128)(2,1)} %param.5) | copy-start | bytes 2408452
  73.9 15.6 %collective-permute-start.1 = (bf16[2,128,1024]{2,1,0:T(8,128)(2,1)S(1)}, bf16[2,128,1024]{2,1,0:T(8,128)(2,1)S(1)}, u32[]{:S(2)}, u32[]{:S(2)}) collective-permute-start(bf16[2,128,1024]{2,1,0:T(8,128)(2,1)S(1)} %expert_rows.4), channel_id=1, source_target_pairs={{0,1},{1,0},{2,3},{3,2},{4,5},{5,4},{6,7},{7,6},{8,9},{9,8},{10,11... | collective-permute-start | bytes 1572872 | tf_op jit(solution)/shard_map/ppermute | solution.py:14
  85.2 1.8 %copy-start.4 = (bf16[2,196,1024]{2,0,1:T(2,128)(2,1)S(1)}, bf16[2,196,1024]{2,0,1:T(2,128)(2,1)}, u32[]{:S(2)}) copy-start(bf16[2,196,1024]{2,0,1:T(2,128)(2,1)} %param.6) | copy-start | bytes 2408452
  85.2 15.5 %collective-permute-start.3 = (bf16[2,128,1024]{2,1,0:T(8,128)(2,1)S(1)}, bf16[2,128,1024]{2,1,0:T(8,128)(2,1)S(1)}, u32[]{:S(2)}, u32[]{:S(2)}) collective-permute-start(bf16[2,128,1024]{2,1,0:T(8,128)(2,1)S(1)} %expert_rows.5), channel_id=1, source_target_pairs={{0,1},{1,0},{2,3},{3,2},{4,5},{5,4},{6,7},{7,6},{8,9},{9,8},{10,11... | collective-permute-start | bytes 1572872 | tf_op jit(solution)/shard_map/ppermute | solution.py:14
  144.0 22.1 %all-to-all-start.2 = ((bf16[256,4,128]{2,1,0:T(4,128)(2,1)}), bf16[256,4,128]{2,1,0:T(4,128)(2,1)S(1)}, u32[]{:S(2)}, u32[]{:S(2)}) async-start(bf16[256,4,128]{2,1,0:T(4,128)(2,1)} %bitcast.19), calls=%async_computation.2 | async-start | bytes 524288 | tf_op jit(solution)/shard_map/all_to_all | solution.py:223

commit v8 on v7

--- a/solution.py
+++ b/solution.py
@@ -177,13 +177,13 @@
     slot_grads = jnp.einsum(
         "imn,imd->ind", combine_b, grad_out, preferred_element_type=jnp.float32
     ).astype(jnp.bfloat16)
-    both = jnp.stack([slot_inputs, slot_grads], axis=0)
-    both = jnp.transpose(both, (2, 0, 1, 3))
+    both = jnp.transpose(jnp.stack([slot_inputs, slot_grads], axis=0), (2, 1, 0, 3))
     experts, _, _, width = both.shape
-    both = lax.all_to_all(both, "expert", split_axis=0, concat_axis=0, tiled=True)
-    both = both.reshape(2, experts // 2, 2, images, width)
-    piece_a = jnp.transpose(both[0], (1, 0, 2, 3)).reshape(2, -1, width)
-    piece_b = jnp.transpose(after(both, piece_a)[1], (1, 0, 2, 3)).reshape(2, -1, width)
+    both = lax.all_to_all(
+        both.reshape(images * experts, 2, width), BOTH, split_axis=0, concat_axis=0, tiled=True
+    )
+    piece_a = jnp.transpose(both[:experts], (1, 0, 2))
+    piece_b = jnp.transpose(after(both, piece_a)[experts:], (1, 0, 2))
     first, second = (
         pltpu.with_memory_space_constraint(weight[0], pltpu.HBM)
         for weight in (in_weight, out_weight)
@@ -198,18 +198,16 @@
     (sent_b,) = expert_pass([pair_b], jnp.bfloat16, first, second)
     back_b = swap(sent_b)
     def packed(mine_part, back_part):
-        half = sum_halves(mine_part, back_part)
-        half = half.reshape(2, experts // 2, images, width)
-        return jnp.transpose(half, (1, 0, 2, 3))
-
-    sums = jnp.pad(packed(mine[0], back_a), ((0, experts // 2), (0, 0), (0, 0), (0, 0)))
+        return jnp.transpose(sum_halves(mine_part, back_part), (1, 0, 2))
+
+    sums = jnp.pad(packed(mine[0], back_a), ((0, experts), (0, 0), (0, 0)))
     sums, flat_tokens, turned, flat_grads, back_b = lax.optimization_barrier(
         (sums, flat_tokens, turned, flat_grads, back_b)
     )
-    sums = lax.dynamic_update_slice(sums, packed(mine[1], back_b), (experts // 2, 0, 0, 0))
-    summed = lax.all_to_all(sums, "expert", split_axis=0, concat_axis=0, tiled=True)
-    slot_outputs = jnp.transpose(summed[:, 0], (1, 0, 2))
-    slot_in_grad = jnp.transpose(summed[:, 1], (1, 0, 2))
+    sums = lax.dynamic_update_slice(sums, packed(mine[1], back_b), (experts, 0, 0))
+    summed = lax.all_to_all(sums, BOTH, split_axis=0, concat_axis=0, tiled=True)
+    summed = jnp.transpose(summed.reshape(experts, images, 2, width), (2, 1, 0, 3))
+    slot_outputs, slot_in_grad = summed[0], summed[1]
     logit_grad, phi_parts = logit_grads(
         flat_tokens, turned, flat_grads, combine, dispatch, slot_outputs, slot_in_grad
     )

time: 167 us -> 163 us (0.976)
  waiting for transfers between devices: 29.5 us -> 34.7 us
  starting transfers between devices: 11.6 us -> 8.19 us
  local copies, waits for them, and re-layouts: 9.62 us -> 6.52 us
  blocking collectives: 86.5 us -> 83.9 us
    ppermute x4, waiting for transfers between devices: 16.9 us -> 22.2 us  [swap(): return lax.ppermute(block, 'hidden', [(0, 1), (1, 0)])]
    ppermute x4, starting transfers between devices: 4.64 us -> 2.02 us  [swap(): return lax.ppermute(block, 'hidden', [(0, 1), (1, 0)])]
    all_to_all x2, blocking collectives: 86.5 us -> 83.9 us  [the longest x1 46.7 us: local(): lax.all_to_all(both.reshape(images * experts, 2, width), BOTH, split_axis...]
  transfers between devices with their start and end apart: 5 -> 5, of which waited for: 5 -> 5; matrix products, arithmetic and copies ran while one was open for 3% -> 2% of each run, Pallas kernels for 13% -> 14%
where the time goes in v8:
time: 163 us
  blocking collectives  83.9 us (51%)
  waiting for transfers between devices  34.7 us (21%)
  Pallas kernels  23.9 us (15%)
  starting transfers between devices  8.19 us (5%)
  local copies, waits for them, and re-layouts  6.52 us (4%)
  matrix products  3.2 us (2%)
  other arithmetic  1.69 us (1%)
    all_to_all x1, blocking collectives, local(): lax.all_to_all(both.reshape(images * experts, 2, width), BOTH, split_axis...  46.7 us
    all_to_all x1, blocking collectives, local(): summed = lax.all_to_all(sums, BOTH, split_axis=0, concat_axis=0, tiled=True)  37.2 us
    ppermute x4, waiting for transfers between devices, swap(): return lax.ppermute(block, 'hidden', [(0, 1), (1, 0)])  22.2 us
    pallas_call x3, Pallas kernels, expert_pass(): pl.pallas_call(lambda *refs: expert_kernel(count, *refs), grid=(hidden //...  21.4 us
    all_to_all x1, waiting for transfers between devices, local(): lax.all_to_all(phi_parts, BOTH, split_axis=0, concat_axis=0, tiled=True)  12.5 us
    all_to_all x1, starting transfers between devices, local(): lax.all_to_all(phi_parts, BOTH, split_axis=0, concat_axis=0, tiled=True)  6.17 us
  transfers between devices with their start and end apart: 5, of which 5 were waited for; matrix products, arithmetic and copies ran while one was open for 2% of the time, Pallas kernels for 14%

profile of v8, /device:TPU:1, one launch (start us, length us, event | category | flops | bytes accessed | tf_op | source)
XLA Modules:
  0.0 162.9 jit_solution(9226973707922391906)
XLA Ops:
  0.7 0.9 copy-done
  1.6 1.5 fusion.10
  3.3 0.4 fusion.19
  3.9 0.4 fusion.2
  4.4 0.4 fusion.3
  4.9 1.1 copy.36
  6.0 46.7 %all_to_all.15 = bf16[256,2,1024]{2,1,0:T(2,128)(2,1)S(1)} all-to-all(bf16[256,2,1024]{2,1,0:T(2,128)(2,1)S(1)} %bitcast.46), channel_id=1, replica_groups=mesh['expert'=128,'hidden'=2] {'expert','hidden'}, dimensions={0} | all-to-all | bytes 2097152 | tf_op jit(solution)/shard_map/all_to_all | solution.py:182
  52.7 0.4 slice.16
  53.2 0.7 collective-permute-start
  53.9 0.3 copy.38
  54.2 7.5 %expert_rows.3 = (f32[2,128,1024]{2,1,0:T(8,128)S(1)}, f32[2,128,1024]{2,1,0:T(8,128)S(1)}) custom-call(bf16[2,128,1024]{2,1,0:T(8,128)(2,1)S(1)} %bitcast.37, bf16[2,128,1024]{2,1,0:T(8,128)(2,1)S(1)} %slice_bitcast_fusion.2.refs_1_, bf16[1024,2048]{1,0:T(8,128)(2,1)} %bitcast.38, bf16[2048,1024]{1,0:T(8,128)(2,1)} %bitcast.41), custom_call_target="tpu_custom_call" | custom-call | flops 4294967296 | bytes 8388608 | tf_op jit(solution)/shard_map/expert_rows/pallas_call | solution.py:63
  61.7 1.0 collective-permute-start.2
  62.7 3.9 %collective-permute-done.refs_0_ = bf16[2,128,1024]{2,1,0:T(8,128)(2,1)S(1)} collective-permute-done((bf16[2,128,1024]{2,1,0:T(8,128)(2,1)S(1)}, bf16[2,128,1024]{2,1,0:T(8,128)(2,1)S(1)}, u32[]{:S(2)}, u32[]{:S(2)}) %collective-permute-start) | collective-permute-done | bytes 524320 | tf_op jit(solution)/shard_map/ppermute | solution.py:14
  66.6 7.0 %expert_rows.4 = bf16[2,128,1024]{2,1,0:T(8,128)(2,1)S(1)} custom-call(bf16[2,128,1024]{2,1,0:T(8,128)(2,1)S(1)} %collective-permute-done.refs_0_, bf16[1024,2048]{1,0:T(8,128)(2,1)} %bitcast.39, bf16[2048,1024]{1,0:T(8,128)(2,1)} %bitcast.42), custom_call_target="tpu_custom_call" | custom-call | flops 2147483648 | bytes 8388608 | tf_op jit(solution)/shard_map/expert_rows/pallas_call | solution.py:63
  73.7 4.2 %collective-permute-done.2.refs_0_ = bf16[2,128,1024]{2,1,0:T(8,128)(2,1)S(1)} collective-permute-done((bf16[2,128,1024]{2,1,0:T(8,128)(2,1)S(1)}, bf16[2,128,1024]{2,1,0:T(8,128)(2,1)S(1)}, u32[]{:S(2)}, u32[]{:S(2)}) %collective-permute-start.2) | collective-permute-done | bytes 524320 | tf_op jit(solution)/shard_map/ppermute | solution.py:14
  77.9 7.0 %expert_rows.5 = bf16[2,128,1024]{2,1,0:T(8,128)(2,1)S(1)} custom-call(bf16[2,128,1024]{2,1,0:T(8,128)(2,1)S(1)} %collective-permute-done.2.refs_0_, bf16[1024,2048]{1,0:T(8,128)(2,1)} %bitcast.40, bf16[2048,1024]{1,0:T(8,128)(2,1)} %bitcast.43), custom_call_target="tpu_custom_call" | custom-call | flops 2147483648 | bytes 8388608 | tf_op jit(solution)/shard_map/expert_rows/pallas_call | solution.py:63
  84.8 0.3 collective-permute-start.3
  85.1 0.2 copy.39.tokens
  85.3 0.2 copy.40.grads
  85.5 0.4 lay_out.1
  85.9 3.2 %collective-permute-done.1.back = bf16[2,128,1024]{2,1,0:T(8,128)(2,1)S(1)} collective-permute-done((bf16[2,128,1024]{2,1,0:T(8,128)(2,1)S(1)}, bf16[2,128,1024]{2,1,0:T(8,128)(2,1)S(1)}, u32[]{:S(2)}, u32[]{:S(2)}) %collective-permute-start.1) | collective-permute-done | bytes 524320 | tf_op jit(solution)/shard_map/ppermute | solution.py:14
  89.4 11.0 %collective-permute-done.3.back = bf16[2,128,1024]{2,1,0:T(8,128)(2,1)S(1)} collective-permute-done((bf16[2,128,1024]{2,1,0:T(8,128)(2,1)S(1)}, bf16[2,128,1024]{2,1,0:T(8,128)(2,1)S(1)}, u32[]{:S(2)}, u32[]{:S(2)}) %collective-permute-start.3) | collective-permute-done | bytes 524320 | tf_op jit(solution)/shard_map/ppermute | solution.py:14
  100.5 1.1 copy.41
  101.6 37.2 %all_to_all.16 = bf16[256,2,1024]{2,1,0:T(2,128)(2,1)S(1)} all-to-all(bf16[256,2,1024]{2,1,0:T(2,128)(2,1)S(1)} %copy.41), channel_id=1, replica_groups=mesh['expert'=128,'hidden'=2] {'expert','hidden'}, dimensions={0} | all-to-all | bytes 2097152 | tf_op jit(solution)/shard_map/all_to_all | solution.py:208
  138.7 0.3 copy.53
  139.1 1.8 %logit_grads.1 = (bf16[2,196,128]{2,1,0:T(8,128)(2,1)S(1)}, bf16[1024,128]{1,0:T(8,128)(2,1)}) custom-call(bf16[2,196,1024]{2,1,0:T(8,128)(2,1)S(1)} %get-tuple-element.29.tokens, bf16[2,1024,196]{2,1,0:T(8,128)(2,1)S(1)} %get-tuple-element.30.turned, bf16[2,196,1024]{2,1,0:T(8,128)(2,1)S(1)} %get-tuple-element.31.grads, ...), custom_call_target="tpu_custom_call" | custom-call | flops 308281344 | bytes 3211264 | tf_op jit(solution)/shard_map/logit_grads/pallas_call | solution.py:150
  140.9 6.2 %all-to-all-start.2 = ((bf16[256,4,128]{2,1,0:T(4,128)(2,1)}), bf16[256,4,128]{2,1,0:T(4,128)(2,1)S(1)}, u32[]{:S(2)}, u32[]{:S(2)}) async-start(bf16[256,4,128]{2,1,0:T(4,128)(2,1)} %bitcast.15), calls=%async_computation.2 | async-start | bytes 524288 | tf_op jit(solution)/shard_map/all_to_all | solution.py:221
  147.1 0.4 fusion.15
  147.5 0.4 add_convert_fusion
  147.9 1.7 %copy.43 = bf16[2,196,1024]{2,0,1:T(2,128)(2,1)} copy(bf16[2,196,1024]{2,1,0:T(8,128)(2,1)S(1)} %add_convert_fusion) | data formatting | bytes 1605632
  149.6 12.5 %all-to-all-done.2 = bf16[256,4,128]{2,1,0:T(4,128)(2,1)S(1)} async-done(((bf16[256,4,128]{2,1,0:T(4,128)(2,1)}), bf16[256,4,128]{2,1,0:T(4,128)(2,1)S(1)}, u32[]{:S(2)}, u32[]{:S(2)}) %all-to-all-start.2) | async-done | bytes 262176 | tf_op jit(solution)/shard_map/all_to_all | solution.py:221
  162.1 0.9 convert_reduce_fusion
  (16 shorter events, 1.1 us)
Async XLA Ops:
  0.6 1.0 copy-start
  0.6 3.2 %copy-start.1 = (bf16[2,196,1024]{2,0,1:T(2,128)(2,1)S(1)}, bf16[2,196,1024]{2,0,1:T(2,128)(2,1)}, u32[]{:S(2)}) copy-start(bf16[2,196,1024]{2,0,1:T(2,128)(2,1)} %param.5) | copy-start | bytes 2408452
  3.1 1.2 copy-start.2
  53.2 13.4 %collective-permute-start = (bf16[2,128,1024]{2,1,0:T(8,128)(2,1)S(1)}, bf16[2,128,1024]{2,1,0:T(8,128)(2,1)S(1)}, u32[]{:S(2)}, u32[]{:S(2)}) collective-permute-start(bf16[2,128,1024]{2,1,0:T(8,128)(2,1)S(1)} %bitcast.36), channel_id=1, source_target_pairs={{0,1},{1,0},{2,3},{3,2},{4,5},{5,4},{6,7},{7,6},{8,9},{9,8},{10,11... | collective-permute-start | bytes 1572872 | tf_op jit(solution)/shard_map/ppermute | solution.py:14
  61.7 16.1 %collective-permute-start.2 = (bf16[2,128,1024]{2,1,0:T(8,128)(2,1)S(1)}, bf16[2,128,1024]{2,1,0:T(8,128)(2,1)S(1)}, u32[]{:S(2)}, u32[]{:S(2)}) collective-permute-start(bf16[2,128,1024]{2,1,0:T(8,128)(2,1)S(1)} %slice_bitcast_fusion.2.refs_1_), channel_id=1, source_target_pairs={{0,1},{1,0},{2,3},{3,2},{4,5},{5,4},{6,7},{7,6},{8,9},{9,8},{10,11... | collective-permute-start | bytes 1572872 | tf_op jit(solution)/shard_map/ppermute | solution.py:14
  73.6 15.5 %collective-permute-start.1 = (bf16[2,128,1024]{2,1,0:T(8,128)(2,1)S(1)}, bf16[2,128,1024]{2,1,0:T(8,128)(2,1)S(1)}, u32[]{:S(2)}, u32[]{:S(2)}) collective-permute-start(bf16[2,128,1024]{2,1,0:T(8,128)(2,1)S(1)} %expert_rows.4), channel_id=1, source_target_pairs={{0,1},{1,0},{2,3},{3,2},{4,5},{5,4},{6,7},{7,6},{8,9},{9,8},{10,11... | collective-permute-start | bytes 1572872 | tf_op jit(solution)/shard_map/ppermute | solution.py:14
  84.8 15.5 %collective-permute-start.3 = (bf16[2,128,1024]{2,1,0:T(8,128)(2,1)S(1)}, bf16[2,128,1024]{2,1,0:T(8,128)(2,1)S(1)}, u32[]{:S(2)}, u32[]{:S(2)}) collective-permute-start(bf16[2,128,1024]{2,1,0:T(8,128)(2,1)S(1)} %expert_rows.5), channel_id=1, source_target_pairs={{0,1},{1,0},{2,3},{3,2},{4,5},{5,4},{6,7},{7,6},{8,9},{9,8},{10,11... | collective-permute-start | bytes 1572872 | tf_op jit(solution)/shard_map/ppermute | solution.py:14
  140.9 21.1 %all-to-all-start.2 = ((bf16[256,4,128]{2,1,0:T(4,128)(2,1)}), bf16[256,4,128]{2,1,0:T(4,128)(2,1)S(1)}, u32[]{:S(2)}, u32[]{:S(2)}) async-start(bf16[256,4,128]{2,1,0:T(4,128)(2,1)} %bitcast.15), calls=%async_computation.2 | async-start | bytes 524288 | tf_op jit(solution)/shard_map/all_to_all | solution.py:221

commit v9 on v8

--- a/solution.py
+++ b/solution.py
@@ -100,14 +100,18 @@
     )(mine, back)
 
 
-def lay_out_kernel(tokens, grads, flat_tokens, turned, flat_grads):
+def lay_out_kernel(
+    tokens, grads, combine, dispatch, flat_tokens, turned, flat_grads, near_combine, near_dispatch
+):
+    near_combine[...] = combine[...]
+    near_dispatch[...] = dispatch[...]
     flat_tokens[...] = tokens[...]
     flat_grads[...] = grads[...]
     for image in range(tokens.shape[0]):
         turned[image] = tokens[image].T
 
 
-def lay_out(tokens, grads):
+def lay_out(tokens, grads, combine, dispatch):
     images, rows, width = tokens.shape
     return pl.pallas_call(
         lay_out_kernel,
@@ -115,13 +119,15 @@
             jax.ShapeDtypeStruct(tokens.shape, tokens.dtype),
             jax.ShapeDtypeStruct((images, width, rows), tokens.dtype),
             jax.ShapeDtypeStruct(grads.shape, grads.dtype),
+            jax.ShapeDtypeStruct(combine.shape, combine.dtype),
+            jax.ShapeDtypeStruct(dispatch.shape, dispatch.dtype),
         ],
         compiler_params=pltpu.CompilerParams(vmem_limit_bytes=16 * 2**20),
         cost_estimate=pl.CostEstimate(
             flops=0, bytes_accessed=10 * tokens.size, transcendentals=0
         ),
         name="lay_out",
-    )(tokens, grads)
+    )(tokens, grads, combine, dispatch)
 
 
 def grad_kernel(tokens, turned, grads, combine, dispatch, outs, backs, logit_grad, phi):
@@ -163,21 +169,51 @@
     )(tokens, turned, grads, combine, dispatch, outs, backs)
 
 
+def slot_kernel(tokens, grads, weight, dispatch_b, dispatch, combine, slots):
+    for image in range(tokens.shape[0]):
+        own = tokens[image]
+        logits = jnp.dot(own, weight[...], preferred_element_type=jnp.float32)
+        disp = jnp.exp(logits - jnp.max(logits, axis=0, keepdims=True))
+        disp = disp / jnp.sum(disp, axis=0, keepdims=True)
+        comb = jnp.exp(logits - jnp.max(logits, axis=1, keepdims=True))
+        comb = comb / jnp.sum(comb, axis=1, keepdims=True)
+        dispatch[image] = disp
+        combine[image] = comb
+        dispatch_b[image] = disp.astype(jnp.bfloat16)
+        slots[0, image] = jnp.dot(
+            disp.T.astype(jnp.bfloat16), own, preferred_element_type=jnp.float32
+        ).astype(jnp.bfloat16)
+        slots[1, image] = jnp.dot(
+            comb.T.astype(jnp.bfloat16), grads[image], preferred_element_type=jnp.float32
+        ).astype(jnp.bfloat16)
+
+
+def slot_rows(tokens, grads, weight):
+    images, rows, width = tokens.shape
+    count = weight.shape[1]
+    wide = jax.ShapeDtypeStruct((images, rows, count), jnp.float32)
+    return pl.pallas_call(
+        slot_kernel,
+        out_shape=[
+            jax.ShapeDtypeStruct((images, rows, count), jnp.bfloat16),
+            wide,
+            wide,
+            jax.ShapeDtypeStruct((2, images, count, width), jnp.bfloat16),
+        ],
+        compiler_params=pltpu.CompilerParams(vmem_limit_bytes=16 * 2**20),
+        cost_estimate=pl.CostEstimate(
+            flops=6 * images * rows * width * count,
+            bytes_accessed=8 * images * rows * width,
+            transcendentals=2 * images * rows * count,
+        ),
+        name="slot_rows",
+    )(tokens, grads, weight)
+
+
 def local(tokens, grad_out, slot_weight, in_weight, out_weight):
     images = tokens.shape[0]
-    logits = jnp.einsum("imd,dn->imn", tokens, slot_weight, preferred_element_type=jnp.float32)
-    logits = lax.optimization_barrier(logits)
-    dispatch = jax.nn.softmax(logits, axis=1)
-    combine = jax.nn.softmax(logits, axis=2)
-    dispatch_b = dispatch.astype(jnp.bfloat16)
-    combine_b = combine.astype(jnp.bfloat16)
-    slot_inputs = jnp.einsum(
-        "imn,imd->ind", dispatch_b, tokens, preferred_element_type=jnp.float32
-    ).astype(jnp.bfloat16)
-    slot_grads = jnp.einsum(
-        "imn,imd->ind", combine_b, grad_out, preferred_element_type=jnp.float32
-    ).astype(jnp.bfloat16)
-    both = jnp.transpose(jnp.stack([slot_inputs, slot_grads], axis=0), (2, 1, 0, 3))
+    dispatch_b, dispatch, combine, slots = slot_rows(tokens, grad_out, slot_weight)
+    both = jnp.transpose(slots, (2, 1, 0, 3))
     experts, _, _, width = both.shape
     both = lax.all_to_all(
         both.reshape(images * experts, 2, width), BOTH, split_axis=0, concat_axis=0, tiled=True
@@ -191,8 +227,8 @@
     pair_a = swap(piece_a)
     mine = expert_pass([piece_a, piece_b], jnp.float32, first, second)
     pair_b = swap(after(piece_b, mine[0]))
-    early_tokens, early_grads, _ = lax.optimization_barrier((tokens, grad_out, mine[0]))
-    flat_tokens, turned, flat_grads = lay_out(early_tokens, early_grads)
+    early = lax.optimization_barrier((tokens, grad_out, combine, dispatch, mine[0]))
+    placed = lay_out(*early[:4])
     (sent_a,) = expert_pass([pair_a], jnp.bfloat16, first, second)
     back_a = swap(sent_a)
     (sent_b,) = expert_pass([pair_b], jnp.bfloat16, first, second)
@@ -201,16 +237,12 @@
         return jnp.transpose(sum_halves(mine_part, back_part), (1, 0, 2))
 
     sums = jnp.pad(packed(mine[0], back_a), ((0, experts), (0, 0), (0, 0)))
-    sums, flat_tokens, turned, flat_grads, back_b = lax.optimization_barrier(
-        (sums, flat_tokens, turned, flat_grads, back_b)
-    )
+    sums, back_b, *placed = lax.optimization_barrier((sums, back_b, *placed))
     sums = lax.dynamic_update_slice(sums, packed(mine[1], back_b), (experts, 0, 0))
     summed = lax.all_to_all(sums, BOTH, split_axis=0, concat_axis=0, tiled=True)
     summed = jnp.transpose(summed.reshape(experts, images, 2, width), (2, 1, 0, 3))
     slot_outputs, slot_in_grad = summed[0], summed[1]
-    logit_grad, phi_parts = logit_grads(
-        flat_tokens, turned, flat_grads, combine, dispatch, slot_outputs, slot_in_grad
-    )
+    logit_grad, phi_parts = logit_grads(*placed, slot_outputs, slot_in_grad)
     input_grad = jnp.einsum(
         "imn,ind->imd", dispatch_b, slot_in_grad, preferred_element_type=jnp.float32
     )

time: 163 us -> 162 us (level)
  matrix products: 3.2 us -> 0.78 us
    dot_general x3 -> x0, matrix products: 2.41 us -> none  [the longest x1 1.52 us: local(): jnp.einsum('imd,dn->imn', tokens, slot_weight, preferred_element_type=jnp...]
    unnamed x8 -> x10, local copies, waits for them, and re-layouts: 2.77 us -> 3.46 us
where the time goes in v9:
time: 162 us
  blocking collectives  83.9 us (52%)
  waiting for transfers between devices  34.6 us (21%)
  Pallas kernels  25.4 us (16%)
  starting transfers between devices  8.22 us (5%)
  local copies, waits for them, and re-layouts  7.21 us (4%)
    all_to_all x1, blocking collectives, local(): lax.all_to_all(both.reshape(images * experts, 2, width), BOTH, split_axis...  46.7 us
    all_to_all x1, blocking collectives, local(): summed = lax.all_to_all(sums, BOTH, split_axis=0, concat_axis=0, tiled=True)  37.2 us
    ppermute x4, waiting for transfers between devices, swap(): return lax.ppermute(block, 'hidden', [(0, 1), (1, 0)])  22.1 us
    pallas_call x3, Pallas kernels, expert_pass(): pl.pallas_call(lambda *refs: expert_kernel(count, *refs), grid=(hidden //...  21.4 us
    all_to_all x1, waiting for transfers between devices, local(): lax.all_to_all(phi_parts, BOTH, split_axis=0, concat_axis=0, tiled=True)  12.5 us
    all_to_all x1, starting transfers between devices, local(): lax.all_to_all(phi_parts, BOTH, split_axis=0, concat_axis=0, tiled=True)  6.17 us
    unnamed x10, local copies, waits for them, and re-layouts  3.46 us
  transfers between devices with their start and end apart: 5, of which 5 were waited for; matrix products, arithmetic and copies ran while one was open for 2% of the time, Pallas kernels for 14%

profile of v9, /device:TPU:1, one launch (start us, length us, event | category | flops | bytes accessed | tf_op | source)
XLA Modules:
  0.0 161.8 jit_solution(1362611693471382041)
XLA Ops:
  0.6 1.4 copy.30.tokens
  2.1 0.2 copy.31.grads
  2.3 1.4 slot_rows.1
  3.7 1.1 copy.32
  4.8 46.7 %all_to_all.15 = bf16[256,2,1024]{2,1,0:T(2,128)(2,1)S(1)} all-to-all(bf16[256,2,1024]{2,1,0:T(2,128)(2,1)S(1)} %bitcast.39), channel_id=1, replica_groups=mesh['expert'=128,'hidden'=2] {'expert','hidden'}, dimensions={0} | all-to-all | bytes 2097152 | tf_op jit(solution)/shard_map/all_to_all | solution.py:218
  51.5 0.4 slice.16
  52.0 0.7 collective-permute-start
  52.7 0.3 copy.34
  53.0 7.5 %expert_rows.3 = (f32[2,128,1024]{2,1,0:T(8,128)S(1)}, f32[2,128,1024]{2,1,0:T(8,128)S(1)}) custom-call(bf16[2,128,1024]{2,1,0:T(8,128)(2,1)S(1)} %bitcast.30, bf16[2,128,1024]{2,1,0:T(8,128)(2,1)S(1)} %slice_bitcast_fusion.2.refs_1_, bf16[1024,2048]{1,0:T(8,128)(2,1)} %bitcast.31, bf16[2048,1024]{1,0:T(8,128)(2,1)} %bitcast.34), custom_call_target="tpu_custom_call" | custom-call | flops 4294967296 | bytes 8388608 | tf_op jit(solution)/shard_map/expert_rows/pallas_call | solution.py:63
  60.5 1.0 collective-permute-start.2
  61.5 3.9 %collective-permute-done.refs_0_ = bf16[2,128,1024]{2,1,0:T(8,128)(2,1)S(1)} collective-permute-done((bf16[2,128,1024]{2,1,0:T(8,128)(2,1)S(1)}, bf16[2,128,1024]{2,1,0:T(8,128)(2,1)S(1)}, u32[]{:S(2)}, u32[]{:S(2)}) %collective-permute-start) | collective-permute-done | bytes 524320 | tf_op jit(solution)/shard_map/ppermute | solution.py:14
  65.4 7.0 %expert_rows.4 = bf16[2,128,1024]{2,1,0:T(8,128)(2,1)S(1)} custom-call(bf16[2,128,1024]{2,1,0:T(8,128)(2,1)S(1)} %collective-permute-done.refs_0_, bf16[1024,2048]{1,0:T(8,128)(2,1)} %bitcast.32, bf16[2048,1024]{1,0:T(8,128)(2,1)} %bitcast.35), custom_call_target="tpu_custom_call" | custom-call | flops 2147483648 | bytes 8388608 | tf_op jit(solution)/shard_map/expert_rows/pallas_call | solution.py:63
  72.5 4.1 %collective-permute-done.2.refs_0_ = bf16[2,128,1024]{2,1,0:T(8,128)(2,1)S(1)} collective-permute-done((bf16[2,128,1024]{2,1,0:T(8,128)(2,1)S(1)}, bf16[2,128,1024]{2,1,0:T(8,128)(2,1)S(1)}, u32[]{:S(2)}, u32[]{:S(2)}) %collective-permute-start.2) | collective-permute-done | bytes 524320 | tf_op jit(solution)/shard_map/ppermute | solution.py:14
  76.7 7.0 %expert_rows.5 = bf16[2,128,1024]{2,1,0:T(8,128)(2,1)S(1)} custom-call(bf16[2,128,1024]{2,1,0:T(8,128)(2,1)S(1)} %collective-permute-done.2.refs_0_, bf16[1024,2048]{1,0:T(8,128)(2,1)} %bitcast.33, bf16[2048,1024]{1,0:T(8,128)(2,1)} %bitcast.36), custom_call_target="tpu_custom_call" | custom-call | flops 2147483648 | bytes 8388608 | tf_op jit(solution)/shard_map/expert_rows/pallas_call | solution.py:63
  83.6 0.3 collective-permute-start.3
  83.9 0.2 copy.35.tokens
  84.1 0.2 copy.36.grads
  84.3 0.4 lay_out.1
  84.8 3.1 %collective-permute-done.1.back = bf16[2,128,1024]{2,1,0:T(8,128)(2,1)S(1)} collective-permute-done((bf16[2,128,1024]{2,1,0:T(8,128)(2,1)S(1)}, bf16[2,128,1024]{2,1,0:T(8,128)(2,1)S(1)}, u32[]{:S(2)}, u32[]{:S(2)}) %collective-permute-start.1) | collective-permute-done | bytes 524320 | tf_op jit(solution)/shard_map/ppermute | solution.py:14
  87.9 0.1 sum_halves.2
  88.1 0.1 pad.4
  88.2 11.0 %collective-permute-done.3.back = bf16[2,128,1024]{2,1,0:T(8,128)(2,1)S(1)} collective-permute-done((bf16[2,128,1024]{2,1,0:T(8,128)(2,1)S(1)}, bf16[2,128,1024]{2,1,0:T(8,128)(2,1)S(1)}, u32[]{:S(2)}, u32[]{:S(2)}) %collective-permute-start.3) | collective-permute-done | bytes 524320 | tf_op jit(solution)/shard_map/ppermute | solution.py:14
  99.3 1.1 copy.37
  100.4 37.2 %all_to_all.16 = bf16[256,2,1024]{2,1,0:T(2,128)(2,1)S(1)} all-to-all(bf16[256,2,1024]{2,1,0:T(2,128)(2,1)S(1)} %copy.37), channel_id=1, replica_groups=mesh['expert'=128,'hidden'=2] {'expert','hidden'}, dimensions={0} | all-to-all | bytes 2097152 | tf_op jit(solution)/shard_map/all_to_all | solution.py:242
  137.5 0.3 copy.43
  137.9 1.8 %logit_grads.1 = (bf16[2,196,128]{2,1,0:T(8,128)(2,1)S(1)}, bf16[1024,128]{1,0:T(8,128)(2,1)}) custom-call(bf16[2,196,1024]{2,1,0:T(8,128)(2,1)S(1)} %get-tuple-element.47.tokens, bf16[2,1024,196]{2,1,0:T(8,128)(2,1)S(1)} %get-tuple-element.48.turned, bf16[2,196,1024]{2,1,0:T(8,128)(2,1)S(1)} %get-tuple-element.49.grads, ...), custom_call_target="tpu_custom_call" | custom-call | flops 308281344 | bytes 3211264 | tf_op jit(solution)/shard_map/logit_grads/pallas_call | solution.py:156
  139.8 6.2 %all-to-all-start.2 = ((bf16[256,4,128]{2,1,0:T(4,128)(2,1)}), bf16[256,4,128]{2,1,0:T(4,128)(2,1)S(1)}, u32[]{:S(2)}, u32[]{:S(2)}) async-start(bf16[256,4,128]{2,1,0:T(4,128)(2,1)} %bitcast.13), calls=%async_computation.2 | async-start | bytes 524288 | tf_op jit(solution)/shard_map/all_to_all | solution.py:253
  145.9 0.4 fusion.1
  146.3 0.4 add_convert_fusion
  146.7 1.7 %copy.39 = bf16[2,196,1024]{2,0,1:T(2,128)(2,1)} copy(bf16[2,196,1024]{2,1,0:T(8,128)(2,1)S(1)} %add_convert_fusion) | data formatting | bytes 1605632
  148.4 12.5 %all-to-all-done.2 = bf16[256,4,128]{2,1,0:T(4,128)(2,1)S(1)} async-done(((bf16[256,4,128]{2,1,0:T(4,128)(2,1)}), bf16[256,4,128]{2,1,0:T(4,128)(2,1)S(1)}, u32[]{:S(2)}, u32[]{:S(2)}) %all-to-all-start.2) | async-done | bytes 262176 | tf_op jit(solution)/shard_map/all_to_all | solution.py:253
  160.9 0.9 convert_reduce_fusion
  (12 shorter events, 0.5 us)
Async XLA Ops:
  0.6 1.5 copy-start.2
  0.6 1.7 %copy-start = (bf16[1024,128]{1,0:T(8,128)(2,1)S(1)}, bf16[1024,128]{1,0:T(8,128)(2,1)}, u32[]{:S(2)}) copy-start(bf16[1024,128]{1,0:T(8,128)(2,1)} %weight.1) | copy-start | bytes 786436
  52.0 13.4 %collective-permute-start = (bf16[2,128,1024]{2,1,0:T(8,128)(2,1)S(1)}, bf16[2,128,1024]{2,1,0:T(8,128)(2,1)S(1)}, u32[]{:S(2)}, u32[]{:S(2)}) collective-permute-start(bf16[2,128,1024]{2,1,0:T(8,128)(2,1)S(1)} %bitcast.29), channel_id=1, source_target_pairs={{0,1},{1,0},{2,3},{3,2},{4,5},{5,4},{6,7},{7,6},{8,9},{9,8},{10,11... | collective-permute-start | bytes 1572872 | tf_op jit(solution)/shard_map/ppermute | solution.py:14
  60.5 16.1 %collective-permute-start.2 = (bf16[2,128,1024]{2,1,0:T(8,128)(2,1)S(1)}, bf16[2,128,1024]{2,1,0:T(8,128)(2,1)S(1)}, u32[]{:S(2)}, u32[]{:S(2)}) collective-permute-start(bf16[2,128,1024]{2,1,0:T(8,128)(2,1)S(1)} %slice_bitcast_fusion.2.refs_1_), channel_id=1, source_target_pairs={{0,1},{1,0},{2,3},{3,2},{4,5},{5,4},{6,7},{7,6},{8,9},{9,8},{10,11... | collective-permute-start | bytes 1572872 | tf_op jit(solution)/shard_map/ppermute | solution.py:14
  72.4 11.5 %copy-start.1 = (bf16[2,196,1024]{2,0,1:T(2,128)(2,1)S(1)}, bf16[2,196,1024]{2,0,1:T(2,128)(2,1)}, u32[]{:S(2)}) copy-start(bf16[2,196,1024]{2,0,1:T(2,128)(2,1)} %param.5) | copy-start | bytes 2408452
  72.4 15.5 %collective-permute-start.1 = (bf16[2,128,1024]{2,1,0:T(8,128)(2,1)S(1)}, bf16[2,128,1024]{2,1,0:T(8,128)(2,1)S(1)}, u32[]{:S(2)}, u32[]{:S(2)}) collective-permute-start(bf16[2,128,1024]{2,1,0:T(8,128)(2,1)S(1)} %expert_rows.4), channel_id=1, source_target_pairs={{0,1},{1,0},{2,3},{3,2},{4,5},{5,4},{6,7},{7,6},{8,9},{9,8},{10,11... | collective-permute-start | bytes 1572872 | tf_op jit(solution)/shard_map/ppermute | solution.py:14
  83.6 15.5 %collective-permute-start.3 = (bf16[2,128,1024]{2,1,0:T(8,128)(2,1)S(1)}, bf16[2,128,1024]{2,1,0:T(8,128)(2,1)S(1)}, u32[]{:S(2)}, u32[]{:S(2)}) collective-permute-start(bf16[2,128,1024]{2,1,0:T(8,128)(2,1)S(1)} %expert_rows.5), channel_id=1, source_target_pairs={{0,1},{1,0},{2,3},{3,2},{4,5},{5,4},{6,7},{7,6},{8,9},{9,8},{10,11... | collective-permute-start | bytes 1572872 | tf_op jit(solution)/shard_map/ppermute | solution.py:14
  139.8 21.1 %all-to-all-start.2 = ((bf16[256,4,128]{2,1,0:T(4,128)(2,1)}), bf16[256,4,128]{2,1,0:T(4,128)(2,1)S(1)}, u32[]{:S(2)}, u32[]{:S(2)}) async-start(bf16[256,4,128]{2,1,0:T(4,128)(2,1)} %bitcast.13), calls=%async_computation.2 | async-start | bytes 524288 | tf_op jit(solution)/shard_map/all_to_all | solution.py:253
